TPU v7x, 32 devices: a whole 2x2x4 slice. The times are simulated.
32 devices in a mesh: gx: 16 (over z, y, x), gy: 2 (over core).
Axes of the slice: x: 2, y: 2, z: 4, core: 2. Of those that a mesh axis runs over, the one named last changes fastest.
Arguments:
- u_old: bfloat16 [32, 4, 64, 128], P('gx', 'gy'), may hold values from -6 to 6
- rhs: bfloat16 [32, 4, 64, 128], P('gx', 'gy'), may hold values from -6 to 6
- classes: int32 [32, 4, 16], P('gx', 'gy'), may hold values from 0 to 7
- flags: int32 [2, 32, 4, 16], P(None, 'gx', 'gy'), may hold values from 0 to 1
- inverse: float32 [8, 64, 64], replicated, may hold values from -2 to 2
- x_face: float32 [8, 16, 16], replicated, may hold values from -2 to 2
- lateral_faces: float32 [4, 8, 16, 16], replicated, may hold values from -1.5 to 1.5
- inflow: float32 [4, 16, 128], P('gy'), may hold values from -6 to 6
Outputs:
- u_new: float32 [32, 4, 64, 128], P('gx', 'gy')
All inputs are finite; a program needn't handle non-finite values.
Results may differ from a plain program's by a relative error of at most 0.0003.
Values may be sent and summed in bfloat16 or wider, within the bound.
No kernel may reach another device: no remote copies, remote signals or barrier semaphores. Data moves between devices by JAX's collectives and lax.ppermute only.
A program may use at most 64 MiB of HBM per device.

v0:
```python
import jax
import jax.numpy as jnp
from jax import lax
from jax.sharding import PartitionSpec as P

TRACERS = 8
NCLASS = 8
NZ = 16


HIGH = lax.Precision.HIGHEST


def passed_along(value, axis, steps):
    count = lax.axis_size(axis)
    initial, last = (max(0, -steps), min(count, count - steps))
    return lax.ppermute(value, axis, [(source, source + steps) for source in range(initial, last)])


def entering_2(value, axis, join, neutral):
    count, mine = (lax.axis_size(axis), lax.axis_index(axis))
    pieces = jax.tree.map(lambda part: lax.all_gather(part, axis), value)
    so_far = jax.tree.map(
        lambda part, zero: jnp.full_like(part, 0) + jnp.asarray(zero, part.dtype), value, neutral
    )

    def turn(position, so_far):
        longer = join(so_far, jax.tree.map(lambda part: part[position], pieces))
        return jax.tree.map(lambda new, old: jnp.where(position < mine, new, old), longer, so_far)

    return lax.fori_loop(0, count - 1, turn, so_far)


def face_traces(field):
    planes, rows_y, columns = (field.shape[0], field.shape[1], field.shape[3])
    cube = field.reshape(planes, rows_y, 4, 4, 4, columns)
    y_low = cube[:, :, :, 0].reshape(planes, rows_y, 16, columns)
    y_high = cube[:, :, :, 3].reshape(planes, rows_y, 16, columns)
    z_low = cube[:, :, :, :, 0].reshape(planes, rows_y, 16, columns)
    z_high = cube[:, :, :, :, 3].reshape(planes, rows_y, 16, columns)
    return (y_low, y_high, z_low, z_high)


def along_z(trace, upward):
    planes, rows_y, columns = (trace.shape[0], trace.shape[1], trace.shape[3])
    split = trace.reshape(planes, rows_y, 16, TRACERS, NZ)
    border = jnp.zeros((planes, rows_y, 16, TRACERS, 1), trace.dtype)
    if upward:
        moved = jnp.concatenate([border, split[..., :-1]], axis=4)
    else:
        moved = jnp.concatenate([split[..., 1:], border], axis=4)
    return moved.reshape(planes, rows_y, 16, columns)


def class_onehot(classes):
    labels = jnp.arange(NCLASS, dtype=jnp.int32)[:, None, None, None]
    return (classes[None] == labels).astype(jnp.float32)


def class_columns(onehot):
    count, planes, rows_y = (onehot.shape[0], onehot.shape[1], onehot.shape[2])
    spread = jnp.broadcast_to(
        onehot[:, :, :, None, None, :], (count, planes, rows_y, 1, TRACERS, NZ)
    )
    return spread.reshape(count, planes, rows_y, 1, TRACERS * NZ)


def flag_columns(flag):
    planes, rows_y = (flag.shape[0], flag.shape[1])
    spread = jnp.broadcast_to(
        flag.astype(jnp.float32)[:, :, None, None, :], (planes, rows_y, 1, TRACERS, NZ)
    )
    return spread.reshape(planes, rows_y, 1, TRACERS * NZ)


def lateral_rhs(rhs, u_old, below_row, above_row, class_cols, flags, lateral_faces):
    y_low, y_high, z_low, z_high = face_traces(u_old)
    from_below = jnp.concatenate([below_row, y_high[:, :-1]], axis=1).astype(jnp.float32)
    from_above = jnp.concatenate([y_low[:, 1:], above_row], axis=1).astype(jnp.float32)
    from_front = along_z(z_high, True).astype(jnp.float32)
    from_back = along_z(z_low, False).astype(jnp.float32)
    y_flag = flag_columns(flags[0])
    z_flag = flag_columns(flags[1])

    def couple(face_index, source, weight):
        every = jnp.einsum("kij,xyjc->kxyic", lateral_faces[face_index], source, precision=HIGH)
        return jnp.sum(every * class_cols, axis=0) * weight

    planes, rows_y, columns = (rhs.shape[0], rhs.shape[1], rhs.shape[3])
    shape = (planes, rows_y, 4, 4, columns)
    cube = rhs.astype(jnp.float32).reshape(planes, rows_y, 4, 4, 4, columns)
    cube = cube.at[:, :, :, 0].add(-couple(0, from_below, 1.0 - y_flag).reshape(shape))
    cube = cube.at[:, :, :, 3].add(-couple(1, from_above, y_flag).reshape(shape))
    cube = cube.at[:, :, :, :, 0].add(-couple(2, from_front, 1.0 - z_flag).reshape(shape))
    cube = cube.at[:, :, :, :, 3].add(-couple(3, from_back, z_flag).reshape(shape))
    return cube.reshape(planes, rows_y, 64, columns)


def apply_inverse(matrices, source, class_cols):
    total = jnp.zeros(source.shape[:2] + (matrices.shape[1], source.shape[3]), jnp.float32)
    for class_id in range(NCLASS):
        total = total + class_cols[class_id] * jnp.einsum(
            "ij,xyjc->xyic", matrices[class_id], source, precision=HIGH
        )
    return total


def pick(table, hot_plane):
    return jnp.einsum("kab,kyz->yzab", table, hot_plane, precision=HIGH)


def applied(selected, trace):
    return jnp.einsum("...yzab,...ybtz->...yatz", selected, trace, precision=HIGH)


def compose(earlier, later):
    joined = jnp.einsum("...yzab,...yzbc->...yzac", later[0], earlier[0], precision=HIGH)
    return (joined, applied(later[0], earlier[1]) + later[1])


def on_device(u_old, rhs, classes, flags, inverse, x_face, lateral_faces, inflow):
    planes, rows_y, columns = (u_old.shape[0], u_old.shape[1], u_old.shape[3])
    y_low, y_high, z_low, z_high = face_traces(u_old)
    below_row = passed_along(y_high[:, -1:], "gy", 1)
    above_row = passed_along(y_low[:, :1], "gy", -1)
    onehot = class_onehot(classes)
    class_cols = class_columns(onehot)
    source = lateral_rhs(rhs, u_old, below_row, above_row, class_cols, flags, lateral_faces)
    coupling = -jnp.einsum("kij,kjl->kil", inverse[:, :, :16], x_face, precision=HIGH)
    transfer = coupling[:, 48:]
    solved_local = apply_inverse(inverse, source, class_cols)
    outflow_rows = solved_local[:, :, 48:]
    hot_planes = jnp.moveaxis(onehot, 1, 0)
    identity_map = jnp.broadcast_to(jnp.eye(16, dtype=jnp.float32), (rows_y, NZ, 16, 16))
    empty_trace = jnp.zeros((rows_y, 16, TRACERS, NZ), jnp.float32)

    def compose_plane(carry, items):
        outflow, hot_plane = items
        step_map = pick(transfer, hot_plane)
        return (compose(carry, (step_map, outflow)), None)

    outflow_split = outflow_rows.reshape(planes, rows_y, 16, TRACERS, NZ)
    (propagator, offset), _ = lax.scan(
        compose_plane, (identity_map, empty_trace), (outflow_split, hot_planes)
    )
    start = inflow.reshape(rows_y, 16, TRACERS, NZ)
    pre_prop, pre_offset = entering_2(
        (propagator, offset), "gx", compose, (identity_map, empty_trace)
    )
    entering = applied(pre_prop, start) + pre_offset

    def sweep(trace, items):
        values, hot_plane = items
        result = values.reshape(rows_y, 64, TRACERS, NZ) + applied(pick(coupling, hot_plane), trace)
        return (result[:, 48:], result.reshape(rows_y, 64, columns))

    _, u_new = lax.scan(sweep, entering, (solved_local, hot_planes))
    return u_new


def solution(mesh):
    in_specs = (
        P("gx", "gy", None, None),
        P("gx", "gy", None, None),
        P("gx", "gy", None),
        P(None, "gx", "gy", None),
        P(),
        P(),
        P(),
        P("gy", None, None),
    )
    out_specs = P("gx", "gy", None, None)
    return jax.shard_map(
        on_device, mesh=mesh, in_specs=in_specs, out_specs=out_specs, check_vma=False
    )
```

profile of v0, /device:TPU:0, one launch (start us, length us, event | category | flops | bytes accessed | tf_op | source)
XLA Modules:
  0.0 244.1 jit_solution(2762123385016849165)
XLA Ops:
  0.8 2.4 collective-permute-start
  11.6 1.5 convolution_negate_fusion
  19.3 3.4 %while.46 = (s32[]{:T(128)}, f32[2,16,16,16]{3,2,1,0:T(8,128)S(1)}, f32[2,16,8,16]{1,2,3,0:T(8,128)S(1)}, f32[2,8,2,16]{3,1,2,0:T(8,128)S(1)}, f32[8,16,16]{2,0,...) while((s32[]{:T(128)}, f32[2,16,16,16]{3,2,1,0:T(8,128)S(1)}, ...), condition=%wide.region_5.0_spmd.clone, body=%wide.region_4.0_spmd.clone.sunk | while | flops 3153923 | bytes 450663 | solution.py:143
  22.7 99.6 %all-gather = f32[32,16,16,16]{3,2,1,0:T(8,128)} all-gather(f32[2,16,16,16]{3,2,1,0:T(8,128)S(1)} %get-tuple-element.228), channel_id=2, replica_groups=mesh['gx'=16,'gy'=2] {'gx'}, dimensions={0}, use_global_device_ids=true | all-gather | bytes 557056 | tf_op jit(solution)/shard_map/all_gather | solution.py:22
  122.4 71.5 %all-gather.1 = f32[32,16,8,16]{3,2,1,0:T(8,128)S(1)} all-gather(f32[2,16,8,16]{3,2,1,0:T(8,128)S(1)} %copy.48), channel_id=3, replica_groups=mesh['gx'=16,'gy'=2] {'gx'}, dimensions={0}, use_global_device_ids=true | all-gather | bytes 278528 | tf_op jit(solution)/shard_map/all_gather | solution.py:22
  194.0 45.9 %while.47 = (s32[]{:T(128)}, f32[2,16,16,16]{3,2,1,0:T(8,128)S(1)}, f32[2,16,8,16]{1,2,3,0:T(8,128)S(1)}, s32[]{:T(128)}, f32[16,2,16,16,16]{4,3,2,1,0:T(8,128)}...) while((s32[]{:T(128)}, f32[2,16,16,16]{3,2,1,0:T(8,128)S(1)}, ...), condition=%wide.region_7.0_spmd.clone, body=%wide.region_6.0_spmd.clone.sunk | while | flops 2383876 | bytes 1657452 | solution.py:31
  194.2 1.5 fusion.144
  195.7 1.3 convolution_select_fusion.2
  197.2 1.5 fusion.144
  198.8 1.3 convolution_select_fusion.2
  200.3 1.5 fusion.144
  203.3 1.5 fusion.144
  206.4 1.5 fusion.144
  209.5 1.5 fusion.144
  212.5 1.5 fusion.144
  215.6 1.5 fusion.144
  218.6 1.5 fusion.144
  221.7 1.5 fusion.144
  224.8 1.5 fusion.144
  227.8 1.5 fusion.144
  230.9 1.5 fusion.144
  233.9 1.5 fusion.144
  237.0 1.5 fusion.144
  240.4 3.7 %while.45 = (s32[]{:T(128)}, f32[2,16,8,16]{1,2,3,0:T(8,128)S(1)}, f32[2,2,64,128]{3,2,1,0:T(8,128)}, f32[2,2,64,128]{3,2,1,0:T(8,128)S(1)}, f32[2,8,2,16]{3,1,2...) while((s32[]{:T(128)}, f32[2,16,8,16]{1,2,3,0:T(8,128)S(1)}, f32[2,2,64,128]{3,2,1,0:T(8,128)}, ...), condition=%wide.region_9.10_spmd, body=%wide.region_8.9_spmd.sunk | while | flops 6307842 | bytes 1172053 | solution.py:157
  (188 shorter events, 42.4 us)
Async XLA Ops:
  0.0 11.6 %copy-start = (f32[8,16,16]{2,1,0:T(8,128)S(1)}, f32[8,16,16]{2,1,0:T(8,128)}, u32[]{:S(2)}) copy-start(f32[8,16,16]{2,1,0:T(8,128)} %param.27) | copy-start | bytes 24580
  0.0 15.9 %copy-start.2 = (f32[4,8,16,16]{3,2,1,0:T(8,128)S(1)}, f32[4,8,16,16]{3,2,1,0:T(8,128)}, u32[]{:S(2)}) copy-start(f32[4,8,16,16]{3,2,1,0:T(8,128)} %param.28) | copy-start | bytes 98308
  0.0 16.9 %copy-start.1 = (f32[8,64,64]{2,1,0:T(8,128)S(1)}, f32[8,64,64]{2,1,0:T(8,128)}, u32[]{:S(2)}) copy-start(f32[8,64,64]{2,1,0:T(8,128)} %param.26) | copy-start | bytes 393220
  0.8 15.1 %collective-permute-start = (bf16[2,1,16,128]{3,2,1,0:T(8,128)(2,1)S(1)}, bf16[2,1,16,128]{3,2,1,0:T(8,128)(2,1)S(1)}, u32[]{:S(2)}, u32[]{:S(2)}) collective-permute-start(bf16[2,1,16,128]{3,2,1,0:T(8,128)(2,1)S(1)} %get-tuple-element.367), channel_id=1, source_target_pairs={{0,1},{2,3},{4,5},{6,7},{8,9},{10,11},{12,13},{14,15},{16,17},{18,... | collective-permute-start | bytes 24584 | tf_op jit(solution)/shard_map/ppermute | solution.py:17
  3.2 13.0 %collective-permute-start.1 = (bf16[2,1,16,128]{3,2,1,0:T(8,128)(2,1)S(1)}, bf16[2,1,16,128]{3,2,1,0:T(8,128)(2,1)S(1)}, u32[]{:S(2)}, u32[]{:S(2)}) collective-permute-start(bf16[2,1,16,128]{3,2,1,0:T(8,128)(2,1)S(1)} %get-tuple-element.366), channel_id=1, source_target_pairs={{1,0},{3,2},{5,4},{7,6},{9,8},{11,10},{13,12},{15,14},{17,16},{19,... | collective-permute-start | bytes 24584 | tf_op jit(solution)/shard_map/ppermute | solution.py:17
where the time goes:
time: 246 us; the launch traced here: 244 us
  blocking collectives  171 us (70%)
  matrix products  53.9 us (22%)
  local copies, waits for them, and re-layouts  9.94 us (4%)
  other arithmetic  3.8 us (2%)
  starting transfers between devices  3.66 us (1%)
    all_gather x2, blocking collectives, entering_2(): pieces = jax.tree.map(lambda part: lax.all_gather(part, axis), value)  171 us
    dot_general x20, matrix products, applied(): jnp.einsum('...yzab,...ybtz->...yatz', selected, trace, precision=HIGH)  25 us
    dot_general x17, matrix products, compose(): jnp.einsum('...yzab,...yzbc->...yzac', later[0], earlier[0], precision=HIGH)  21 us
  transfers between devices with their start and end apart: 2, of which 0 were waited for; matrix products, arithmetic and copies ran while one was open for 5% of the time, Pallas kernels for 0%

commit v1 on v0

v1 whole, which is shorter than its diff:
```python
import functools

import jax
import jax.numpy as jnp
from jax import lax
from jax.experimental import pallas as pl
from jax.experimental.pallas import tpu as pltpu
from jax.sharding import PartitionSpec as P

FACE = 16
HIGH = lax.Precision.HIGHEST
F32 = jnp.float32
BF16 = jnp.bfloat16


def iota(shape, dim):
    return lax.broadcasted_iota(jnp.int32, shape, dim)


def exact(left, right):
    return jnp.dot(left, right, precision=HIGH, preferred_element_type=F32)


def split(value):
    high = value.astype(BF16)
    return high, (value - high.astype(F32)).astype(BF16)


def params_kernel(inv_ref, x_ref, lat_ref, full_ref, coup_ref, step_ref):
    count, nodes, _ = inv_ref.shape
    column = iota((nodes, 256), 1)
    at = column - 128
    face, item = (at - 64) // FACE, at % FACE
    high, low = item // 4, item % 4
    lateral = jnp.where(face < 2, 16 * high + low + 12 * (face == 1), 16 * high + 4 * low + 3 * (face == 3))
    inner = jnp.where(at < FACE, at, -1)
    source = jnp.where(column < 128, column, jnp.where(at >= 64, lateral, inner))
    chosen = (iota((nodes, 256), 0) == source).astype(F32)
    gathered = exact(inv_ref[...].reshape(count * nodes, nodes), chosen)
    tile = (iota((FACE, 128), 1) % FACE == iota((FACE, 128), 0)).astype(F32)
    lat = exact(lat_ref[...].reshape(4 * count * FACE, FACE), tile)
    x_low = exact(x_ref[...].reshape(count * FACE, FACE), tile)
    row, lane = iota((128, 128), 0) // FACE, iota((128, 128), 1) // FACE
    keep = (row == lane) | ((row == 0) & (lane < 3))
    lane_at = iota((nodes, 128), 1)
    outs = []
    for k in range(count):
        rows = [x_low[k * FACE:(k + 1) * FACE], jnp.zeros((48, 128), F32)]
        for f in range(4):
            begin = (f * count + k) * FACE
            rows.append(lat[begin:begin + FACE])
        blocks = jnp.where(keep, jnp.concatenate(rows, axis=0), 0.0)
        here = pl.ds(k * nodes, nodes)
        joined = -exact(gathered[k * nodes:(k + 1) * nodes, 128:], blocks)
        both = jnp.where(lane_at < 64, gathered[k * nodes:(k + 1) * nodes, :128], joined)
        first, second = split(both)
        full_ref[here, 0:128] = first
        full_ref[here, 128:256] = second
        first, second = split(joined)
        coup_ref[here, :] = jnp.where(lane_at < 32, first.astype(F32), second.astype(F32)).astype(BF16)
        outs.append(joined[nodes - FACE:])
    step_ref[...] = jnp.concatenate(outs, axis=0).T[:FACE]


def encode(value):
    width = value.shape[1]
    tile = (iota((FACE, 256), 1) % FACE == iota((FACE, 256), 0)).astype(F32)
    spread = exact(value.T, tile)
    spread = jnp.where(iota((width, 256), 0) % FACE == iota((width, 256), 1) // FACE, spread, 0.0)
    gather = (iota((8, width), 1) // FACE == iota((8, width), 0)).astype(F32)
    return exact(gather, spread)


def decode(value):
    spread = (iota((128, 8), 0) // FACE == iota((128, 8), 1)).astype(F32)
    rows = exact(spread, value)
    rows = jnp.where(iota((128, 256), 0) % FACE == iota((128, 256), 1) // FACE, rows, 0.0)
    fold = (iota((256, 128), 0) % FACE == iota((256, 128), 1)).astype(F32)
    return exact(rows, fold).T[:FACE]


def block_diagonal(step):
    rows = jnp.concatenate([step] * 16, axis=0)
    return jnp.where(iota((256, 256), 0) // FACE == iota((256, 256), 1) // FACE, rows, 0.0)


def join(earlier, later):
    moved = exact(earlier, block_diagonal(later[:FACE]))
    return moved + jnp.concatenate([jnp.zeros((FACE, 256), F32), later[FACE:]], axis=0)


def advance(trace, later):
    return exact(trace, block_diagonal(later[:FACE])) + later[FACE:]


def sources_kernel(gy_size, u_ref, rhs_ref, below_ref, above_ref, cls_ref, flag_ref, full_ref, step_ref, x_ref, row_ref, map_ref):
    planes, rows_y, nodes, columns = u_ref.shape
    place = lax.axis_index("gy")
    node, item = iota((nodes, nodes), 1), iota((nodes, nodes), 0)
    face, high, low = item // FACE, item % FACE // 4, item % 4
    wanted = jnp.where(face < 2, 16 * high + low + 12 * (face == 1), 16 * high + 4 * low + 3 * (face == 3))
    chosen = (node == wanted).astype(BF16)

    def faces(value):
        return jnp.dot(chosen, value, preferred_element_type=F32)

    labels = []
    for x in range(planes):
        labels.append(cls_ref[x])
    for d in range(2):
        for x in range(planes):
            labels.append(flag_ref[d, x])
    labels = jnp.concatenate(labels, axis=0).astype(F32)
    tile = (iota((FACE, columns), 1) % FACE == iota((FACE, columns), 0)).astype(F32)
    on_columns = jnp.dot(labels, tile, preferred_element_type=F32)
    wide = (iota((FACE, 256), 1) // FACE == iota((FACE, 256), 0)).astype(F32)
    on_wide = jnp.dot(labels, wide, preferred_element_type=F32)
    row_ref[...] = on_columns
    z_at = iota((FACE, columns), 1) % FACE
    out_rows = [full_ref[pl.ds(k * nodes + nodes - FACE, FACE), :] for k in range(8)]
    out_rows = jnp.concatenate(out_rows, axis=0)
    row_class = iota((128, columns), 0) // FACE
    pick_row, pick_lane = iota((128, 256), 0), iota((128, 256), 1)
    maps = [None] * rows_y
    for x in range(planes):
        own = [faces(u_ref[x, y]) for y in range(rows_y)]
        under = jnp.where(place > 0, faces(below_ref[x, below_ref.shape[1] - 1])[16:32], 0.0)
        over = jnp.where(place < gy_size - 1, faces(above_ref[x, 0])[0:16], 0.0)
        for y in range(rows_y):
            at = x * rows_y + y
            y_flag = on_columns[planes * rows_y + at][None, :]
            z_flag = on_columns[2 * planes * rows_y + at][None, :]
            from_below = own[y - 1][16:32] if y > 0 else under
            from_above = own[y + 1][0:16] if y < rows_y - 1 else over
            from_front = jnp.where(z_at == 0, 0.0, pltpu.roll(own[y][48:64], 1, 1))
            from_back = jnp.where(z_at == FACE - 1, 0.0, pltpu.roll(own[y][32:48], columns - 1, 1))
            lateral = jnp.concatenate(
                [
                    from_below * (1.0 - y_flag),
                    from_above * y_flag,
                    from_front * (1.0 - z_flag),
                    from_back * z_flag,
                ],
                axis=0,
            ).astype(BF16)
            data = jnp.concatenate([rhs_ref[x, y], lateral], axis=0)
            x_ref[x, y] = data
            every = jnp.dot(out_rows, jnp.concatenate([data, data], axis=0), preferred_element_type=F32)
            every = jnp.where(row_class == on_columns[at][None, :].astype(jnp.int32), every, 0.0)
            outflow = sum(every[k * FACE:(k + 1) * FACE] for k in range(8))
            wide_class = on_wide[at][None, :].astype(jnp.int32)
            pick = (pick_row // FACE == wide_class) & (pick_row % FACE == pick_lane % FACE)
            linear = exact(step_ref[...], pick.astype(F32))
            here = jnp.concatenate([linear, encode(outflow)], axis=0)
            maps[y] = here if maps[y] is None else join(maps[y], here)
    for y in range(rows_y):
        map_ref[y] = maps[y]


def solve_kernel(x_ref, row_ref, full_ref, inflow_ref, w_ref, start_ref):
    planes, rows_y, _, columns = x_ref.shape
    nodes = w_ref.shape[2]
    for x in range(planes):
        for y in range(rows_y):
            data = x_ref[x, y]
            every = jnp.dot(full_ref[...], jnp.concatenate([data, data], axis=0), preferred_element_type=F32)
            label = row_ref[pl.ds(x * rows_y + y, 1), :]
            total = jnp.zeros((nodes, columns), F32)
            for k in range(8):
                total = total + jnp.where(label == k, every[k * nodes:(k + 1) * nodes], 0.0)
            w_ref[x, y] = total
    for y in range(rows_y):
        start_ref[y] = encode(inflow_ref[y])


def group_kernel(size, power, *refs):
    blocks, (total_ref, before_ref, held) = refs[:size], refs[size:]
    for s in range(size):
        held[s] = blocks[s][...]
    mine = lax.axis_index("gx") % size
    for y in range(total_ref.shape[0]):
        so_far, before = None, None
        for j in range(size):
            slot = (mine ^ j) if power else (mine - j + size) % size
            if j > 0:
                before = so_far if before is None else jnp.where(mine >= j, so_far, before)
            block = held[slot, y]
            so_far = block if so_far is None else join(so_far, block)
        total_ref[y] = so_far
        if before is None:
            before = so_far
        same = (iota((24, 256), 1) % FACE == iota((24, 256), 0)).astype(F32)
        before_ref[y] = jnp.where(mine > 0, before, same)


def finish_kernel(size, inner, power, *refs):
    blocks = refs[:size]
    before_ref, start_ref, w_ref, row_ref, coup_ref, out_ref, held = refs[size:]
    planes, rows_y, nodes, columns = w_ref.shape
    for s in range(size):
        held[s] = blocks[s][...]
    mine = lax.axis_index("gx") // inner
    for y in range(rows_y):
        trace = start_ref[y]
        for j in range(size - 1):
            slot = (mine ^ j) if power else (mine - j + size) % size
            trace = jnp.where(mine > j, advance(trace, held[slot, y]), trace)
        trace = advance(trace, before_ref[y])
        trace = decode(trace)
        for x in range(planes):
            first, second = split(trace)
            both = jnp.concatenate([first, second, first, jnp.zeros((128 - 48, columns), BF16)], axis=0)
            every = jnp.dot(coup_ref[...], both, preferred_element_type=F32)
            label = row_ref[pl.ds(x * rows_y + y, 1), :]
            total = w_ref[x, y]
            for k in range(8):
                total = total + jnp.where(label == k, every[k * nodes:(k + 1) * nodes], 0.0)
            out_ref[x, y] = total
            trace = total[nodes - FACE:]


def moved(value, pairs):
    return lax.ppermute(value, ("gx", "gy"), pairs)


def shape(dims, kind=F32):
    return jax.ShapeDtypeStruct(dims, kind)


def call(kernel, outs, name, args, scratch=(), flops=1000000, limit=48):
    return pl.pallas_call(
        kernel,
        out_shape=outs,
        in_specs=[pl.BlockSpec(memory_space=pltpu.VMEM)] * len(args),
        out_specs=jax.tree.map(lambda _: pl.BlockSpec(memory_space=pltpu.VMEM), outs),
        scratch_shapes=list(scratch),
        name=name,
        cost_estimate=pl.CostEstimate(flops=flops, bytes_accessed=500000, transcendentals=0),
        compiler_params=pltpu.CompilerParams(vmem_limit_bytes=limit * 1024 * 1024),
    )(*args)


def on_device(gx_size, gy_size, u_old, rhs, classes, flags, inverse, x_face, lateral_faces, inflow):
    planes, rows_y, nodes, columns = u_old.shape
    count = inverse.shape[0]
    everyone = [(x, y) for x in range(gx_size) for y in range(gy_size)]

    def at(x, y):
        return x * gy_size + y

    if gy_size == 2:
        below = above = moved(u_old, [(at(x, y), at(x, 1 - y)) for x, y in everyone])
    else:
        below = moved(u_old[:, rows_y - 1:], [(at(x, y), at(x, y + 1)) for x, y in everyone if y + 1 < gy_size])
        above = moved(u_old[:, :1], [(at(x, y), at(x, y - 1)) for x, y in everyone if y > 0])
    full, coup, step = call(
        params_kernel,
        (shape((count * nodes, 256), BF16), shape((count * nodes, 128), BF16), shape((FACE, 128))),
        "class_matrices",
        (inverse, x_face, lateral_faces),
    )
    data, labels, here = call(
        functools.partial(sources_kernel, gy_size),
        (
            shape((planes, rows_y, 128, columns), BF16),
            shape((3 * planes * rows_y, columns)),
            shape((rows_y, 24, 256)),
        ),
        "sources",
        (u_old, rhs, below, above, classes, flags, full, step),
    )
    inner = 4 if gx_size % 4 == 0 else 1
    outer = gx_size // inner
    power = outer & (outer - 1) == 0
    blocks = [here]
    for s in range(1, inner):
        blocks.append(moved(here, [(at(x, y), at(x ^ s, y)) for x, y in everyone]))
    solved, start = call(
        solve_kernel,
        (shape((planes, rows_y, nodes, columns)), shape((rows_y, 8, 256))),
        "local_solve",
        (data, labels, full, inflow),
    )
    total, before = call(
        functools.partial(group_kernel, inner, True),
        (shape((rows_y, 24, 256)), shape((rows_y, 24, 256))),
        "group_maps",
        tuple(blocks),
        [pltpu.VMEM((inner, rows_y, 24, 256), F32)],
    )
    blocks = [total]
    for s in range(1, outer):
        if power:
            pairs = [(at(x, y), at(x ^ (s * inner), y)) for x, y in everyone]
        else:
            pairs = [(at(x, y), at((x + s * inner) % gx_size, y)) for x, y in everyone]
        blocks.append(moved(total, pairs))
    return call(
        functools.partial(finish_kernel, outer, inner, power),
        shape((planes, rows_y, nodes, columns)),
        "finish",
        tuple(blocks) + (before, start, solved, labels, coup),
        [pltpu.VMEM((outer, rows_y, 24, 256), F32)],
    )


def solution(mesh):
    in_specs = (
        P("gx", "gy", None, None),
        P("gx", "gy", None, None),
        P("gx", "gy", None),
        P(None, "gx", "gy", None),
        P(),
        P(),
        P(),
        P("gy", None, None),
    )
    out_specs = P("gx", "gy", None, None)
    body = functools.partial(on_device, mesh.shape["gx"], mesh.shape["gy"])
    return jax.shard_map(body, mesh=mesh, in_specs=in_specs, out_specs=out_specs, check_vma=False)
```

time: 246 us -> 31.8 us (0.13)
  blocking collectives: 171 us -> 0 us
  matrix products: 53.9 us -> 0 us
  Pallas kernels: 0 us -> 12.2 us
  waiting for transfers between devices: 0.01 us -> 6.95 us
  local copies, waits for them, and re-layouts: 9.94 us -> 3.41 us
  starting transfers between devices: 3.66 us -> 8.93 us
  other arithmetic: 3.8 us -> 0 us
    all_gather x2 -> x0, blocking collectives: 171 us -> none  [entering_2(): pieces = jax.tree.map(lambda part: lax.all_gather(part, axis), value)]
    dot_general x54 -> x0, matrix products: 53.9 us -> none  [the longest x20 25 us: applied(): jnp.einsum('...yzab,...ybtz->...yatz', selected, trace, precision=HIGH)]
    pallas_call x0 -> x5, Pallas kernels: none -> 12.2 us  [call(): pl.pallas_call(kernel, out_shape=outs, in_specs=[pl.BlockSpec(memory_spac...]
    ppermute x2 -> x7, waiting for transfers between devices: 0.01 us -> 6.95 us  [moved(): return lax.ppermute(value, ('gx', 'gy'), pairs)]
    ppermute x2 -> x7, starting transfers between devices: 3.66 us -> 8.93 us  [moved(): return lax.ppermute(value, ('gx', 'gy'), pairs)]
    unnamed x9 -> x16, local copies, waits for them, and re-layouts: 0.12 us -> 3.41 us
    convert_element_type x5 -> x0, other arithmetic: 2.78 us -> none  [the longest x3 2.06 us: class_onehot(): return (classes[None] == labels).astype(jnp.float32)]
    dynamic_slice x38 -> x0, local copies, waits for them, and re-layouts: 2.47 us -> none  [the longest x30 1.98 us: turn(): longer = join(so_far, jax.tree.map(lambda part: part[position], pieces))]
  transfers between devices with their start and end apart: 2 -> 7, of which waited for: 0 -> 5; matrix products, arithmetic and copies ran while one was open for 5% -> 0% of each run, Pallas kernels for 0% -> 9%
where the time goes in v1:
time: 31.8 us; the launch traced here: 31.6 us
  Pallas kernels  12.2 us (38%)
  starting transfers between devices  8.93 us (28%)
  waiting for transfers between devices  6.95 us (22%)
  local copies, waits for them, and re-layouts  3.41 us (11%)
    pallas_call x5, Pallas kernels, call(): pl.pallas_call(kernel, out_shape=outs, in_specs=[pl.BlockSpec(memory_spac...  12.2 us
    ppermute x7, starting transfers between devices, moved(): return lax.ppermute(value, ('gx', 'gy'), pairs)  8.93 us
    ppermute x7, waiting for transfers between devices, moved(): return lax.ppermute(value, ('gx', 'gy'), pairs)  6.95 us
    unnamed x16, local copies, waits for them, and re-layouts  3.41 us
  transfers between devices with their start and end apart: 7, of which 5 were waited for; matrix products, arithmetic and copies ran while one was open for 0% of the time, Pallas kernels for 9%

profile of v1, /device:TPU:0, one launch (start us, length us, event | category | flops | bytes accessed | tf_op | source)
XLA Modules:
  0.0 31.6 jit_solution(12534247073505749650)
XLA Ops:
  0.0 0.5 %collective-permute-start = (bf16[2,2,64,128]{3,2,1,0:T(8,128)(2,1)}, bf16[2,2,64,128]{3,2,1,0:T(8,128)(2,1)S(1)}, u32[]{:S(2)}, u32[]{:S(2)}) collective-permute-start(bf16[2,2,64,128]{3,2,1,0:T(8,128)(2,1)} %u_ref.1), channel_id=1, source_target_pairs={{0,1},{1,0},{2,3},{3,2},{4,5},{5,4},{6,7},{7,6},{8,9},{9,8},{10,11... | collective-permute-start | bytes 196616 | tf_op jit(solution)/shard_map/ppermute | solution.py:223
  0.5 0.9 %copy-done = f32[8,64,64]{2,1,0:T(8,128)S(1)} copy-done((f32[8,64,64]{2,1,0:T(8,128)S(1)}, f32[8,64,64]{2,1,0:T(8,128)}, u32[]{:S(2)}) %copy-start) | copy-done | bytes 131096
  1.4 0.9 %copy-done.1 = f32[4,8,16,16]{3,2,1,0:T(8,128)S(1)} copy-done((f32[4,8,16,16]{3,2,1,0:T(8,128)S(1)}, f32[4,8,16,16]{3,2,1,0:T(8,128)}, u32[]{:S(2)}) %copy-start.1) | copy-done | bytes 32792
  2.4 0.8 %copy-done.2 = f32[8,16,16]{2,1,0:T(8,128)S(1)} copy-done((f32[8,16,16]{2,1,0:T(8,128)S(1)}, f32[8,16,16]{2,1,0:T(8,128)}, u32[]{:S(2)}) %copy-start.2) | copy-done | bytes 8216
  3.2 1.7 %class_matrices.1 = (bf16[512,256]{1,0:T(8,128)(2,1)S(1)}, bf16[512,128]{1,0:T(8,128)(2,1)S(1)}, f32[16,128]{1,0:T(8,128)S(1)}) custom-call(f32[8,64,64]{2,1,0:T(8,128)S(1)} %copy-done, f32[8,16,16]{2,1,0:T(8,128)S(1)} %copy-done.2, f32[4,8,16,16]{3,2,1,0:T(8,128)S(1)} %copy-done.1), custom_call_target="tpu_custom_call" | custom-call | flops 1000000 | bytes 500000 | tf_op jit(solution)/shard_map/class_matrices/pallas_call | solution.py:231
  5.0 0.0 collective-permute-done.below_ref.above_ref
  5.0 0.7 %copy-done.7 = s32[2,2,16]{2,1,0:T(2,128)S(1)} copy-done((s32[2,2,16]{2,1,0:T(2,128)S(1)}, s32[2,2,16]{2,1,0:T(2,128)}, u32[]{:S(2)}) %copy-start.7) | copy-done | bytes 280
  5.6 3.0 %sources.1 = (bf16[2,2,128,128]{3,2,1,0:T(8,128)(2,1)S(1)}, f32[12,128]{1,0:T(8,128)S(1)}, f32[2,24,256]{2,1,0:T(8,128)S(1)}) custom-call(bf16[2,2,64,128]{3,2,1,0:T(8,128)(2,1)S(1)} %copy-done.3, bf16[2,2,64,128]{3,2,1,0:T(8,128)(2,1)S(1)} %copy-done.4, bf16[2,2,64,128]{3,2,1,0:T(8,128)(2,1)S(1)} %collective-permute-done.below_ref.above_ref, ...), custom_call_target="tpu_custom_call" | custom-call | flops 1000000 | bytes 500000 | tf_op jit(solution)/shard_map/sources/pallas_call | solution.py:231
  8.7 3.5 %collective-permute-start.3 = (f32[2,24,256]{2,1,0:T(8,128)S(1)}, f32[2,24,256]{2,1,0:T(8,128)S(1)}, u32[]{:S(2)}, u32[]{:S(2)}) collective-permute-start(f32[2,24,256]{2,1,0:T(8,128)S(1)} %get-tuple-element.17.refs_0_), channel_id=1, source_target_pairs={{0,6},{1,7},{2,4},{3,5},{4,2},{5,3},{6,0},{7,1},{8,14},{9,15},{10,... | collective-permute-start | bytes 147464 | tf_op jit(solution)/shard_map/ppermute | solution.py:223
  12.1 0.5 %collective-permute-start.2 = (f32[2,24,256]{2,1,0:T(8,128)S(1)}, f32[2,24,256]{2,1,0:T(8,128)S(1)}, u32[]{:S(2)}, u32[]{:S(2)}) collective-permute-start(f32[2,24,256]{2,1,0:T(8,128)S(1)} %get-tuple-element.17.refs_0_), channel_id=1, source_target_pairs={{0,4},{1,5},{2,6},{3,7},{4,0},{5,1},{6,2},{7,3},{8,12},{9,13},{10,... | collective-permute-start | bytes 147464 | tf_op jit(solution)/shard_map/ppermute | solution.py:223
  12.6 0.1 collective-permute-start.1
  12.8 1.8 %collective-permute-done.3.refs_3_ = f32[2,24,256]{2,1,0:T(8,128)S(1)} collective-permute-done((f32[2,24,256]{2,1,0:T(8,128)S(1)}, f32[2,24,256]{2,1,0:T(8,128)S(1)}, u32[]{:S(2)}, u32[]{:S(2)}) %collective-permute-start.3) | collective-permute-done | bytes 49184 | tf_op jit(solution)/shard_map/ppermute | solution.py:223
  14.5 1.7 %collective-permute-done.2.refs_2_ = f32[2,24,256]{2,1,0:T(8,128)S(1)} collective-permute-done((f32[2,24,256]{2,1,0:T(8,128)S(1)}, f32[2,24,256]{2,1,0:T(8,128)S(1)}, u32[]{:S(2)}, u32[]{:S(2)}) %collective-permute-start.2) | collective-permute-done | bytes 49184 | tf_op jit(solution)/shard_map/ppermute | solution.py:223
  16.2 0.5 %collective-permute-done.1.refs_1_ = f32[2,24,256]{2,1,0:T(8,128)S(1)} collective-permute-done((f32[2,24,256]{2,1,0:T(8,128)S(1)}, f32[2,24,256]{2,1,0:T(8,128)S(1)}, u32[]{:S(2)}, u32[]{:S(2)}) %collective-permute-start.1) | collective-permute-done | bytes 49184 | tf_op jit(solution)/shard_map/ppermute | solution.py:223
  16.7 1.4 %group_maps.1 = (f32[2,24,256]{2,1,0:T(8,128)S(1)}, f32[2,24,256]{2,1,0:T(8,128)S(1)}) custom-call(f32[2,24,256]{2,1,0:T(8,128)S(1)} %get-tuple-element.17.refs_0_, f32[2,24,256]{2,1,0:T(8,128)S(1)} %collective-permute-done.1.refs_1_, f32[2,24,256]{2,1,0:T(8,128)S(1)} %collective-permute-done.2.refs_2_, f32[2,24,256]{2,1,0:T(8,128)S(1)} %collective-permute-done.3.refs_3_), custom_call_target="tpu_custom_call" | custom-call | flops 1000000 | bytes 500000 | tf_op jit(solution)/shard_map/group_maps/pallas_call | solution.py:231
  18.1 3.6 %collective-permute-start.6 = (f32[2,24,256]{2,1,0:T(8,128)S(1)}, f32[2,24,256]{2,1,0:T(8,128)S(1)}, u32[]{:S(2)}, u32[]{:S(2)}) collective-permute-start(f32[2,24,256]{2,1,0:T(8,128)S(1)} %get-tuple-element.18.refs_0_), channel_id=1, source_target_pairs={{0,24},{1,25},{2,26},{3,27},{4,28},{5,29},{6,30},{7,31},{8,16},{9,... | collective-permute-start | bytes 147464 | tf_op jit(solution)/shard_map/ppermute | solution.py:223
  21.8 0.0 collective-permute-start.5
  21.8 0.8 %collective-permute-start.4 = (f32[2,24,256]{2,1,0:T(8,128)S(1)}, f32[2,24,256]{2,1,0:T(8,128)S(1)}, u32[]{:S(2)}, u32[]{:S(2)}) collective-permute-start(f32[2,24,256]{2,1,0:T(8,128)S(1)} %get-tuple-element.18.refs_0_), channel_id=1, source_target_pairs={{0,8},{1,9},{2,10},{3,11},{4,12},{5,13},{6,14},{7,15},{8,0},{9,1},... | collective-permute-start | bytes 147464 | tf_op jit(solution)/shard_map/ppermute | solution.py:223
  22.6 0.0 copy-done.5
  22.6 1.2 %local_solve.1 = (f32[2,2,64,128]{3,2,1,0:T(8,128)S(1)}, f32[2,8,256]{2,1,0:T(8,128)S(1)}) custom-call(bf16[2,2,128,128]{3,2,1,0:T(8,128)(2,1)S(1)} %get-tuple-element.20.x_ref, f32[12,128]{1,0:T(8,128)S(1)} %get-tuple-element.21.row_ref.refs_7_, bf16[512,256]{1,0:T(8,128)(2,1)S(1)} %get-tuple-element.15.full_ref, f32[2,16,128]{2,1,0:T(8,128)S(1)} %copy-done.5), custom_call_target="tpu_custom_call" | custom-call | flops 1000000 | bytes 500000 | tf_op jit(solution)/shard_map/local_solve/pallas_call | solution.py:231
  23.8 0.4 %collective-permute-done.6.refs_3_ = f32[2,24,256]{2,1,0:T(8,128)S(1)} collective-permute-done((f32[2,24,256]{2,1,0:T(8,128)S(1)}, f32[2,24,256]{2,1,0:T(8,128)S(1)}, u32[]{:S(2)}, u32[]{:S(2)}) %collective-permute-start.6) | collective-permute-done | bytes 49184 | tf_op jit(solution)/shard_map/ppermute | solution.py:223
  24.2 2.5 %collective-permute-done.5.refs_2_ = f32[2,24,256]{2,1,0:T(8,128)S(1)} collective-permute-done((f32[2,24,256]{2,1,0:T(8,128)S(1)}, f32[2,24,256]{2,1,0:T(8,128)S(1)}, u32[]{:S(2)}, u32[]{:S(2)}) %collective-permute-start.5) | collective-permute-done | bytes 49184 | tf_op jit(solution)/shard_map/ppermute | solution.py:223
  26.8 0.0 collective-permute-done.4.refs_1_
  26.8 4.8 %finish.1 = f32[2,2,64,128]{3,2,1,0:T(8,128)} custom-call(f32[2,24,256]{2,1,0:T(8,128)S(1)} %get-tuple-element.18.refs_0_, f32[2,24,256]{2,1,0:T(8,128)S(1)} %collective-permute-done.4.refs_1_, f32[2,24,256]{2,1,0:T(8,128)S(1)} %collective-permute-done.5.refs_2_, f32[2,24,256]{2,1,0:T(8,128)S(1)} %collective-permute-done.6.refs_3_, ...), custom_call_target="tpu_custom_call" | custom-call | flops 1000000 | bytes 500000 | tf_op jit(solution)/shard_map/finish/pallas_call | solution.py:231
  (11 shorter events, 0.0 us)
Async XLA Ops:
  0.0 5.0 %collective-permute-start = (bf16[2,2,64,128]{3,2,1,0:T(8,128)(2,1)}, bf16[2,2,64,128]{3,2,1,0:T(8,128)(2,1)S(1)}, u32[]{:S(2)}, u32[]{:S(2)}) collective-permute-start(bf16[2,2,64,128]{3,2,1,0:T(8,128)(2,1)} %u_ref.1), channel_id=1, source_target_pairs={{0,1},{1,0},{2,3},{3,2},{4,5},{5,4},{6,7},{7,6},{8,9},{9,8},{10,11... | collective-permute-start | bytes 196616 | tf_op jit(solution)/shard_map/ppermute | solution.py:223
  0.5 0.9 %copy-start = (f32[8,64,64]{2,1,0:T(8,128)S(1)}, f32[8,64,64]{2,1,0:T(8,128)}, u32[]{:S(2)}) copy-start(f32[8,64,64]{2,1,0:T(8,128)} %inv_ref.1) | copy-start | bytes 393220
  1.4 0.9 %copy-start.1 = (f32[4,8,16,16]{3,2,1,0:T(8,128)S(1)}, f32[4,8,16,16]{3,2,1,0:T(8,128)}, u32[]{:S(2)}) copy-start(f32[4,8,16,16]{3,2,1,0:T(8,128)} %lat_ref.1) | copy-start | bytes 98308
  2.4 0.8 %copy-start.2 = (f32[8,16,16]{2,1,0:T(8,128)S(1)}, f32[8,16,16]{2,1,0:T(8,128)}, u32[]{:S(2)}) copy-start(f32[8,16,16]{2,1,0:T(8,128)} %x_ref.1) | copy-start | bytes 24580
  3.2 1.8 %copy-start.3 = (bf16[2,2,64,128]{3,2,1,0:T(8,128)(2,1)S(1)}, bf16[2,2,64,128]{3,2,1,0:T(8,128)(2,1)}, u32[]{:S(2)}) copy-start(bf16[2,2,64,128]{3,2,1,0:T(8,128)(2,1)} %u_ref.1) | copy-start | bytes 196612
  3.2 1.8 %copy-start.4 = (bf16[2,2,64,128]{3,2,1,0:T(8,128)(2,1)S(1)}, bf16[2,2,64,128]{3,2,1,0:T(8,128)(2,1)}, u32[]{:S(2)}) copy-start(bf16[2,2,64,128]{3,2,1,0:T(8,128)(2,1)} %rhs_ref.1) | copy-start | bytes 196612
  3.2 1.8 %copy-start.6 = (s32[2,2,2,16]{3,2,1,0:T(2,128)S(1)}, s32[2,2,2,16]{3,2,1,0:T(2,128)}, u32[]{:S(2)}) copy-start(s32[2,2,2,16]{3,2,1,0:T(2,128)} %flag_ref.1) | copy-start | bytes 1540
  5.0 0.7 %copy-start.7 = (s32[2,2,16]{2,1,0:T(2,128)S(1)}, s32[2,2,16]{2,1,0:T(2,128)}, u32[]{:S(2)}) copy-start(s32[2,2,16]{2,1,0:T(2,128)} %cls_ref.1) | copy-start | bytes 772
  8.7 5.9 %collective-permute-start.3 = (f32[2,24,256]{2,1,0:T(8,128)S(1)}, f32[2,24,256]{2,1,0:T(8,128)S(1)}, u32[]{:S(2)}, u32[]{:S(2)}) collective-permute-start(f32[2,24,256]{2,1,0:T(8,128)S(1)} %get-tuple-element.17.refs_0_), channel_id=1, source_target_pairs={{0,6},{1,7},{2,4},{3,5},{4,2},{5,3},{6,0},{7,1},{8,14},{9,15},{10,... | collective-permute-start | bytes 147464 | tf_op jit(solution)/shard_map/ppermute | solution.py:223
  12.1 4.1 %collective-permute-start.2 = (f32[2,24,256]{2,1,0:T(8,128)S(1)}, f32[2,24,256]{2,1,0:T(8,128)S(1)}, u32[]{:S(2)}, u32[]{:S(2)}) collective-permute-start(f32[2,24,256]{2,1,0:T(8,128)S(1)} %get-tuple-element.17.refs_0_), channel_id=1, source_target_pairs={{0,4},{1,5},{2,6},{3,7},{4,0},{5,1},{6,2},{7,3},{8,12},{9,13},{10,... | collective-permute-start | bytes 147464 | tf_op jit(solution)/shard_map/ppermute | solution.py:223
  12.6 4.1 %collective-permute-start.1 = (f32[2,24,256]{2,1,0:T(8,128)S(1)}, f32[2,24,256]{2,1,0:T(8,128)S(1)}, u32[]{:S(2)}, u32[]{:S(2)}) collective-permute-start(f32[2,24,256]{2,1,0:T(8,128)S(1)} %get-tuple-element.17.refs_0_), channel_id=1, source_target_pairs={{0,2},{1,3},{2,0},{3,1},{4,6},{5,7},{6,4},{7,5},{8,10},{9,11},{10,... | collective-permute-start | bytes 147464 | tf_op jit(solution)/shard_map/ppermute | solution.py:223
  16.7 5.8 %copy-start.5 = (f32[2,16,128]{2,1,0:T(8,128)S(1)}, f32[2,16,128]{2,1,0:T(8,128)}, u32[]{:S(2)}) copy-start(f32[2,16,128]{2,1,0:T(8,128)} %inflow_ref.1) | copy-start | bytes 49156
  18.1 6.1 %collective-permute-start.6 = (f32[2,24,256]{2,1,0:T(8,128)S(1)}, f32[2,24,256]{2,1,0:T(8,128)S(1)}, u32[]{:S(2)}, u32[]{:S(2)}) collective-permute-start(f32[2,24,256]{2,1,0:T(8,128)S(1)} %get-tuple-element.18.refs_0_), channel_id=1, source_target_pairs={{0,24},{1,25},{2,26},{3,27},{4,28},{5,29},{6,30},{7,31},{8,16},{9,... | collective-permute-start | bytes 147464 | tf_op jit(solution)/shard_map/ppermute | solution.py:223
  21.8 5.0 %collective-permute-start.5 = (f32[2,24,256]{2,1,0:T(8,128)S(1)}, f32[2,24,256]{2,1,0:T(8,128)S(1)}, u32[]{:S(2)}, u32[]{:S(2)}) collective-permute-start(f32[2,24,256]{2,1,0:T(8,128)S(1)} %get-tuple-element.18.refs_0_), channel_id=1, source_target_pairs={{0,16},{1,17},{2,18},{3,19},{4,20},{5,21},{6,22},{7,23},{8,24},{9,... | collective-permute-start | bytes 147464 | tf_op jit(solution)/shard_map/ppermute | solution.py:223
  21.8 5.0 %collective-permute-start.4 = (f32[2,24,256]{2,1,0:T(8,128)S(1)}, f32[2,24,256]{2,1,0:T(8,128)S(1)}, u32[]{:S(2)}, u32[]{:S(2)}) collective-permute-start(f32[2,24,256]{2,1,0:T(8,128)S(1)} %get-tuple-element.18.refs_0_), channel_id=1, source_target_pairs={{0,8},{1,9},{2,10},{3,11},{4,12},{5,13},{6,14},{7,15},{8,0},{9,1},... | collective-permute-start | bytes 147464 | tf_op jit(solution)/shard_map/ppermute | solution.py:223

commit v2 on v1

v2 whole, which is shorter than its diff:
```python
import functools

import jax
import jax.numpy as jnp
from jax import lax
from jax.experimental import pallas as pl
from jax.experimental.pallas import tpu as pltpu
from jax.sharding import PartitionSpec as P

FACE = 16
HIGH = lax.Precision.HIGHEST
F32 = jnp.float32
BF16 = jnp.bfloat16


def iota(shape, dim):
    return lax.broadcasted_iota(jnp.int32, shape, dim)


def exact(left, right):
    return jnp.dot(left, right, precision=HIGH, preferred_element_type=F32)


def split(value):
    high = value.astype(BF16)
    return high, (value - high.astype(F32)).astype(BF16)


def wanted_node(face, item):
    high, low = item // 4, item % 4
    return jnp.where(face < 2, 16 * high + low + 12 * (face == 1), 16 * high + 4 * low + 3 * (face == 3))


def dot(left, right):
    return jnp.dot(left, right, preferred_element_type=F32)


def dot_rows(left, right):
    return lax.dot_general(left, right, (((1,), (1,)), ((), ())), preferred_element_type=F32)


def applied(rows, linear):
    lane = iota((rows.shape[0], 128), 1)
    halves = []
    for begin in (0, 128):
        part, total = rows[:, begin:begin + 128], None
        for b in range(FACE):
            near = jnp.take_along_axis(part, lane // FACE * FACE + b, axis=1, mode="promise_in_bounds")
            term = near * linear[b:b + 1, begin:begin + 128]
            total = term if total is None else total + term
        halves.append(total)
    return jnp.concatenate(halves, axis=1)


def join(earlier, later):
    moved_rows = applied(earlier, later[:FACE])
    return jnp.concatenate([moved_rows[:FACE], moved_rows[FACE:] + later[FACE:]], axis=0)


def advance(trace, later):
    return applied(trace, later[:FACE]) + later[FACE:]


def encode(value):
    high, low = split(value)
    both = jnp.concatenate([high, low], axis=1)
    tile = (iota((256, FACE), 0) % FACE == iota((256, FACE), 1)).astype(BF16)
    spread = dot(tile, both)
    keep = iota((256, 256), 0) // FACE == iota((256, 256), 1) % FACE
    spread = jnp.where(keep, spread, 0.0).astype(BF16)
    gather = (iota((8, 256), 1) % 128 // FACE == iota((8, 256), 0)).astype(BF16)
    return dot_rows(gather, spread)


def class_products(inv_rows, weights):
    count = inv_rows.shape[0]
    high, low = split(inv_rows)
    parts = dot(jnp.concatenate([high, low], axis=0), weights)
    return -(parts[:count, :128] + parts[:count, 128:] + parts[count:, :128])


def with_inverse(inv_rows, products):
    count = inv_rows.shape[0]
    wide = jnp.concatenate([inv_rows, jnp.zeros((count, 128 - inv_rows.shape[1]), F32)], axis=1)
    return jnp.where(iota((count, 128), 1) < 64, wide, products)


def in_parts(value):
    high, low = split(value)
    return jnp.concatenate([high, low], axis=1)


def coupling_parts(products):
    high, low = split(products)
    lane = iota(products.shape, 1)
    return jnp.where(lane < 32, high.astype(F32), jnp.where(lane < 48, low.astype(F32), 0.0)).astype(BF16)


def params_kernel(inv_hbm, x_hbm, lat_hbm, cls_hbm, flag_hbm, weight_ref, out_ref, step_ref, lin_ref, label_ref,
                  inv_ref, x_ref, lat_ref, cls_ref, flag_ref, sems):
    pairs = ((lat_hbm, lat_ref), (x_hbm, x_ref), (inv_hbm, inv_ref), (cls_hbm, cls_ref), (flag_hbm, flag_ref))
    copies = [pltpu.make_async_copy(a, b, sems.at[i]) for i, (a, b) in enumerate(pairs)]
    for copy in copies:
        copy.start()
    count, nodes, _ = inv_ref.shape
    planes, rows_y, _ = cls_ref.shape
    item, lane = iota((FACE, 128), 0), iota((FACE, 128), 1)
    places = [(lane == 64 + FACE * f + item).astype(BF16) for f in range(4)]
    places.append(((lane < 48) & (lane % FACE == item)).astype(BF16))
    at = iota((nodes, 5 * FACE), 1)
    wanted = jnp.where(at < 64, wanted_node(at // FACE, at % FACE), at - 64)
    chosen = (iota((nodes, 5 * FACE), 0) == wanted).astype(BF16)
    for copy in copies:
        copy.wait()
    placed = []
    for f in range(5):
        rows = (lat_ref[f] if f < 4 else x_ref[...]).reshape(count * FACE, FACE)
        placed.append(dot(jnp.concatenate(split(rows), axis=0), places[f]).astype(BF16))
    columns = []
    for k in range(count):
        for part in range(2):
            begin = part * count * FACE + k * FACE
            columns.append(jnp.concatenate([p[begin:begin + FACE] for p in placed], axis=0))
    weights = dot(chosen, jnp.concatenate(columns, axis=1)).astype(BF16)
    weight_ref[...] = weights
    outs, steps = [], []
    for k in range(count):
        inv_rows = inv_ref[k, nodes - FACE:, :]
        products = class_products(inv_rows, weights[:, 256 * k:256 * k + 256])
        outs.append(with_inverse(inv_rows, products))
        steps.append(products)
    out_ref[...] = in_parts(jnp.concatenate(outs, axis=0))
    step = coupling_parts(jnp.concatenate(steps, axis=0))
    step_ref[...] = step
    flip_row, flip_lane = iota((2 * FACE, 128), 0), iota((2 * FACE, 128), 1)
    flip = (flip_lane == flip_row + FACE * (flip_row >= FACE)).astype(BF16)
    turned = dot_rows(flip, step).astype(BF16)
    labels = [cls_ref[x] for x in range(planes)]
    labels += [flag_ref[d, x] for d in range(2) for x in range(planes)]
    labels = jnp.concatenate(labels, axis=0).astype(F32).astype(BF16)
    tile = (iota((FACE, 128), 1) % FACE == iota((FACE, 128), 0)).astype(BF16)
    label_ref[...] = dot(labels, tile)
    wide = (iota((FACE, 256), 1) // FACE == iota((FACE, 256), 0)).astype(BF16)
    on_wide = dot(labels, wide).astype(jnp.int32)
    pick_row, pick_lane = iota((128, 256), 0), iota((128, 256), 1)
    same = pick_row % FACE == pick_lane % FACE
    for y in range(rows_y):
        whole = None
        for x in range(planes):
            here = on_wide[x * rows_y + y:x * rows_y + y + 1]
            pick = jnp.where(same & (pick_row // FACE == here), 1.0, 0.0).astype(BF16)
            both = dot(turned, pick)
            linear = both[:FACE] + both[FACE:]
            lin_ref[x, y] = linear
            whole = linear if whole is None else applied(whole, linear)
        lin_ref[planes, y] = whole


def class_sum(every, label, rows):
    total = None
    for k in range(8):
        term = jnp.where(label == k, every[k * rows:(k + 1) * rows], 0.0)
        total = term if total is None else total + term
    return total


def stacked(value):
    first, second = split(value)
    rest = jnp.zeros((128 - 3 * FACE, value.shape[1]), BF16)
    return jnp.concatenate([first, second, first, rest], axis=0)


def sources_kernel(gy_size, u_ref, rhs_ref, below_ref, above_ref, label_ref, out_ref, step_ref, lin_ref, x_ref, flow_ref, map_ref):
    planes, rows_y, nodes, columns = u_ref.shape
    place = lax.axis_index("gy")
    node, item = iota((nodes, nodes), 1), iota((nodes, nodes), 0)
    chosen = (node == wanted_node(item // FACE, item % FACE)).astype(BF16)
    own = [u_ref[x, y] for x in range(planes) for y in range(rows_y)]
    other = [below_ref[x, below_ref.shape[1] - 1] for x in range(planes)] + [above_ref[x, 0] for x in range(planes)]
    faces = dot(chosen, jnp.concatenate(own + other, axis=1))
    faces = [faces[:, i * columns:(i + 1) * columns] for i in range(len(own) + len(other))]
    z_at = iota((FACE, columns), 1) % FACE
    has_below = jnp.where(place > 0, 1.0, 0.0)
    has_above = jnp.where(place < gy_size - 1, 1.0, 0.0)
    data = []
    for x in range(planes):
        under = faces[len(own) + x][16:32] * has_below
        over = faces[len(own) + planes + x][0:16] * has_above
        for y in range(rows_y):
            at = x * rows_y + y
            y_flag = label_ref[pl.ds(planes * rows_y + at, 1), :]
            z_flag = label_ref[pl.ds(2 * planes * rows_y + at, 1), :]
            from_below = faces[at - 1][16:32] if y > 0 else under
            from_above = faces[at + 1][0:16] if y < rows_y - 1 else over
            from_front = jnp.where(z_at == 0, 0.0, pltpu.roll(faces[at][48:64], 1, 1))
            from_back = jnp.where(z_at == FACE - 1, 0.0, pltpu.roll(faces[at][32:48], columns - 1, 1))
            lateral = jnp.concatenate(
                [
                    from_below * (1.0 - y_flag),
                    from_above * y_flag,
                    from_front * (1.0 - z_flag),
                    from_back * z_flag,
                ],
                axis=0,
            ).astype(BF16)
            here = jnp.concatenate([rhs_ref[x, y], lateral], axis=0)
            x_ref[x, y] = here
            data.append(here)
    data = jnp.concatenate(data, axis=1)
    every = dot(out_ref[...], jnp.concatenate([data, data], axis=0))
    total = None
    for x in range(planes):
        begin = x * rows_y * columns
        label = jnp.concatenate([label_ref[pl.ds(x * rows_y + y, 1), :] for y in range(rows_y)], axis=1)
        flow = class_sum(every[:, begin:begin + rows_y * columns], label, FACE)
        flow_ref[x] = flow
        if total is not None:
            flow = flow + class_sum(dot(step_ref[...], stacked(total)), label, FACE)
        total = flow
    for y in range(rows_y):
        map_ref[y, 0:FACE] = lin_ref[planes, y]
        map_ref[y, FACE:] = encode(total[:, y * columns:(y + 1) * columns])


def block_diagonal(linear):
    keep = (iota((256, 256), 0) // FACE == iota((256, 256), 1) // FACE).astype(BF16)
    return [jnp.concatenate([part] * 16, axis=0) * keep for part in split(linear)]


def join_blocks(earlier, later):
    high, low = split(jnp.concatenate([earlier, jnp.zeros((8, 256), F32)], axis=0))
    first, second = block_diagonal(later[:FACE])
    parts = dot(jnp.concatenate([high, low], axis=0), first)
    total = (parts[:32] + parts[32:] + dot(high, second))[:24]
    return jnp.concatenate([total[:FACE], total[FACE:] + later[FACE:]], axis=0)


def group_kernel(size, power, *refs):
    blocks, total_ref, held = refs[:size], refs[size], refs[size + 1]
    for s in range(size):
        held[s] = blocks[s][...]
    mine = lax.axis_index("gx") % size
    for y in range(total_ref.shape[0]):
        maps = [held[(mine ^ j) if power else (mine - j + size) % size, y] for j in range(size)]
        while len(maps) > 1:
            maps = [join_blocks(maps[i], maps[i + 1]) if i + 1 < len(maps) else maps[i] for i in range(0, len(maps), 2)]
        total_ref[y] = maps[0]


def solve_kernel(size, power, *refs):
    blocks = refs[:size]
    data_ref, label_ref, weight_ref, lin_ref, flow_ref, inv_ref, inflow_ref = refs[size:size + 7]
    w_ref, start_ref, coup_ref, before_ref, mask_ref, held, full_ref = refs[size + 7:]
    planes, rows_y, nodes, columns = w_ref.shape
    for k in range(inv_ref.shape[0]):
        inv_rows = inv_ref[k]
        products = class_products(inv_rows, weight_ref[:, 256 * k:256 * k + 256])
        here = pl.ds(k * nodes, nodes)
        moved_over = pltpu.roll(products, FACE * k, 1) if k else products
        coupling = jnp.where(iota((nodes, 128), 1) // FACE == k, moved_over, 0.0 if k == 0 else coupling)
        full_ref[here, :] = in_parts(with_inverse(inv_rows, products))
    coup_ref[...] = in_parts(coupling)
    for x in range(planes):
        for y in range(rows_y):
            label = label_ref[pl.ds(x * rows_y + y, 1), :]
            mask_ref[x, y] = jnp.where(iota((128, 128), 0) // FACE == label, 1.0, 0.0).T
            data = data_ref[x, y]
            every = dot(full_ref[...], jnp.concatenate([data, data], axis=0))
            w_ref[x, y] = class_sum(every, label, nodes)
    for s in range(size):
        held[s] = blocks[s][...]
    mine = lax.axis_index("gx") % size
    same = (iota((24, 256), 1) % FACE == iota((24, 256), 0)).astype(F32)
    for y in range(rows_y):
        start_ref[y] = encode(inflow_ref[y])
        before = same
        for j in range(size - 1):
            block = held[(mine ^ j) if power else (mine - j + size) % size, y]
            before = jnp.where(mine > j, block if j == 0 else join(before, block), before)
        for x in range(planes):
            before_ref[x, y] = before
            if x < planes - 1:
                offset = encode(flow_ref[x, :, y * columns:(y + 1) * columns])
                before = join(before, jnp.concatenate([lin_ref[x, y], offset], axis=0))


def finish_kernel(size, inner, power, *refs):
    blocks = refs[:size]
    before_ref, start_ref, w_ref, mask_ref, coup_ref, out_ref, held = refs[size:]
    planes, rows_y, nodes, columns = w_ref.shape
    for s in range(size):
        held[s] = blocks[s][...]
    mine = lax.axis_index("gx") // inner
    traces = []
    for y in range(rows_y):
        trace = start_ref[y]
        for j in range(size - 1):
            slot = (mine ^ j) if power else (mine - j + size) % size
            trace = jnp.where(mine > j, advance(trace, held[slot, y]), trace)
        traces.append(trace)
    entering = [advance(traces[y], before_ref[x, y]) for x in range(planes) for y in range(rows_y)]
    entering = jnp.concatenate(entering, axis=1)
    first, second = split(entering)
    row, lane = iota((256, 2 * FACE), 0), iota((256, 2 * FACE), 1)
    spread = (lane == row % 128 // FACE + FACE * (row >= 128)).astype(BF16)
    rest = jnp.zeros((8, entering.shape[1]), BF16)
    rows = dot(spread, jnp.concatenate([first, rest, second, rest], axis=0))
    keep = iota((256, 256), 0) % FACE == iota((256, 256), 1) // FACE
    fold = (iota((256, 128), 0) % FACE == iota((256, 128), 1) % FACE).astype(BF16)
    parts = [jnp.where(keep, rows[:, at:at + 256], 0.0).astype(BF16) for at in range(0, rows.shape[1], 256)]
    values = dot(jnp.concatenate(parts, axis=0), fold)
    coupling = coup_ref[...]
    for x in range(planes):
        for y in range(rows_y):
            begin = (x * rows_y + y) * 256
            first = (values[begin:begin + 128] * mask_ref[x, y]).astype(BF16)
            second = (values[begin + 128:begin + 256] * mask_ref[x, y]).astype(BF16)
            sums = dot_rows(coupling, jnp.concatenate([first, first], axis=1)) + dot_rows(coupling[:, :128], second)
            out_ref[x, y] = w_ref[x, y] + sums


def moved(value, pairs):
    return lax.ppermute(value, ("gx", "gy"), pairs)


def shape(dims, kind=F32):
    return jax.ShapeDtypeStruct(dims, kind)


def call(kernel, outs, name, args, scratch=(), flops=1000000, limit=48, space=pltpu.VMEM):
    return pl.pallas_call(
        kernel,
        out_shape=outs,
        in_specs=[pl.BlockSpec(memory_space=space)] * len(args),
        out_specs=jax.tree.map(lambda _: pl.BlockSpec(memory_space=pltpu.VMEM), outs),
        scratch_shapes=list(scratch),
        name=name,
        cost_estimate=pl.CostEstimate(flops=flops, bytes_accessed=500000, transcendentals=0),
        compiler_params=pltpu.CompilerParams(vmem_limit_bytes=limit * 1024 * 1024),
    )(*args)


def on_device(gx_size, gy_size, u_old, rhs, classes, flags, inverse, x_face, lateral_faces, inflow):
    planes, rows_y, nodes, columns = u_old.shape
    count = inverse.shape[0]
    everyone = [(x, y) for x in range(gx_size) for y in range(gy_size)]

    def at(x, y):
        return x * gy_size + y

    if gy_size == 2:
        below = above = moved(u_old, [(at(x, y), at(x, 1 - y)) for x, y in everyone])
    else:
        below = moved(u_old[:, rows_y - 1:], [(at(x, y), at(x, y + 1)) for x, y in everyone if y + 1 < gy_size])
        above = moved(u_old[:, :1], [(at(x, y), at(x, y - 1)) for x, y in everyone if y > 0])
    weights, out_rows, step, linear, labels = call(
        params_kernel,
        (
            shape((nodes, count * 256), BF16),
            shape((count * FACE, 256), BF16),
            shape((count * FACE, 128), BF16),
            shape((planes + 1, rows_y, FACE, 256)),
            shape((3 * planes * rows_y, columns)),
        ),
        "class_matrices",
        tuple(
            pltpu.with_memory_space_constraint(value, pltpu.HBM)
            for value in (inverse, x_face, lateral_faces, classes, flags)
        ),
        [
            pltpu.VMEM(inverse.shape, F32),
            pltpu.VMEM(x_face.shape, F32),
            pltpu.VMEM(lateral_faces.shape, F32),
            pltpu.VMEM(classes.shape, jnp.int32),
            pltpu.VMEM(flags.shape, jnp.int32),
            pltpu.SemaphoreType.DMA((5,)),
        ],
        space=pltpu.HBM,
    )
    data, flow, here = call(
        functools.partial(sources_kernel, gy_size),
        (
            shape((planes, rows_y, 128, columns), BF16),
            shape((planes, FACE, rows_y * columns)),
            shape((rows_y, 24, 256)),
        ),
        "sources",
        (u_old, rhs, below, above, labels, out_rows, step, linear),
    )
    inner = 4 if gx_size % 4 == 0 else 1
    outer = gx_size // inner
    power = outer & (outer - 1) == 0
    near = [here]
    for s in range(1, inner):
        near.append(moved(here, [(at(x, y), at(x ^ s, y)) for x, y in everyone]))
    total = call(
        functools.partial(group_kernel, inner, True),
        shape((rows_y, 24, 256)),
        "group_maps",
        tuple(near),
        [pltpu.VMEM((inner, rows_y, 24, 256), F32)],
    )
    blocks = [total]
    for s in range(1, outer):
        if power:
            pairs = [(at(x, y), at(x ^ (s * inner), y)) for x, y in everyone]
        else:
            pairs = [(at(x, y), at((x + s * inner) % gx_size, y)) for x, y in everyone]
        blocks.append(moved(total, pairs))
    solved, start, coup, before, masks = call(
        functools.partial(solve_kernel, inner, True),
        (
            shape((planes, rows_y, nodes, columns)),
            shape((rows_y, 8, 256)),
            shape((nodes, 256), BF16),
            shape((planes, rows_y, 24, 256)),
            shape((planes, rows_y, 128, 128)),
        ),
        "local_solve",
        tuple(near) + (data, labels, weights, linear, flow, inverse, inflow),
        [pltpu.VMEM((inner, rows_y, 24, 256), F32), pltpu.VMEM((count * nodes, 256), BF16)],
    )
    return call(
        functools.partial(finish_kernel, outer, inner, power),
        shape((planes, rows_y, nodes, columns)),
        "finish",
        tuple(blocks) + (before, start, solved, masks, coup),
        [pltpu.VMEM((outer, rows_y, 24, 256), F32)],
    )


def solution(mesh):
    in_specs = (
        P("gx", "gy", None, None),
        P("gx", "gy", None, None),
        P("gx", "gy", None),
        P(None, "gx", "gy", None),
        P(),
        P(),
        P(),
        P("gy", None, None),
    )
    out_specs = P("gx", "gy", None, None)
    body = functools.partial(on_device, mesh.shape["gx"], mesh.shape["gy"])
    return jax.shard_map(body, mesh=mesh, in_specs=in_specs, out_specs=out_specs, check_vma=False)
```

time: 31.8 us -> 23.3 us (0.73)
  Pallas kernels: 12.2 us -> 7.38 us
  local copies, waits for them, and re-layouts: 3.41 us -> 0.02 us
    pallas_call x5, Pallas kernels: 12.2 us -> 7.38 us  [call(): pl.pallas_call(kernel, out_shape=outs, in_specs=[pl.BlockSpec(memory_spac...]
    unnamed x16 -> x8, local copies, waits for them, and re-layouts: 3.41 us -> 0.02 us
  transfers between devices with their start and end apart: 7 -> 7, of which waited for: 5 -> 5; matrix products, arithmetic and copies ran while one was open for 0% -> 0% of each run, Pallas kernels for 9% -> 16%
where the time goes in v2:
time: 23.3 us; the launch traced here: 23.1 us
  starting transfers between devices  8.95 us (38%)
  Pallas kernels  7.38 us (32%)
  waiting for transfers between devices  6.73 us (29%)
    ppermute x7, starting transfers between devices, moved(): return lax.ppermute(value, ('gx', 'gy'), pairs)  8.95 us
    pallas_call x5, Pallas kernels, call(): pl.pallas_call(kernel, out_shape=outs, in_specs=[pl.BlockSpec(memory_spac...  7.38 us
    ppermute x7, waiting for transfers between devices, moved(): return lax.ppermute(value, ('gx', 'gy'), pairs)  6.73 us
  transfers between devices with their start and end apart: 7, of which 5 were waited for; matrix products, arithmetic and copies ran while one was open for 0% of the time, Pallas kernels for 16%

profile of v2, /device:TPU:0, one launch (start us, length us, event | category | flops | bytes accessed | tf_op | source)
XLA Modules:
  0.0 23.1 jit_solution(6704009402764170268)
XLA Ops:
  0.0 0.5 %collective-permute-start = (bf16[2,2,64,128]{3,2,1,0:T(8,128)(2,1)}, bf16[2,2,64,128]{3,2,1,0:T(8,128)(2,1)S(1)}, u32[]{:S(2)}, u32[]{:S(2)}) collective-permute-start(bf16[2,2,64,128]{3,2,1,0:T(8,128)(2,1)} %u_ref.1), channel_id=1, source_target_pairs={{0,1},{1,0},{2,3},{3,2},{4,5},{5,4},{6,7},{7,6},{8,9},{9,8},{10,11... | collective-permute-start | bytes 196616 | tf_op jit(solution)/shard_map/ppermute | solution.py:323
  0.5 2.3 %class_matrices.1 = (bf16[64,2048]{1,0:T(8,128)(2,1)S(1)}, bf16[128,256]{1,0:T(8,128)(2,1)S(1)}, bf16[128,128]{1,0:T(8,128)(2,1)S(1)}, f32[3,2,16,256]{3,2,1,0:T(8,128)S(1)}, f32[12,128]{1,0:T(8,128)S(1)}) custom-call(f32[8,64,64]{2,1,0:T(8,128)} %refs_9_.1, f32[8,16,16]{2,1,0:T(8,128)} %x_hbm.1, f32[4,8,16,16]{3,2,1,0:T(8,128)} %lat_hbm.1, ...), custom_call_target="tpu_custom_call" | custom-call | flops 1000000 | bytes 500000 | tf_op jit(solution)/shard_map/class_matrices/pallas_call | solution.py:331
  2.8 0.0 collective-permute-done.below_ref.above_ref
  2.8 0.0 copy-done.1
  2.8 0.0 copy-done.2
  2.8 0.0 copy-start
  2.9 0.9 %sources.1 = (bf16[2,2,128,128]{3,2,1,0:T(8,128)(2,1)S(1)}, f32[2,16,256]{2,1,0:T(8,128)S(1)}, f32[2,24,256]{2,1,0:T(8,128)S(1)}) custom-call(bf16[2,2,64,128]{3,2,1,0:T(8,128)(2,1)S(1)} %copy-done.1, bf16[2,2,64,128]{3,2,1,0:T(8,128)(2,1)S(1)} %copy-done.2, bf16[2,2,64,128]{3,2,1,0:T(8,128)(2,1)S(1)} %collective-permute-done.below_ref.above_ref, ...), custom_call_target="tpu_custom_call" | custom-call | flops 1000000 | bytes 500000 | tf_op jit(solution)/shard_map/sources/pallas_call | solution.py:331
  3.8 3.5 %collective-permute-start.3 = (f32[2,24,256]{2,1,0:T(8,128)S(1)}, f32[2,24,256]{2,1,0:T(8,128)S(1)}, u32[]{:S(2)}, u32[]{:S(2)}) collective-permute-start(f32[2,24,256]{2,1,0:T(8,128)S(1)} %get-tuple-element.22.refs_0_), channel_id=1, source_target_pairs={{0,6},{1,7},{2,4},{3,5},{4,2},{5,3},{6,0},{7,1},{8,14},{9,15},{10,... | collective-permute-start | bytes 147464 | tf_op jit(solution)/shard_map/ppermute | solution.py:323
  7.3 0.5 %collective-permute-start.2 = (f32[2,24,256]{2,1,0:T(8,128)S(1)}, f32[2,24,256]{2,1,0:T(8,128)S(1)}, u32[]{:S(2)}, u32[]{:S(2)}) collective-permute-start(f32[2,24,256]{2,1,0:T(8,128)S(1)} %get-tuple-element.22.refs_0_), channel_id=1, source_target_pairs={{0,4},{1,5},{2,6},{3,7},{4,0},{5,1},{6,2},{7,3},{8,12},{9,13},{10,... | collective-permute-start | bytes 147464 | tf_op jit(solution)/shard_map/ppermute | solution.py:323
  7.8 0.1 collective-permute-start.1
  7.9 1.8 %collective-permute-done.3.refs_3_ = f32[2,24,256]{2,1,0:T(8,128)S(1)} collective-permute-done((f32[2,24,256]{2,1,0:T(8,128)S(1)}, f32[2,24,256]{2,1,0:T(8,128)S(1)}, u32[]{:S(2)}, u32[]{:S(2)}) %collective-permute-start.3) | collective-permute-done | bytes 49184 | tf_op jit(solution)/shard_map/ppermute | solution.py:323
  9.6 1.7 %collective-permute-done.2.refs_2_ = f32[2,24,256]{2,1,0:T(8,128)S(1)} collective-permute-done((f32[2,24,256]{2,1,0:T(8,128)S(1)}, f32[2,24,256]{2,1,0:T(8,128)S(1)}, u32[]{:S(2)}, u32[]{:S(2)}) %collective-permute-start.2) | collective-permute-done | bytes 49184 | tf_op jit(solution)/shard_map/ppermute | solution.py:323
  11.4 0.5 %collective-permute-done.1.refs_1_ = f32[2,24,256]{2,1,0:T(8,128)S(1)} collective-permute-done((f32[2,24,256]{2,1,0:T(8,128)S(1)}, f32[2,24,256]{2,1,0:T(8,128)S(1)}, u32[]{:S(2)}, u32[]{:S(2)}) %collective-permute-start.1) | collective-permute-done | bytes 49184 | tf_op jit(solution)/shard_map/ppermute | solution.py:323
  11.9 0.5 %group_maps.1.refs_0_ = f32[2,24,256]{2,1,0:T(8,128)S(1)} custom-call(f32[2,24,256]{2,1,0:T(8,128)S(1)} %get-tuple-element.22.refs_0_, f32[2,24,256]{2,1,0:T(8,128)S(1)} %collective-permute-done.1.refs_1_, f32[2,24,256]{2,1,0:T(8,128)S(1)} %collective-permute-done.2.refs_2_, f32[2,24,256]{2,1,0:T(8,128)S(1)} %collective-permute-done.3.refs_3_), custom_call_target="tpu_custom_call" | custom-call | flops 1000000 | bytes 500000 | tf_op jit(solution)/shard_map/group_maps/pallas_call | solution.py:331
  12.4 3.6 %collective-permute-start.6 = (f32[2,24,256]{2,1,0:T(8,128)S(1)}, f32[2,24,256]{2,1,0:T(8,128)S(1)}, u32[]{:S(2)}, u32[]{:S(2)}) collective-permute-start(f32[2,24,256]{2,1,0:T(8,128)S(1)} %group_maps.1.refs_0_), channel_id=1, source_target_pairs={{0,24},{1,25},{2,26},{3,27},{4,28},{5,29},{6,30},{7,31},{8,16},{9,... | collective-permute-start | bytes 147464 | tf_op jit(solution)/shard_map/ppermute | solution.py:323
  16.0 0.0 collective-permute-start.5
  16.0 0.8 %collective-permute-start.4 = (f32[2,24,256]{2,1,0:T(8,128)S(1)}, f32[2,24,256]{2,1,0:T(8,128)S(1)}, u32[]{:S(2)}, u32[]{:S(2)}) collective-permute-start(f32[2,24,256]{2,1,0:T(8,128)S(1)} %group_maps.1.refs_0_), channel_id=1, source_target_pairs={{0,8},{1,9},{2,10},{3,11},{4,12},{5,13},{6,14},{7,15},{8,0},{9,1},... | collective-permute-start | bytes 147464 | tf_op jit(solution)/shard_map/ppermute | solution.py:323
  16.8 0.0 copy-done
  16.8 0.0 copy-done.3
  16.8 1.5 %local_solve.1 = (f32[2,2,64,128]{3,2,1,0:T(8,128)S(1)}, f32[2,8,256]{2,1,0:T(8,128)S(1)}, bf16[64,256]{1,0:T(8,128)(2,1)S(1)}, f32[2,2,24,256]{3,2,1,0:T(8,128)S(1)}, f32[2,2,128,128]{3,2,1,0:T(8,128)S(1)}) custom-call(f32[2,24,256]{2,1,0:T(8,128)S(1)} %get-tuple-element.22.refs_0_, f32[2,24,256]{2,1,0:T(8,128)S(1)} %collective-permute-done.1.refs_1_, ...), custom_call_target="tpu_custom_call" | custom-call | flops 1000000 | bytes 500000 | tf_op jit(solution)/shard_map/local_solve/pallas_call | solution.py:331
  18.2 0.1 collective-permute-done.6.refs_3_
  18.3 2.7 %collective-permute-done.5.refs_2_ = f32[2,24,256]{2,1,0:T(8,128)S(1)} collective-permute-done((f32[2,24,256]{2,1,0:T(8,128)S(1)}, f32[2,24,256]{2,1,0:T(8,128)S(1)}, u32[]{:S(2)}, u32[]{:S(2)}) %collective-permute-start.5) | collective-permute-done | bytes 49184 | tf_op jit(solution)/shard_map/ppermute | solution.py:323
  21.0 0.0 collective-permute-done.4.refs_1_
  21.0 2.2 %finish.1 = f32[2,2,64,128]{3,2,1,0:T(8,128)} custom-call(f32[2,24,256]{2,1,0:T(8,128)S(1)} %group_maps.1.refs_0_, f32[2,24,256]{2,1,0:T(8,128)S(1)} %collective-permute-done.4.refs_1_, f32[2,24,256]{2,1,0:T(8,128)S(1)} %collective-permute-done.5.refs_2_, f32[2,24,256]{2,1,0:T(8,128)S(1)} %collective-permute-done.6.refs_3_, ...), custom_call_target="tpu_custom_call" | custom-call | flops 1000000 | bytes 500000 | tf_op jit(solution)/shard_map/finish/pallas_call | solution.py:331
  (3 shorter events, 0.0 us)
Async XLA Ops:
  0.0 2.8 %copy-start.1 = (bf16[2,2,64,128]{3,2,1,0:T(8,128)(2,1)S(1)}, bf16[2,2,64,128]{3,2,1,0:T(8,128)(2,1)}, u32[]{:S(2)}) copy-start(bf16[2,2,64,128]{3,2,1,0:T(8,128)(2,1)} %u_ref.1) | copy-start | bytes 196612
  0.0 2.8 %copy-start.2 = (bf16[2,2,64,128]{3,2,1,0:T(8,128)(2,1)S(1)}, bf16[2,2,64,128]{3,2,1,0:T(8,128)(2,1)}, u32[]{:S(2)}) copy-start(bf16[2,2,64,128]{3,2,1,0:T(8,128)(2,1)} %rhs_ref.1) | copy-start | bytes 196612
  0.0 2.8 %collective-permute-start = (bf16[2,2,64,128]{3,2,1,0:T(8,128)(2,1)}, bf16[2,2,64,128]{3,2,1,0:T(8,128)(2,1)S(1)}, u32[]{:S(2)}, u32[]{:S(2)}) collective-permute-start(bf16[2,2,64,128]{3,2,1,0:T(8,128)(2,1)} %u_ref.1), channel_id=1, source_target_pairs={{0,1},{1,0},{2,3},{3,2},{4,5},{5,4},{6,7},{7,6},{8,9},{9,8},{10,11... | collective-permute-start | bytes 196616 | tf_op jit(solution)/shard_map/ppermute | solution.py:323
  2.8 13.9 %copy-start = (f32[8,64,64]{2,1,0:T(8,128)S(1)}, f32[8,64,64]{2,1,0:T(8,128)}, u32[]{:S(2)}) copy-start(f32[8,64,64]{2,1,0:T(8,128)} %refs_9_.1) | copy-start | bytes 393220
  3.8 5.9 %collective-permute-start.3 = (f32[2,24,256]{2,1,0:T(8,128)S(1)}, f32[2,24,256]{2,1,0:T(8,128)S(1)}, u32[]{:S(2)}, u32[]{:S(2)}) collective-permute-start(f32[2,24,256]{2,1,0:T(8,128)S(1)} %get-tuple-element.22.refs_0_), channel_id=1, source_target_pairs={{0,6},{1,7},{2,4},{3,5},{4,2},{5,3},{6,0},{7,1},{8,14},{9,15},{10,... | collective-permute-start | bytes 147464 | tf_op jit(solution)/shard_map/ppermute | solution.py:323
  7.3 4.1 %collective-permute-start.2 = (f32[2,24,256]{2,1,0:T(8,128)S(1)}, f32[2,24,256]{2,1,0:T(8,128)S(1)}, u32[]{:S(2)}, u32[]{:S(2)}) collective-permute-start(f32[2,24,256]{2,1,0:T(8,128)S(1)} %get-tuple-element.22.refs_0_), channel_id=1, source_target_pairs={{0,4},{1,5},{2,6},{3,7},{4,0},{5,1},{6,2},{7,3},{8,12},{9,13},{10,... | collective-permute-start | bytes 147464 | tf_op jit(solution)/shard_map/ppermute | solution.py:323
  7.8 4.1 %collective-permute-start.1 = (f32[2,24,256]{2,1,0:T(8,128)S(1)}, f32[2,24,256]{2,1,0:T(8,128)S(1)}, u32[]{:S(2)}, u32[]{:S(2)}) collective-permute-start(f32[2,24,256]{2,1,0:T(8,128)S(1)} %get-tuple-element.22.refs_0_), channel_id=1, source_target_pairs={{0,2},{1,3},{2,0},{3,1},{4,6},{5,7},{6,4},{7,5},{8,10},{9,11},{10,... | collective-permute-start | bytes 147464 | tf_op jit(solution)/shard_map/ppermute | solution.py:323
  11.9 4.9 %copy-start.3 = (f32[2,16,128]{2,1,0:T(8,128)S(1)}, f32[2,16,128]{2,1,0:T(8,128)}, u32[]{:S(2)}) copy-start(f32[2,16,128]{2,1,0:T(8,128)} %refs_10_.1) | copy-start | bytes 49156
  12.4 5.9 %collective-permute-start.6 = (f32[2,24,256]{2,1,0:T(8,128)S(1)}, f32[2,24,256]{2,1,0:T(8,128)S(1)}, u32[]{:S(2)}, u32[]{:S(2)}) collective-permute-start(f32[2,24,256]{2,1,0:T(8,128)S(1)} %group_maps.1.refs_0_), channel_id=1, source_target_pairs={{0,24},{1,25},{2,26},{3,27},{4,28},{5,29},{6,30},{7,31},{8,16},{9,... | collective-permute-start | bytes 147464 | tf_op jit(solution)/shard_map/ppermute | solution.py:323
  16.0 5.0 %collective-permute-start.5 = (f32[2,24,256]{2,1,0:T(8,128)S(1)}, f32[2,24,256]{2,1,0:T(8,128)S(1)}, u32[]{:S(2)}, u32[]{:S(2)}) collective-permute-start(f32[2,24,256]{2,1,0:T(8,128)S(1)} %group_maps.1.refs_0_), channel_id=1, source_target_pairs={{0,16},{1,17},{2,18},{3,19},{4,20},{5,21},{6,22},{7,23},{8,24},{9,... | collective-permute-start | bytes 147464 | tf_op jit(solution)/shard_map/ppermute | solution.py:323
  16.0 5.0 %collective-permute-start.4 = (f32[2,24,256]{2,1,0:T(8,128)S(1)}, f32[2,24,256]{2,1,0:T(8,128)S(1)}, u32[]{:S(2)}, u32[]{:S(2)}) collective-permute-start(f32[2,24,256]{2,1,0:T(8,128)S(1)} %group_maps.1.refs_0_), channel_id=1, source_target_pairs={{0,8},{1,9},{2,10},{3,11},{4,12},{5,13},{6,14},{7,15},{8,0},{9,1},... | collective-permute-start | bytes 147464 | tf_op jit(solution)/shard_map/ppermute | solution.py:323

commit v3 on v2

--- a/solution.py
+++ b/solution.py
@@ -247,76 +247,122 @@
         total_ref[y] = maps[0]
 
 
+def carried(parts, traces, count):
+    first, second = split(jnp.concatenate(traces, axis=1))
+    row, lane = iota((256, 2 * FACE), 0), iota((256, 2 * FACE), 1)
+    spread = (lane == row % 128 // FACE + FACE * (row >= 128)).astype(BF16)
+    rest = jnp.zeros((8, first.shape[1]), BF16)
+    rows = dot(spread, jnp.concatenate([first, rest, second, rest], axis=0))
+    keep = iota((256, 256), 0) % FACE == iota((256, 256), 1) // FACE
+    sums = []
+    for y, part in enumerate(parts):
+        here = jnp.where(keep, rows[:, y * 256:y * 256 + 256], 0.0).astype(BF16)
+        high = part[:count]
+        by_first = dot_rows(part, here[:128])
+        sums.append(by_first[:count] + by_first[count:] + dot_rows(high, here[128:]))
+    return sums
+
+
+def write_nodes(result_ref, out_ref, sems, base_ref, part_ref, traces):
+    planes, rows_y, nodes, _ = result_ref.shape
+    sums = carried([part_ref[y] for y in range(rows_y)], traces, planes * nodes)
+    copies = []
+    for y in range(rows_y):
+        for x in range(planes):
+            result_ref[x, y] = base_ref[x, y] + sums[y][x * nodes:(x + 1) * nodes]
+            copies.append(pltpu.make_async_copy(result_ref.at[x, y], out_ref.at[x, y], sems.at[x, y]))
+            copies[-1].start()
+    for copy in copies:
+        copy.wait()
+
+
 def solve_kernel(size, power, *refs):
     blocks = refs[:size]
     data_ref, label_ref, weight_ref, lin_ref, flow_ref, inv_ref, inflow_ref = refs[size:size + 7]
-    w_ref, start_ref, coup_ref, before_ref, mask_ref, held, full_ref = refs[size + 7:]
-    planes, rows_y, nodes, columns = w_ref.shape
+    base_ref, start_ref, part_ref, out_ref, held, full_ref, result_ref, sems = refs[size + 7:]
+    planes, rows_y, nodes, columns = base_ref.shape
+    coupling = jnp.zeros((nodes, 128), F32)
     for k in range(inv_ref.shape[0]):
         inv_rows = inv_ref[k]
         products = class_products(inv_rows, weight_ref[:, 256 * k:256 * k + 256])
         here = pl.ds(k * nodes, nodes)
-        moved_over = pltpu.roll(products, FACE * k, 1) if k else products
-        coupling = jnp.where(iota((nodes, 128), 1) // FACE == k, moved_over, 0.0 if k == 0 else coupling)
+        shifted = pltpu.roll(products, FACE * k, 1) if k else products
+        coupling = jnp.where(iota((nodes, 128), 1) // FACE == k, shifted, coupling)
         full_ref[here, :] = in_parts(with_inverse(inv_rows, products))
-    coup_ref[...] = in_parts(coupling)
-    for x in range(planes):
-        for y in range(rows_y):
-            label = label_ref[pl.ds(x * rows_y + y, 1), :]
-            mask_ref[x, y] = jnp.where(iota((128, 128), 0) // FACE == label, 1.0, 0.0).T
-            data = data_ref[x, y]
-            every = dot(full_ref[...], jnp.concatenate([data, data], axis=0))
-            w_ref[x, y] = class_sum(every, label, nodes)
+    coupling = jnp.concatenate(split(coupling), axis=0)
     for s in range(size):
         held[s] = blocks[s][...]
-    mine = lax.axis_index("gx") % size
+    place = lax.axis_index("gx")
+    mine = place % size
     same = (iota((24, 256), 1) % FACE == iota((24, 256), 0)).astype(F32)
+    wide = (iota((FACE, 256), 1) // FACE == iota((FACE, 256), 0)).astype(BF16)
+    row, lane = iota((128, 256), 0), iota((128, 256), 1)
+    starts = []
     for y in range(rows_y):
-        start_ref[y] = encode(inflow_ref[y])
+        start = encode(inflow_ref[y])
+        start_ref[y] = start
+        starts.append(start)
         before = same
         for j in range(size - 1):
             block = held[(mine ^ j) if power else (mine - j + size) % size, y]
-            before = jnp.where(mine > j, block if j == 0 else join(before, block), before)
+            before = jnp.where(mine > j, block if j == 0 else join_blocks(before, block), before)
         for x in range(planes):
-            before_ref[x, y] = before
+            at = x * rows_y + y
+            label = label_ref[pl.ds(at, 1), :]
+            data = data_ref[x, y]
+            every = dot(full_ref[...], jnp.concatenate([data, data], axis=0))
+            local = class_sum(every, label, nodes)
+            on_wide = dot(label[:, :FACE].astype(BF16), wide).astype(jnp.int32)
+            pick = jnp.where((row % FACE == lane % FACE) & (row // FACE == on_wide), 1.0, 0.0).astype(BF16)
+            chosen = dot(coupling, pick).astype(BF16)
+            local = local + carried([chosen], [before[FACE:]], nodes)[0]
+            base_ref[x, y] = local
+            first, second = block_diagonal(before[:FACE])
+            products = dot_rows(chosen, first)
+            products = products[:nodes] + products[nodes:] + dot_rows(chosen[:nodes], second)
+            high, low = split(products)
+            part_ref[y, pl.ds(x * nodes, nodes), :] = high
+            part_ref[y, pl.ds((planes + x) * nodes, nodes), :] = low
             if x < planes - 1:
                 offset = encode(flow_ref[x, :, y * columns:(y + 1) * columns])
-                before = join(before, jnp.concatenate([lin_ref[x, y], offset], axis=0))
+                before = join_blocks(before, jnp.concatenate([lin_ref[x, y], offset], axis=0))
+
+    @pl.when(place < size)
+    def _():
+        write_nodes(result_ref, out_ref, sems, base_ref, part_ref, [start_ref[y] for y in range(rows_y)])
 
 
 def finish_kernel(size, inner, power, *refs):
     blocks = refs[:size]
-    before_ref, start_ref, w_ref, mask_ref, coup_ref, out_ref, held = refs[size:]
-    planes, rows_y, nodes, columns = w_ref.shape
-    for s in range(size):
-        held[s] = blocks[s][...]
+    start_ref, base_ref, part_ref, _, out_ref, result_ref, sems = refs[size:size + 7]
+    rows_y = base_ref.shape[1]
     mine = lax.axis_index("gx") // inner
-    traces = []
-    for y in range(rows_y):
-        trace = start_ref[y]
-        for j in range(size - 1):
-            slot = (mine ^ j) if power else (mine - j + size) % size
-            trace = jnp.where(mine > j, advance(trace, held[slot, y]), trace)
-        traces.append(trace)
-    entering = [advance(traces[y], before_ref[x, y]) for x in range(planes) for y in range(rows_y)]
-    entering = jnp.concatenate(entering, axis=1)
-    first, second = split(entering)
-    row, lane = iota((256, 2 * FACE), 0), iota((256, 2 * FACE), 1)
-    spread = (lane == row % 128 // FACE + FACE * (row >= 128)).astype(BF16)
-    rest = jnp.zeros((8, entering.shape[1]), BF16)
-    rows = dot(spread, jnp.concatenate([first, rest, second, rest], axis=0))
-    keep = iota((256, 256), 0) % FACE == iota((256, 256), 1) // FACE
-    fold = (iota((256, 128), 0) % FACE == iota((256, 128), 1) % FACE).astype(BF16)
-    parts = [jnp.where(keep, rows[:, at:at + 256], 0.0).astype(BF16) for at in range(0, rows.shape[1], 256)]
-    values = dot(jnp.concatenate(parts, axis=0), fold)
-    coupling = coup_ref[...]
-    for x in range(planes):
-        for y in range(rows_y):
-            begin = (x * rows_y + y) * 256
-            first = (values[begin:begin + 128] * mask_ref[x, y]).astype(BF16)
-            second = (values[begin + 128:begin + 256] * mask_ref[x, y]).astype(BF16)
-            sums = dot_rows(coupling, jnp.concatenate([first, first], axis=1)) + dot_rows(coupling[:, :128], second)
-            out_ref[x, y] = w_ref[x, y] + sums
+    if power and size <= 4:
+        for place in range(1, size):
+            @pl.when(mine == place)
+            def _():
+                traces = []
+                for y in range(rows_y):
+                    trace = start_ref[y]
+                    for j in range(place):
+                        trace = advance(trace, blocks[place ^ j][y])
+                    traces.append(trace)
+                write_nodes(result_ref, out_ref, sems, base_ref, part_ref, traces)
+    else:
+        held = refs[size + 7]
+        for s in range(size):
+            held[s] = blocks[s][...]
+
+        @pl.when(mine > 0)
+        def _():
+            traces = []
+            for y in range(rows_y):
+                trace = start_ref[y]
+                for j in range(size - 1):
+                    slot = (mine ^ j) if power else (mine - j + size) % size
+                    trace = jnp.where(mine > j, advance(trace, held[slot, y]), trace)
+                traces.append(trace)
+            write_nodes(result_ref, out_ref, sems, base_ref, part_ref, traces)
 
 
 def moved(value, pairs):
@@ -327,15 +373,26 @@
     return jax.ShapeDtypeStruct(dims, kind)
 
 
-def call(kernel, outs, name, args, scratch=(), flops=1000000, limit=48, space=pltpu.VMEM):
+def call(kernel, outs, name, args, scratch=(), space=pltpu.VMEM, out_spaces=None, aliases=None, limit=48):
+    many = isinstance(outs, tuple)
+    spaces = out_spaces or ((pltpu.VMEM,) * len(outs) if many else pltpu.VMEM)
+    if isinstance(space, tuple):
+        in_specs = [pl.BlockSpec(memory_space=one) for one in space]
+    else:
+        in_specs = [pl.BlockSpec(memory_space=space)] * len(args)
+    if many:
+        out_specs = tuple(pl.BlockSpec(memory_space=one) for one in spaces)
+    else:
+        out_specs = pl.BlockSpec(memory_space=spaces)
     return pl.pallas_call(
         kernel,
         out_shape=outs,
-        in_specs=[pl.BlockSpec(memory_space=space)] * len(args),
-        out_specs=jax.tree.map(lambda _: pl.BlockSpec(memory_space=pltpu.VMEM), outs),
+        in_specs=in_specs,
+        out_specs=out_specs,
         scratch_shapes=list(scratch),
+        input_output_aliases=aliases or {},
         name=name,
-        cost_estimate=pl.CostEstimate(flops=flops, bytes_accessed=500000, transcendentals=0),
+        cost_estimate=pl.CostEstimate(flops=1000000, bytes_accessed=500000, transcendentals=0),
         compiler_params=pltpu.CompilerParams(vmem_limit_bytes=limit * 1024 * 1024),
     )(*args)
 
@@ -407,25 +464,32 @@
         else:
             pairs = [(at(x, y), at((x + s * inner) % gx_size, y)) for x, y in everyone]
         blocks.append(moved(total, pairs))
-    solved, start, coup, before, masks = call(
+    nodes_shape = (planes, rows_y, nodes, columns)
+    writing = [pltpu.VMEM(nodes_shape, F32), pltpu.SemaphoreType.DMA((planes, rows_y))]
+    base, start, parts, out = call(
         functools.partial(solve_kernel, inner, True),
         (
-            shape((planes, rows_y, nodes, columns)),
+            shape(nodes_shape),
             shape((rows_y, 8, 256)),
-            shape((nodes, 256), BF16),
-            shape((planes, rows_y, 24, 256)),
-            shape((planes, rows_y, 128, 128)),
+            shape((rows_y, 2 * planes * nodes, 256), BF16),
+            pltpu.HBM(nodes_shape, F32),
         ),
         "local_solve",
         tuple(near) + (data, labels, weights, linear, flow, inverse, inflow),
-        [pltpu.VMEM((inner, rows_y, 24, 256), F32), pltpu.VMEM((count * nodes, 256), BF16)],
+        [pltpu.VMEM((inner, rows_y, 24, 256), F32), pltpu.VMEM((count * nodes, 256), BF16)] + writing,
+        out_spaces=(pltpu.VMEM, pltpu.VMEM, pltpu.VMEM, pltpu.HBM),
     )
+    held = [] if power and outer <= 4 else [pltpu.VMEM((outer, rows_y, 24, 256), F32)]
+    args = tuple(blocks) + (start, base, parts, out)
     return call(
         functools.partial(finish_kernel, outer, inner, power),
-        shape((planes, rows_y, nodes, columns)),
+        pltpu.HBM(nodes_shape, F32),
         "finish",
-        tuple(blocks) + (before, start, solved, masks, coup),
-        [pltpu.VMEM((outer, rows_y, 24, 256), F32)],
+        args,
+        writing + held,
+        space=(pltpu.VMEM,) * (len(args) - 1) + (pltpu.HBM,),
+        out_spaces=pltpu.HBM,
+        aliases={len(args) - 1: 0},
     )
 
 

time: 23.3 us -> 21.2 us (0.910)
  waiting for transfers between devices: 6.73 us -> 4.1 us
  Pallas kernels: 7.38 us -> 7.88 us
    ppermute x7, waiting for transfers between devices: 6.73 us -> 4.1 us  [moved(): return lax.ppermute(value, ('gx', 'gy'), pairs)]
    pallas_call x5, Pallas kernels: 7.38 us -> 7.88 us  [call(): pl.pallas_call(kernel, out_shape=outs, in_specs=in_specs, out_specs=out_s...]
  transfers between devices with their start and end apart: 7 -> 7, of which waited for: 5 -> 4; matrix products, arithmetic and copies ran while one was open for 0% -> 0% of each run, Pallas kernels for 16% -> 31%
where the time goes in v3:
time: 21.2 us; the launch traced here: 21 us
  starting transfers between devices  8.95 us (42%)
  Pallas kernels  7.88 us (37%)
  waiting for transfers between devices  4.1 us (19%)
    ppermute x7, starting transfers between devices, moved(): return lax.ppermute(value, ('gx', 'gy'), pairs)  8.95 us
    pallas_call x5, Pallas kernels, call(): pl.pallas_call(kernel, out_shape=outs, in_specs=in_specs, out_specs=out_s...  7.88 us
    ppermute x7, waiting for transfers between devices, moved(): return lax.ppermute(value, ('gx', 'gy'), pairs)  4.1 us
  transfers between devices with their start and end apart: 7, of which 4 were waited for; matrix products, arithmetic and copies ran while one was open for 0% of the time, Pallas kernels for 31%

profile of v3, /device:TPU:0, one launch (start us, length us, event | category | flops | bytes accessed | tf_op | source)
XLA Modules:
  0.0 21.0 jit_solution(15819270099000366620)
XLA Ops:
  0.0 0.0 copy-start.1
  0.0 0.5 %collective-permute-start = (bf16[2,2,64,128]{3,2,1,0:T(8,128)(2,1)}, bf16[2,2,64,128]{3,2,1,0:T(8,128)(2,1)S(1)}, u32[]{:S(2)}, u32[]{:S(2)}) collective-permute-start(bf16[2,2,64,128]{3,2,1,0:T(8,128)(2,1)} %u_ref.1), channel_id=1, source_target_pairs={{0,1},{1,0},{2,3},{3,2},{4,5},{5,4},{6,7},{7,6},{8,9},{9,8},{10,11... | collective-permute-start | bytes 196616 | tf_op jit(solution)/shard_map/ppermute | solution.py:369
  0.5 2.3 %class_matrices.1 = (bf16[64,2048]{1,0:T(8,128)(2,1)S(1)}, bf16[128,256]{1,0:T(8,128)(2,1)S(1)}, bf16[128,128]{1,0:T(8,128)(2,1)S(1)}, f32[3,2,16,256]{3,2,1,0:T(8,128)S(1)}, f32[12,128]{1,0:T(8,128)S(1)}) custom-call(f32[8,64,64]{2,1,0:T(8,128)} %refs_9_.1, f32[8,16,16]{2,1,0:T(8,128)} %x_hbm.1, f32[4,8,16,16]{3,2,1,0:T(8,128)} %lat_hbm.1, ...), custom_call_target="tpu_custom_call" | custom-call | flops 1000000 | bytes 500000 | tf_op jit(solution)/shard_map/class_matrices/pallas_call | solution.py:387
  2.8 0.0 collective-permute-done.below_ref.above_ref
  2.8 0.0 copy-done.1
  2.8 0.0 copy-done.2
  2.8 0.0 copy-start
  2.9 0.9 %sources.1 = (bf16[2,2,128,128]{3,2,1,0:T(8,128)(2,1)S(1)}, f32[2,16,256]{2,1,0:T(8,128)S(1)}, f32[2,24,256]{2,1,0:T(8,128)S(1)}) custom-call(bf16[2,2,64,128]{3,2,1,0:T(8,128)(2,1)S(1)} %copy-done.1, bf16[2,2,64,128]{3,2,1,0:T(8,128)(2,1)S(1)} %copy-done.2, bf16[2,2,64,128]{3,2,1,0:T(8,128)(2,1)S(1)} %collective-permute-done.below_ref.above_ref, ...), custom_call_target="tpu_custom_call" | custom-call | flops 1000000 | bytes 500000 | tf_op jit(solution)/shard_map/sources/pallas_call | solution.py:387
  3.8 3.5 %collective-permute-start.3 = (f32[2,24,256]{2,1,0:T(8,128)S(1)}, f32[2,24,256]{2,1,0:T(8,128)S(1)}, u32[]{:S(2)}, u32[]{:S(2)}) collective-permute-start(f32[2,24,256]{2,1,0:T(8,128)S(1)} %get-tuple-element.21.refs_0_), channel_id=1, source_target_pairs={{0,6},{1,7},{2,4},{3,5},{4,2},{5,3},{6,0},{7,1},{8,14},{9,15},{10,... | collective-permute-start | bytes 147464 | tf_op jit(solution)/shard_map/ppermute | solution.py:369
  7.3 0.5 %collective-permute-start.2 = (f32[2,24,256]{2,1,0:T(8,128)S(1)}, f32[2,24,256]{2,1,0:T(8,128)S(1)}, u32[]{:S(2)}, u32[]{:S(2)}) collective-permute-start(f32[2,24,256]{2,1,0:T(8,128)S(1)} %get-tuple-element.21.refs_0_), channel_id=1, source_target_pairs={{0,4},{1,5},{2,6},{3,7},{4,0},{5,1},{6,2},{7,3},{8,12},{9,13},{10,... | collective-permute-start | bytes 147464 | tf_op jit(solution)/shard_map/ppermute | solution.py:369
  7.8 0.1 collective-permute-start.1
  7.9 1.8 %collective-permute-done.3.refs_3_ = f32[2,24,256]{2,1,0:T(8,128)S(1)} collective-permute-done((f32[2,24,256]{2,1,0:T(8,128)S(1)}, f32[2,24,256]{2,1,0:T(8,128)S(1)}, u32[]{:S(2)}, u32[]{:S(2)}) %collective-permute-start.3) | collective-permute-done | bytes 49184 | tf_op jit(solution)/shard_map/ppermute | solution.py:369
  9.6 1.7 %collective-permute-done.2.refs_2_ = f32[2,24,256]{2,1,0:T(8,128)S(1)} collective-permute-done((f32[2,24,256]{2,1,0:T(8,128)S(1)}, f32[2,24,256]{2,1,0:T(8,128)S(1)}, u32[]{:S(2)}, u32[]{:S(2)}) %collective-permute-start.2) | collective-permute-done | bytes 49184 | tf_op jit(solution)/shard_map/ppermute | solution.py:369
  11.4 0.5 %collective-permute-done.1.refs_1_ = f32[2,24,256]{2,1,0:T(8,128)S(1)} collective-permute-done((f32[2,24,256]{2,1,0:T(8,128)S(1)}, f32[2,24,256]{2,1,0:T(8,128)S(1)}, u32[]{:S(2)}, u32[]{:S(2)}) %collective-permute-start.1) | collective-permute-done | bytes 49184 | tf_op jit(solution)/shard_map/ppermute | solution.py:369
  11.9 0.5 %group_maps.1.refs_0_ = f32[2,24,256]{2,1,0:T(8,128)S(1)} custom-call(f32[2,24,256]{2,1,0:T(8,128)S(1)} %get-tuple-element.21.refs_0_, f32[2,24,256]{2,1,0:T(8,128)S(1)} %collective-permute-done.1.refs_1_, f32[2,24,256]{2,1,0:T(8,128)S(1)} %collective-permute-done.2.refs_2_, f32[2,24,256]{2,1,0:T(8,128)S(1)} %collective-permute-done.3.refs_3_), custom_call_target="tpu_custom_call" | custom-call | flops 1000000 | bytes 500000 | tf_op jit(solution)/shard_map/group_maps/pallas_call | solution.py:387
  12.4 3.6 %collective-permute-start.6 = (f32[2,24,256]{2,1,0:T(8,128)S(1)}, f32[2,24,256]{2,1,0:T(8,128)S(1)}, u32[]{:S(2)}, u32[]{:S(2)}) collective-permute-start(f32[2,24,256]{2,1,0:T(8,128)S(1)} %group_maps.1.refs_0_), channel_id=1, source_target_pairs={{0,24},{1,25},{2,26},{3,27},{4,28},{5,29},{6,30},{7,31},{8,16},{9,... | collective-permute-start | bytes 147464 | tf_op jit(solution)/shard_map/ppermute | solution.py:369
  16.0 0.0 collective-permute-start.5
  16.0 0.8 %collective-permute-start.4 = (f32[2,24,256]{2,1,0:T(8,128)S(1)}, f32[2,24,256]{2,1,0:T(8,128)S(1)}, u32[]{:S(2)}, u32[]{:S(2)}) collective-permute-start(f32[2,24,256]{2,1,0:T(8,128)S(1)} %group_maps.1.refs_0_), channel_id=1, source_target_pairs={{0,8},{1,9},{2,10},{3,11},{4,12},{5,13},{6,14},{7,15},{8,0},{9,1},... | collective-permute-start | bytes 147464 | tf_op jit(solution)/shard_map/ppermute | solution.py:369
  16.8 0.0 copy-done
  16.8 0.0 copy-done.3
  16.8 4.1 %local_solve.1 = (f32[2,2,64,128]{3,2,1,0:T(8,128)S(1)}, f32[2,8,256]{2,1,0:T(8,128)S(1)}, bf16[2,256,256]{2,1,0:T(8,128)(2,1)S(1)}, f32[2,2,64,128]{3,2,1,0:T(8,128)}) custom-call(f32[2,24,256]{2,1,0:T(8,128)S(1)} %get-tuple-element.21.refs_0_, f32[2,24,256]{2,1,0:T(8,128)S(1)} %collective-permute-done.1.refs_1_, ...), custom_call_target="tpu_custom_call" | custom-call | flops 1000000 | bytes 500000 | tf_op jit(solution)/shard_map/local_solve/pallas_call | solution.py:387
  20.9 0.0 collective-permute-done.6.refs_3_
  20.9 0.1 collective-permute-done.5.refs_2_
  21.0 0.0 collective-permute-done.4.refs_1_
  (3 shorter events, 0.0 us)
Async XLA Ops:
  0.0 2.8 %copy-start.1 = (bf16[2,2,64,128]{3,2,1,0:T(8,128)(2,1)S(1)}, bf16[2,2,64,128]{3,2,1,0:T(8,128)(2,1)}, u32[]{:S(2)}) copy-start(bf16[2,2,64,128]{3,2,1,0:T(8,128)(2,1)} %u_ref.1) | copy-start | bytes 196612
  0.0 2.8 %copy-start.2 = (bf16[2,2,64,128]{3,2,1,0:T(8,128)(2,1)S(1)}, bf16[2,2,64,128]{3,2,1,0:T(8,128)(2,1)}, u32[]{:S(2)}) copy-start(bf16[2,2,64,128]{3,2,1,0:T(8,128)(2,1)} %rhs_ref.1) | copy-start | bytes 196612
  0.0 2.8 %collective-permute-start = (bf16[2,2,64,128]{3,2,1,0:T(8,128)(2,1)}, bf16[2,2,64,128]{3,2,1,0:T(8,128)(2,1)S(1)}, u32[]{:S(2)}, u32[]{:S(2)}) collective-permute-start(bf16[2,2,64,128]{3,2,1,0:T(8,128)(2,1)} %u_ref.1), channel_id=1, source_target_pairs={{0,1},{1,0},{2,3},{3,2},{4,5},{5,4},{6,7},{7,6},{8,9},{9,8},{10,11... | collective-permute-start | bytes 196616 | tf_op jit(solution)/shard_map/ppermute | solution.py:369
  2.8 13.9 %copy-start = (f32[8,64,64]{2,1,0:T(8,128)S(1)}, f32[8,64,64]{2,1,0:T(8,128)}, u32[]{:S(2)}) copy-start(f32[8,64,64]{2,1,0:T(8,128)} %refs_9_.1) | copy-start | bytes 393220
  3.8 5.9 %collective-permute-start.3 = (f32[2,24,256]{2,1,0:T(8,128)S(1)}, f32[2,24,256]{2,1,0:T(8,128)S(1)}, u32[]{:S(2)}, u32[]{:S(2)}) collective-permute-start(f32[2,24,256]{2,1,0:T(8,128)S(1)} %get-tuple-element.21.refs_0_), channel_id=1, source_target_pairs={{0,6},{1,7},{2,4},{3,5},{4,2},{5,3},{6,0},{7,1},{8,14},{9,15},{10,... | collective-permute-start | bytes 147464 | tf_op jit(solution)/shard_map/ppermute | solution.py:369
  7.3 4.1 %collective-permute-start.2 = (f32[2,24,256]{2,1,0:T(8,128)S(1)}, f32[2,24,256]{2,1,0:T(8,128)S(1)}, u32[]{:S(2)}, u32[]{:S(2)}) collective-permute-start(f32[2,24,256]{2,1,0:T(8,128)S(1)} %get-tuple-element.21.refs_0_), channel_id=1, source_target_pairs={{0,4},{1,5},{2,6},{3,7},{4,0},{5,1},{6,2},{7,3},{8,12},{9,13},{10,... | collective-permute-start | bytes 147464 | tf_op jit(solution)/shard_map/ppermute | solution.py:369
  7.8 4.1 %collective-permute-start.1 = (f32[2,24,256]{2,1,0:T(8,128)S(1)}, f32[2,24,256]{2,1,0:T(8,128)S(1)}, u32[]{:S(2)}, u32[]{:S(2)}) collective-permute-start(f32[2,24,256]{2,1,0:T(8,128)S(1)} %get-tuple-element.21.refs_0_), channel_id=1, source_target_pairs={{0,2},{1,3},{2,0},{3,1},{4,6},{5,7},{6,4},{7,5},{8,10},{9,11},{10,... | collective-permute-start | bytes 147464 | tf_op jit(solution)/shard_map/ppermute | solution.py:369
  11.9 4.9 %copy-start.3 = (f32[2,16,128]{2,1,0:T(8,128)S(1)}, f32[2,16,128]{2,1,0:T(8,128)}, u32[]{:S(2)}) copy-start(f32[2,16,128]{2,1,0:T(8,128)} %refs_10_.1) | copy-start | bytes 49156
  12.4 8.5 %collective-permute-start.6 = (f32[2,24,256]{2,1,0:T(8,128)S(1)}, f32[2,24,256]{2,1,0:T(8,128)S(1)}, u32[]{:S(2)}, u32[]{:S(2)}) collective-permute-start(f32[2,24,256]{2,1,0:T(8,128)S(1)} %group_maps.1.refs_0_), channel_id=1, source_target_pairs={{0,24},{1,25},{2,26},{3,27},{4,28},{5,29},{6,30},{7,31},{8,16},{9,... | collective-permute-start | bytes 147464 | tf_op jit(solution)/shard_map/ppermute | solution.py:369
  16.0 5.0 %collective-permute-start.5 = (f32[2,24,256]{2,1,0:T(8,128)S(1)}, f32[2,24,256]{2,1,0:T(8,128)S(1)}, u32[]{:S(2)}, u32[]{:S(2)}) collective-permute-start(f32[2,24,256]{2,1,0:T(8,128)S(1)} %group_maps.1.refs_0_), channel_id=1, source_target_pairs={{0,16},{1,17},{2,18},{3,19},{4,20},{5,21},{6,22},{7,23},{8,24},{9,... | collective-permute-start | bytes 147464 | tf_op jit(solution)/shard_map/ppermute | solution.py:369
  16.0 5.0 %collective-permute-start.4 = (f32[2,24,256]{2,1,0:T(8,128)S(1)}, f32[2,24,256]{2,1,0:T(8,128)S(1)}, u32[]{:S(2)}, u32[]{:S(2)}) collective-permute-start(f32[2,24,256]{2,1,0:T(8,128)S(1)} %group_maps.1.refs_0_), channel_id=1, source_target_pairs={{0,8},{1,9},{2,10},{3,11},{4,12},{5,13},{6,14},{7,15},{8,0},{9,1},... | collective-permute-start | bytes 147464 | tf_op jit(solution)/shard_map/ppermute | solution.py:369

commit v4 on v3

--- a/solution.py
+++ b/solution.py
@@ -72,9 +72,15 @@
     return dot_rows(gather, spread)
 
 
-def class_products(inv_rows, weights):
-    count = inv_rows.shape[0]
-    high, low = split(inv_rows)
+def face_columns(inv_rows, nodes):
+    at = iota((nodes, 5 * FACE), 1)
+    wanted = jnp.where(at < 64, wanted_node(at // FACE, at % FACE), at - 64)
+    chosen = (iota((nodes, 5 * FACE), 0) == wanted).astype(BF16)
+    return dot(jnp.concatenate(split(inv_rows), axis=0), chosen).astype(BF16)
+
+
+def class_products(high, low, weights):
+    count = high.shape[0]
     parts = dot(jnp.concatenate([high, low], axis=0), weights)
     return -(parts[:count, :128] + parts[:count, 128:] + parts[count:, :128])
 
@@ -96,64 +102,53 @@
     return jnp.where(lane < 32, high.astype(F32), jnp.where(lane < 48, low.astype(F32), 0.0)).astype(BF16)
 
 
-def params_kernel(inv_hbm, x_hbm, lat_hbm, cls_hbm, flag_hbm, weight_ref, out_ref, step_ref, lin_ref, label_ref,
-                  inv_ref, x_ref, lat_ref, cls_ref, flag_ref, sems):
-    pairs = ((lat_hbm, lat_ref), (x_hbm, x_ref), (inv_hbm, inv_ref), (cls_hbm, cls_ref), (flag_hbm, flag_ref))
+def params_kernel(cls_hbm, flag_hbm, x_hbm, lat_hbm, inv_hbm, weight_ref, out_ref, step_ref, label_ref,
+                  cls_ref, flag_ref, x_ref, lat_ref, inv_ref, sems):
+    pairs = ((cls_hbm, cls_ref), (flag_hbm, flag_ref), (x_hbm, x_ref), (lat_hbm, lat_ref), (inv_hbm, inv_ref))
     copies = [pltpu.make_async_copy(a, b, sems.at[i]) for i, (a, b) in enumerate(pairs)]
     for copy in copies:
         copy.start()
     count, nodes, _ = inv_ref.shape
-    planes, rows_y, _ = cls_ref.shape
+    planes = cls_ref.shape[0]
     item, lane = iota((FACE, 128), 0), iota((FACE, 128), 1)
     places = [(lane == 64 + FACE * f + item).astype(BF16) for f in range(4)]
     places.append(((lane < 48) & (lane % FACE == item)).astype(BF16))
-    at = iota((nodes, 5 * FACE), 1)
-    wanted = jnp.where(at < 64, wanted_node(at // FACE, at % FACE), at - 64)
-    chosen = (iota((nodes, 5 * FACE), 0) == wanted).astype(BF16)
-    for copy in copies:
+    for copy in copies[:2]:
+        copy.wait()
+    labels = [cls_ref[x] for x in range(planes)]
+    labels += [flag_ref[d, x] for d in range(2) for x in range(planes)]
+    labels = jnp.concatenate(labels, axis=0).astype(F32).astype(BF16)
+    tile = (iota((FACE, 128), 1) % FACE == iota((FACE, 128), 0)).astype(BF16)
+    label_ref[...] = dot(labels, tile)
+    for copy in copies[2:]:
         copy.wait()
     placed = []
     for f in range(5):
         rows = (lat_ref[f] if f < 4 else x_ref[...]).reshape(count * FACE, FACE)
         placed.append(dot(jnp.concatenate(split(rows), axis=0), places[f]).astype(BF16))
-    columns = []
+    inv_rows = [inv_ref[k, nodes - FACE:, :] for k in range(count)]
+    gathered = face_columns(jnp.concatenate(inv_rows, axis=0), nodes)
+    outs, steps = [], []
     for k in range(count):
+        columns = []
         for part in range(2):
             begin = part * count * FACE + k * FACE
             columns.append(jnp.concatenate([p[begin:begin + FACE] for p in placed], axis=0))
-    weights = dot(chosen, jnp.concatenate(columns, axis=1)).astype(BF16)
-    weight_ref[...] = weights
-    outs, steps = [], []
-    for k in range(count):
-        inv_rows = inv_ref[k, nodes - FACE:, :]
-        products = class_products(inv_rows, weights[:, 256 * k:256 * k + 256])
-        outs.append(with_inverse(inv_rows, products))
+        weights = jnp.concatenate(columns, axis=1)
+        weight_ref[:, 256 * k:256 * k + 256] = weights
+        low = (count + k) * FACE
+        products = class_products(gathered[k * FACE:k * FACE + FACE], gathered[low:low + FACE], weights)
+        outs.append(with_inverse(inv_rows[k], products))
         steps.append(products)
     out_ref[...] = in_parts(jnp.concatenate(outs, axis=0))
-    step = coupling_parts(jnp.concatenate(steps, axis=0))
-    step_ref[...] = step
-    flip_row, flip_lane = iota((2 * FACE, 128), 0), iota((2 * FACE, 128), 1)
-    flip = (flip_lane == flip_row + FACE * (flip_row >= FACE)).astype(BF16)
-    turned = dot_rows(flip, step).astype(BF16)
-    labels = [cls_ref[x] for x in range(planes)]
-    labels += [flag_ref[d, x] for d in range(2) for x in range(planes)]
-    labels = jnp.concatenate(labels, axis=0).astype(F32).astype(BF16)
-    tile = (iota((FACE, 128), 1) % FACE == iota((FACE, 128), 0)).astype(BF16)
-    label_ref[...] = dot(labels, tile)
+    step_ref[...] = coupling_parts(jnp.concatenate(steps, axis=0))
+
+
+def picked(label, count):
     wide = (iota((FACE, 256), 1) // FACE == iota((FACE, 256), 0)).astype(BF16)
-    on_wide = dot(labels, wide).astype(jnp.int32)
-    pick_row, pick_lane = iota((128, 256), 0), iota((128, 256), 1)
-    same = pick_row % FACE == pick_lane % FACE
-    for y in range(rows_y):
-        whole = None
-        for x in range(planes):
-            here = on_wide[x * rows_y + y:x * rows_y + y + 1]
-            pick = jnp.where(same & (pick_row // FACE == here), 1.0, 0.0).astype(BF16)
-            both = dot(turned, pick)
-            linear = both[:FACE] + both[FACE:]
-            lin_ref[x, y] = linear
-            whole = linear if whole is None else applied(whole, linear)
-        lin_ref[planes, y] = whole
+    on_wide = dot(label[:, :FACE].astype(BF16), wide).astype(jnp.int32)
+    row, lane = iota((count * FACE, 256), 0), iota((count * FACE, 256), 1)
+    return jnp.where((row % FACE == lane % FACE) & (row // FACE == on_wide), 1.0, 0.0).astype(BF16)
 
 
 def class_sum(every, label, rows):
@@ -170,14 +165,22 @@
     return jnp.concatenate([first, second, first, rest], axis=0)
 
 
-def sources_kernel(gy_size, u_ref, rhs_ref, below_ref, above_ref, label_ref, out_ref, step_ref, lin_ref, x_ref, flow_ref, map_ref):
+def sources_kernel(gy_size, u_ref, rhs_ref, below_ref, above_ref, label_ref, out_ref, step_ref, x_ref, flow_ref, lin_ref, map_ref):
     planes, rows_y, nodes, columns = u_ref.shape
     place = lax.axis_index("gy")
     node, item = iota((nodes, nodes), 1), iota((nodes, nodes), 0)
     chosen = (node == wanted_node(item // FACE, item % FACE)).astype(BF16)
     own = [u_ref[x, y] for x in range(planes) for y in range(rows_y)]
     other = [below_ref[x, below_ref.shape[1] - 1] for x in range(planes)] + [above_ref[x, 0] for x in range(planes)]
+    step = step_ref[...]
+    row, lane = iota((2 * FACE, 128), 0), iota((2 * FACE, 128), 1)
+    flip = (lane == row + FACE * (row >= FACE)).astype(BF16)
+    turned = dot_rows(flip, step).astype(BF16)
     faces = dot(chosen, jnp.concatenate(own + other, axis=1))
+    picks = []
+    for at in range(planes * rows_y):
+        picks.append(picked(label_ref[pl.ds(at, 1), :], step.shape[0] // FACE))
+    linear = dot(turned, jnp.concatenate(picks, axis=1))
     faces = [faces[:, i * columns:(i + 1) * columns] for i in range(len(own) + len(other))]
     z_at = iota((FACE, columns), 1) % FACE
     has_below = jnp.where(place > 0, 1.0, 0.0)
@@ -208,6 +211,22 @@
             data.append(here)
     data = jnp.concatenate(data, axis=1)
     every = dot(out_ref[...], jnp.concatenate([data, data], axis=0))
+    keep = (iota((256, 256), 0) // FACE == iota((256, 256), 1) // FACE).astype(BF16)
+    wholes = []
+    for at in range(planes * rows_y):
+        here = linear[:, at * 256:at * 256 + 256]
+        lin_ref[at // rows_y, at % rows_y] = here[:FACE] + here[FACE:]
+        both = here.astype(BF16)
+        if at < rows_y:
+            wholes.append((here[:FACE] + here[FACE:], both))
+        else:
+            pair = wholes[at % rows_y][1]
+            first, second = [jnp.concatenate([part] * 16, axis=0) * keep for part in (both[:FACE], both[FACE:])]
+            parts = dot(pair, first)
+            whole = parts[:FACE] + parts[FACE:] + dot(pair[:FACE], second)
+            if at < (planes - 1) * rows_y:
+                both = jnp.concatenate(split(whole), axis=0)
+            wholes[at % rows_y] = (whole, both)
     total = None
     for x in range(planes):
         begin = x * rows_y * columns
@@ -218,7 +237,7 @@
             flow = flow + class_sum(dot(step_ref[...], stacked(total)), label, FACE)
         total = flow
     for y in range(rows_y):
-        map_ref[y, 0:FACE] = lin_ref[planes, y]
+        map_ref[y, 0:FACE] = wholes[y][0]
         map_ref[y, FACE:] = encode(total[:, y * columns:(y + 1) * columns])
 
 
@@ -227,24 +246,48 @@
     return [jnp.concatenate([part] * 16, axis=0) * keep for part in split(linear)]
 
 
-def join_blocks(earlier, later):
-    high, low = split(jnp.concatenate([earlier, jnp.zeros((8, 256), F32)], axis=0))
-    first, second = block_diagonal(later[:FACE])
-    parts = dot(jnp.concatenate([high, low], axis=0), first)
-    total = (parts[:32] + parts[32:] + dot(high, second))[:24]
-    return jnp.concatenate([total[:FACE], total[FACE:] + later[FACE:]], axis=0)
-
-
-def group_kernel(size, power, *refs):
-    blocks, total_ref, held = refs[:size], refs[size], refs[size + 1]
-    for s in range(size):
-        held[s] = blocks[s][...]
-    mine = lax.axis_index("gx") % size
-    for y in range(total_ref.shape[0]):
-        maps = [held[(mine ^ j) if power else (mine - j + size) % size, y] for j in range(size)]
-        while len(maps) > 1:
-            maps = [join_blocks(maps[i], maps[i + 1]) if i + 1 < len(maps) else maps[i] for i in range(0, len(maps), 2)]
-        total_ref[y] = maps[0]
+def join_many(pairs):
+    ready = []
+    for earlier, later in pairs:
+        halves = split(jnp.concatenate([earlier, jnp.zeros((8, 256), F32)], axis=0))
+        ready.append((halves[0], jnp.concatenate(halves, axis=0), block_diagonal(later[:FACE])))
+    firsts = [dot(both, blocks[0]) for _, both, blocks in ready]
+    seconds = [dot(high, blocks[1]) for high, _, blocks in ready]
+    joined = []
+    for parts, more, (_, later) in zip(firsts, seconds, pairs):
+        total = (parts[:32] + parts[32:] + more)[:24]
+        joined.append(jnp.concatenate([total[:FACE], total[FACE:] + later[FACE:]], axis=0))
+    return joined
+
+
+def block_slot(mine, other, size, power):
+    step = (mine ^ other) if power else (mine - other + size) % size
+    return (size - step) % size
+
+
+def group_kernel(size, power, outer, *refs):
+    blocks, total_ref, held = refs[:size], refs[size + 1], refs[size + 2]
+    place = lax.axis_index("gx")
+    mine = place % size
+    rows_y = total_ref.shape[0]
+
+    @pl.when(place // size < outer - 1)
+    def _():
+        for s in range(size):
+            held[s] = blocks[s][...]
+        slots = [block_slot(mine, j, size, power) for j in range(size)]
+        maps = [[held[slot, y] for slot in slots] for y in range(rows_y)]
+        while len(maps[0]) > 1:
+            length = len(maps[0])
+            joined = join_many([(maps[y][i], maps[y][i + 1]) for y in range(rows_y) for i in range(0, length - 1, 2)])
+            half = length // 2
+            maps = [joined[y * half:y * half + half] + maps[y][2 * half:] for y in range(rows_y)]
+        for y in range(rows_y):
+            total_ref[y] = maps[y][0]
+
+    @pl.when(place // size == outer - 1)
+    def _():
+        total_ref[...] = jnp.zeros(total_ref.shape, F32)
 
 
 def carried(parts, traces, count):
@@ -254,13 +297,10 @@
     rest = jnp.zeros((8, first.shape[1]), BF16)
     rows = dot(spread, jnp.concatenate([first, rest, second, rest], axis=0))
     keep = iota((256, 256), 0) % FACE == iota((256, 256), 1) // FACE
-    sums = []
-    for y, part in enumerate(parts):
-        here = jnp.where(keep, rows[:, y * 256:y * 256 + 256], 0.0).astype(BF16)
-        high = part[:count]
-        by_first = dot_rows(part, here[:128])
-        sums.append(by_first[:count] + by_first[count:] + dot_rows(high, here[128:]))
-    return sums
+    here = [jnp.where(keep, rows[:, y * 256:y * 256 + 256], 0.0).astype(BF16) for y in range(len(parts))]
+    by_first = [dot_rows(part, data[:128]) for part, data in zip(parts, here)]
+    by_second = [dot_rows(part[:count], data[128:]) for part, data in zip(parts, here)]
+    return [first[:count] + first[count:] + second for first, second in zip(by_first, by_second)]
 
 
 def write_nodes(result_ref, out_ref, sems, base_ref, part_ref, traces):
@@ -276,56 +316,65 @@
         copy.wait()
 
 
-def solve_kernel(size, power, *refs):
-    blocks = refs[:size]
-    data_ref, label_ref, weight_ref, lin_ref, flow_ref, inv_ref, inflow_ref = refs[size:size + 7]
-    base_ref, start_ref, part_ref, out_ref, held, full_ref, result_ref, sems = refs[size + 7:]
+def local_kernel(data_ref, label_ref, weight_ref, flow_ref, inv_ref, inflow_ref, base_ref, start_ref, chosen_ref, offset_ref, full_ref):
     planes, rows_y, nodes, columns = base_ref.shape
     coupling = jnp.zeros((nodes, 128), F32)
-    for k in range(inv_ref.shape[0]):
+    count = inv_ref.shape[0]
+    gathered = face_columns(inv_ref[...].reshape(count * nodes, nodes), nodes)
+    for k in range(count):
         inv_rows = inv_ref[k]
-        products = class_products(inv_rows, weight_ref[:, 256 * k:256 * k + 256])
+        low = (count + k) * nodes
+        products = class_products(
+            gathered[k * nodes:k * nodes + nodes], gathered[low:low + nodes], weight_ref[:, 256 * k:256 * k + 256]
+        )
         here = pl.ds(k * nodes, nodes)
         shifted = pltpu.roll(products, FACE * k, 1) if k else products
         coupling = jnp.where(iota((nodes, 128), 1) // FACE == k, shifted, coupling)
         full_ref[here, :] = in_parts(with_inverse(inv_rows, products))
     coupling = jnp.concatenate(split(coupling), axis=0)
+    for y in range(rows_y):
+        start_ref[y] = encode(inflow_ref[y])
+    for x in range(planes):
+        for y in range(rows_y):
+            label = label_ref[pl.ds(x * rows_y + y, 1), :]
+            data = data_ref[x, y]
+            every = dot(full_ref[...], jnp.concatenate([data, data], axis=0))
+            base_ref[x, y] = class_sum(every, label, nodes)
+            chosen_ref[x, y] = dot(coupling, picked(label, count)).astype(BF16)
+            if x < planes - 1:
+                offset_ref[x, y] = encode(flow_ref[x, :, y * columns:(y + 1) * columns])
+
+
+def carry_kernel(size, power, *refs):
+    blocks = refs[:size]
+    local_ref, start_ref, chosen_ref, offset_ref, lin_ref = refs[size:size + 5]
+    base_ref, part_ref, out_ref, held, result_ref, sems = refs[size + 5:]
+    planes, rows_y, nodes, _ = base_ref.shape
     for s in range(size):
         held[s] = blocks[s][...]
     place = lax.axis_index("gx")
     mine = place % size
     same = (iota((24, 256), 1) % FACE == iota((24, 256), 0)).astype(F32)
-    wide = (iota((FACE, 256), 1) // FACE == iota((FACE, 256), 0)).astype(BF16)
-    row, lane = iota((128, 256), 0), iota((128, 256), 1)
-    starts = []
-    for y in range(rows_y):
-        start = encode(inflow_ref[y])
-        start_ref[y] = start
-        starts.append(start)
-        before = same
-        for j in range(size - 1):
-            block = held[(mine ^ j) if power else (mine - j + size) % size, y]
-            before = jnp.where(mine > j, block if j == 0 else join_blocks(before, block), before)
-        for x in range(planes):
-            at = x * rows_y + y
-            label = label_ref[pl.ds(at, 1), :]
-            data = data_ref[x, y]
-            every = dot(full_ref[...], jnp.concatenate([data, data], axis=0))
-            local = class_sum(every, label, nodes)
-            on_wide = dot(label[:, :FACE].astype(BF16), wide).astype(jnp.int32)
-            pick = jnp.where((row % FACE == lane % FACE) & (row // FACE == on_wide), 1.0, 0.0).astype(BF16)
-            chosen = dot(coupling, pick).astype(BF16)
-            local = local + carried([chosen], [before[FACE:]], nodes)[0]
-            base_ref[x, y] = local
-            first, second = block_diagonal(before[:FACE])
-            products = dot_rows(chosen, first)
-            products = products[:nodes] + products[nodes:] + dot_rows(chosen[:nodes], second)
-            high, low = split(products)
+    ahead = [same] * rows_y
+    for j in range(size - 1):
+        slot = block_slot(mine, j, size, power)
+        block = [held[slot, y] for y in range(rows_y)]
+        joined = block if j == 0 else join_many([(ahead[y], block[y]) for y in range(rows_y)])
+        ahead = [jnp.where(mine > j, joined[y], ahead[y]) for y in range(rows_y)]
+    for x in range(planes):
+        chosen = [chosen_ref[x, y] for y in range(rows_y)]
+        sums = carried(chosen, [ahead[y][FACE:] for y in range(rows_y)], nodes)
+        pairs = [block_diagonal(ahead[y][:FACE]) for y in range(rows_y)]
+        firsts = [dot_rows(chosen[y], pairs[y][0]) for y in range(rows_y)]
+        seconds = [dot_rows(chosen[y][:nodes], pairs[y][1]) for y in range(rows_y)]
+        for y in range(rows_y):
+            base_ref[x, y] = local_ref[x, y] + sums[y]
+            high, low = split(firsts[y][:nodes] + firsts[y][nodes:] + seconds[y])
             part_ref[y, pl.ds(x * nodes, nodes), :] = high
             part_ref[y, pl.ds((planes + x) * nodes, nodes), :] = low
-            if x < planes - 1:
-                offset = encode(flow_ref[x, :, y * columns:(y + 1) * columns])
-                before = join_blocks(before, jnp.concatenate([lin_ref[x, y], offset], axis=0))
+        if x < planes - 1:
+            own = [jnp.concatenate([lin_ref[x, y], offset_ref[x, y]], axis=0) for y in range(rows_y)]
+            ahead = join_many([(ahead[y], own[y]) for y in range(rows_y)])
 
     @pl.when(place < size)
     def _():
@@ -341,12 +390,9 @@
         for place in range(1, size):
             @pl.when(mine == place)
             def _():
-                traces = []
-                for y in range(rows_y):
-                    trace = start_ref[y]
-                    for j in range(place):
-                        trace = advance(trace, blocks[place ^ j][y])
-                    traces.append(trace)
+                traces = [start_ref[y] for y in range(rows_y)]
+                for j in range(place):
+                    traces = [advance(traces[y], blocks[block_slot(place, j, size, power)][y]) for y in range(rows_y)]
                 write_nodes(result_ref, out_ref, sems, base_ref, part_ref, traces)
     else:
         held = refs[size + 7]
@@ -359,7 +405,7 @@
             for y in range(rows_y):
                 trace = start_ref[y]
                 for j in range(size - 1):
-                    slot = (mine ^ j) if power else (mine - j + size) % size
+                    slot = block_slot(mine, j, size, power)
                     trace = jnp.where(mine > j, advance(trace, held[slot, y]), trace)
                 traces.append(trace)
             write_nodes(result_ref, out_ref, sems, base_ref, part_ref, traces)
@@ -410,74 +456,85 @@
     else:
         below = moved(u_old[:, rows_y - 1:], [(at(x, y), at(x, y + 1)) for x, y in everyone if y + 1 < gy_size])
         above = moved(u_old[:, :1], [(at(x, y), at(x, y - 1)) for x, y in everyone if y > 0])
-    weights, out_rows, step, linear, labels = call(
+    weights, out_rows, step, labels = call(
         params_kernel,
         (
-            shape((nodes, count * 256), BF16),
+            shape((5 * FACE, count * 256), BF16),
             shape((count * FACE, 256), BF16),
             shape((count * FACE, 128), BF16),
-            shape((planes + 1, rows_y, FACE, 256)),
             shape((3 * planes * rows_y, columns)),
         ),
         "class_matrices",
         tuple(
             pltpu.with_memory_space_constraint(value, pltpu.HBM)
-            for value in (inverse, x_face, lateral_faces, classes, flags)
+            for value in (classes, flags, x_face, lateral_faces, inverse)
         ),
         [
-            pltpu.VMEM(inverse.shape, F32),
+            pltpu.VMEM(classes.shape, jnp.int32),
+            pltpu.VMEM(flags.shape, jnp.int32),
             pltpu.VMEM(x_face.shape, F32),
             pltpu.VMEM(lateral_faces.shape, F32),
-            pltpu.VMEM(classes.shape, jnp.int32),
-            pltpu.VMEM(flags.shape, jnp.int32),
+            pltpu.VMEM(inverse.shape, F32),
             pltpu.SemaphoreType.DMA((5,)),
         ],
         space=pltpu.HBM,
     )
-    data, flow, here = call(
+    data, flow, linear, here = call(
         functools.partial(sources_kernel, gy_size),
         (
             shape((planes, rows_y, 128, columns), BF16),
             shape((planes, FACE, rows_y * columns)),
+            shape((planes, rows_y, FACE, 256)),
             shape((rows_y, 24, 256)),
         ),
         "sources",
-        (u_old, rhs, below, above, labels, out_rows, step, linear),
+        (u_old, rhs, below, above, labels, out_rows, step),
     )
     inner = 4 if gx_size % 4 == 0 else 1
     outer = gx_size // inner
     power = outer & (outer - 1) == 0
     near = [here]
-    for s in range(1, inner):
+    for s in range(inner - 1, 0, -1):
         near.append(moved(here, [(at(x, y), at(x ^ s, y)) for x, y in everyone]))
+    nodes_shape = (planes, rows_y, nodes, columns)
+    writing = [pltpu.VMEM(nodes_shape, F32), pltpu.SemaphoreType.DMA((planes, rows_y))]
+    local, start, chosen, offsets = call(
+        local_kernel,
+        (
+            shape(nodes_shape),
+            shape((rows_y, 8, 256)),
+            shape((planes, rows_y, 2 * nodes, 256), BF16),
+            shape((max(planes - 1, 1), rows_y, 8, 256)),
+        ),
+        "local_solve",
+        (data, labels, weights, flow, inverse, inflow),
+        [pltpu.VMEM((count * nodes, 256), BF16)],
+    )
     total = call(
-        functools.partial(group_kernel, inner, True),
+        functools.partial(group_kernel, inner, True, outer),
         shape((rows_y, 24, 256)),
         "group_maps",
-        tuple(near),
+        tuple(near) + (start,),
         [pltpu.VMEM((inner, rows_y, 24, 256), F32)],
     )
     blocks = [total]
-    for s in range(1, outer):
+    for s in range(outer - 1, 0, -1):
         if power:
             pairs = [(at(x, y), at(x ^ (s * inner), y)) for x, y in everyone]
         else:
             pairs = [(at(x, y), at((x + s * inner) % gx_size, y)) for x, y in everyone]
         blocks.append(moved(total, pairs))
-    nodes_shape = (planes, rows_y, nodes, columns)
-    writing = [pltpu.VMEM(nodes_shape, F32), pltpu.SemaphoreType.DMA((planes, rows_y))]
-    base, start, parts, out = call(
-        functools.partial(solve_kernel, inner, True),
+    base, parts, out = call(
+        functools.partial(carry_kernel, inner, True),
         (
             shape(nodes_shape),
-            shape((rows_y, 8, 256)),
             shape((rows_y, 2 * planes * nodes, 256), BF16),
             pltpu.HBM(nodes_shape, F32),
         ),
-        "local_solve",
-        tuple(near) + (data, labels, weights, linear, flow, inverse, inflow),
-        [pltpu.VMEM((inner, rows_y, 24, 256), F32), pltpu.VMEM((count * nodes, 256), BF16)] + writing,
-        out_spaces=(pltpu.VMEM, pltpu.VMEM, pltpu.VMEM, pltpu.HBM),
+        "carry_maps",
+        tuple(near) + (local, start, chosen, offsets, linear),
+        [pltpu.VMEM((inner, rows_y, 24, 256), F32)] + writing,
+        out_spaces=(pltpu.VMEM, pltpu.VMEM, pltpu.HBM),
     )
     held = [] if power and outer <= 4 else [pltpu.VMEM((outer, rows_y, 24, 256), F32)]
     args = tuple(blocks) + (start, base, parts, out)

time: 21.2 us -> 19.9 us (0.939)
  waiting for transfers between devices: 4.1 us -> 3.31 us
  Pallas kernels: 7.88 us -> 7.34 us
    ppermute x7, waiting for transfers between devices: 4.1 us -> 3.31 us  [moved(): return lax.ppermute(value, ('gx', 'gy'), pairs)]
    pallas_call x5 -> x6, Pallas kernels: 7.88 us -> 7.34 us  [call(): pl.pallas_call(kernel, out_shape=outs, in_specs=in_specs, out_specs=out_s...]
  transfers between devices with their start and end apart: 7 -> 7, of which waited for: 4 -> 3; matrix products, arithmetic and copies ran while one was open for 0% -> 0% of each run, Pallas kernels for 31% -> 30%
where the time goes in v4:
time: 19.9 us; the launch traced here: 19.7 us
  starting transfers between devices  8.98 us (45%)
  Pallas kernels  7.34 us (37%)
  waiting for transfers between devices  3.31 us (17%)
    ppermute x7, starting transfers between devices, moved(): return lax.ppermute(value, ('gx', 'gy'), pairs)  8.98 us
    pallas_call x6, Pallas kernels, call(): pl.pallas_call(kernel, out_shape=outs, in_specs=in_specs, out_specs=out_s...  7.34 us
    ppermute x7, waiting for transfers between devices, moved(): return lax.ppermute(value, ('gx', 'gy'), pairs)  3.31 us
  transfers between devices with their start and end apart: 7, of which 3 were waited for; matrix products, arithmetic and copies ran while one was open for 0% of the time, Pallas kernels for 30%

profile of v4, /device:TPU:0, one launch (start us, length us, event | category | flops | bytes accessed | tf_op | source)
XLA Modules:
  0.0 19.7 jit_solution(10269714242432795465)
XLA Ops:
  0.0 0.5 %collective-permute-start = (bf16[2,2,64,128]{3,2,1,0:T(8,128)(2,1)}, bf16[2,2,64,128]{3,2,1,0:T(8,128)(2,1)S(1)}, u32[]{:S(2)}, u32[]{:S(2)}) collective-permute-start(bf16[2,2,64,128]{3,2,1,0:T(8,128)(2,1)} %u_ref.1), channel_id=1, source_target_pairs={{0,1},{1,0},{2,3},{3,2},{4,5},{5,4},{6,7},{7,6},{8,9},{9,8},{10,11... | collective-permute-start | bytes 196616 | tf_op jit(solution)/shard_map/ppermute | solution.py:415
  0.5 1.5 %class_matrices.1 = (bf16[80,2048]{1,0:T(8,128)(2,1)S(1)}, bf16[128,256]{1,0:T(8,128)(2,1)S(1)}, bf16[128,128]{1,0:T(8,128)(2,1)S(1)}, f32[12,128]{1,0:T(8,128)S(1)}) custom-call(s32[2,2,16]{2,1,0:T(2,128)} %cls_hbm.1, s32[2,2,2,16]{3,2,1,0:T(2,128)} %flag_hbm.1, f32[8,16,16]{2,1,0:T(8,128)} %x_hbm.1, f32[4,8,16,16]{3,2,1,0:T(8,128)} %lat_hbm.1, ...), custom_call_target="tpu_custom_call" | custom-call | flops 1000000 | bytes 500000 | tf_op jit(solution)/shard_map/class_matrices/pallas_call | solution.py:433
  2.0 0.0 copy-start
  2.0 0.0 collective-permute-done.below_ref.above_ref
  2.0 0.0 copy-done.1
  2.0 0.0 copy-done.2
  2.1 0.0 copy-start.3
  2.1 0.9 %sources.1 = (bf16[2,2,128,128]{3,2,1,0:T(8,128)(2,1)S(1)}, f32[2,16,256]{2,1,0:T(8,128)S(1)}, f32[2,2,16,256]{3,2,1,0:T(8,128)S(1)}, f32[2,24,256]{2,1,0:T(8,128)S(1)}) custom-call(bf16[2,2,64,128]{3,2,1,0:T(8,128)(2,1)S(1)} %copy-done.1, bf16[2,2,64,128]{3,2,1,0:T(8,128)(2,1)S(1)} %copy-done.2, ...), custom_call_target="tpu_custom_call" | custom-call | flops 1000000 | bytes 500000 | tf_op jit(solution)/shard_map/sources/pallas_call | solution.py:433
  2.9 3.5 %collective-permute-start.1 = (f32[2,24,256]{2,1,0:T(8,128)S(1)}, f32[2,24,256]{2,1,0:T(8,128)S(1)}, u32[]{:S(2)}, u32[]{:S(2)}) collective-permute-start(f32[2,24,256]{2,1,0:T(8,128)S(1)} %get-tuple-element.23.refs_0_), channel_id=1, source_target_pairs={{0,6},{1,7},{2,4},{3,5},{4,2},{5,3},{6,0},{7,1},{8,14},{9,15},{10,... | collective-permute-start | bytes 147464 | tf_op jit(solution)/shard_map/ppermute | solution.py:415
  6.4 0.5 %collective-permute-start.2 = (f32[2,24,256]{2,1,0:T(8,128)S(1)}, f32[2,24,256]{2,1,0:T(8,128)S(1)}, u32[]{:S(2)}, u32[]{:S(2)}) collective-permute-start(f32[2,24,256]{2,1,0:T(8,128)S(1)} %get-tuple-element.23.refs_0_), channel_id=1, source_target_pairs={{0,4},{1,5},{2,6},{3,7},{4,0},{5,1},{6,2},{7,3},{8,12},{9,13},{10,... | collective-permute-start | bytes 147464 | tf_op jit(solution)/shard_map/ppermute | solution.py:415
  6.9 0.1 collective-permute-start.3
  7.0 0.0 copy-done
  7.0 1.8 %local_solve.1 = (f32[2,2,64,128]{3,2,1,0:T(8,128)S(1)}, f32[2,8,256]{2,1,0:T(8,128)S(1)}, bf16[2,2,128,256]{3,2,1,0:T(8,128)(2,1)S(1)}, f32[1,2,8,256]{3,2,1,0:T(8,128)S(1)}) custom-call(bf16[2,2,128,128]{3,2,1,0:T(8,128)(2,1)S(1)} %get-tuple-element.24.data_ref, f32[12,128]{1,0:T(8,128)S(1)} %get-tuple-element.20.label_ref, ...), custom_call_target="tpu_custom_call" | custom-call | flops 1000000 | bytes 500000 | tf_op jit(solution)/shard_map/local_solve/pallas_call | solution.py:433
  8.8 0.0 collective-permute-done.1.refs_1_
  8.9 1.6 %collective-permute-done.2.refs_2_ = f32[2,24,256]{2,1,0:T(8,128)S(1)} collective-permute-done((f32[2,24,256]{2,1,0:T(8,128)S(1)}, f32[2,24,256]{2,1,0:T(8,128)S(1)}, u32[]{:S(2)}, u32[]{:S(2)}) %collective-permute-start.2) | collective-permute-done | bytes 49184 | tf_op jit(solution)/shard_map/ppermute | solution.py:415
  10.5 0.5 %collective-permute-done.3.refs_3_ = f32[2,24,256]{2,1,0:T(8,128)S(1)} collective-permute-done((f32[2,24,256]{2,1,0:T(8,128)S(1)}, f32[2,24,256]{2,1,0:T(8,128)S(1)}, u32[]{:S(2)}, u32[]{:S(2)}) %collective-permute-start.3) | collective-permute-done | bytes 49184 | tf_op jit(solution)/shard_map/ppermute | solution.py:415
  11.0 0.5 %group_maps.1.refs_0_ = f32[2,24,256]{2,1,0:T(8,128)S(1)} custom-call(f32[2,24,256]{2,1,0:T(8,128)S(1)} %get-tuple-element.23.refs_0_, f32[2,24,256]{2,1,0:T(8,128)S(1)} %collective-permute-done.1.refs_1_, f32[2,24,256]{2,1,0:T(8,128)S(1)} %collective-permute-done.2.refs_2_, f32[2,24,256]{2,1,0:T(8,128)S(1)} %collective-permute-done.3.refs_3_, ...), custom_call_target="tpu_custom_call" | custom-call | flops 1000000 | bytes 500000 | tf_op jit(solution)/shard_map/group_maps/pallas_call | solution.py:433
  11.5 3.1 %collective-permute-start.4 = (f32[2,24,256]{2,1,0:T(8,128)S(1)}, f32[2,24,256]{2,1,0:T(8,128)S(1)}, u32[]{:S(2)}, u32[]{:S(2)}) collective-permute-start(f32[2,24,256]{2,1,0:T(8,128)S(1)} %group_maps.1.refs_0_), channel_id=1, source_target_pairs={{0,24},{1,25},{2,26},{3,27},{4,28},{5,29},{6,30},{7,31},{8,16},{9,... | collective-permute-start | bytes 147464 | tf_op jit(solution)/shard_map/ppermute | solution.py:415
  14.6 0.0 collective-permute-start.5
  14.6 1.3 %collective-permute-start.6 = (f32[2,24,256]{2,1,0:T(8,128)S(1)}, f32[2,24,256]{2,1,0:T(8,128)S(1)}, u32[]{:S(2)}, u32[]{:S(2)}) collective-permute-start(f32[2,24,256]{2,1,0:T(8,128)S(1)} %group_maps.1.refs_0_), channel_id=1, source_target_pairs={{0,8},{1,9},{2,10},{3,11},{4,12},{5,13},{6,14},{7,15},{8,0},{9,1},... | collective-permute-start | bytes 147464 | tf_op jit(solution)/shard_map/ppermute | solution.py:415
  16.0 2.6 %carry_maps.1 = (f32[2,2,64,128]{3,2,1,0:T(8,128)S(1)}, bf16[2,256,256]{2,1,0:T(8,128)(2,1)S(1)}, f32[2,2,64,128]{3,2,1,0:T(8,128)}) custom-call(f32[2,24,256]{2,1,0:T(8,128)S(1)} %get-tuple-element.23.refs_0_, f32[2,24,256]{2,1,0:T(8,128)S(1)} %collective-permute-done.1.refs_1_, f32[2,24,256]{2,1,0:T(8,128)S(1)} %collective-permute-done.2.refs_2_, ...), custom_call_target="tpu_custom_call" | custom-call | flops 1000000 | bytes 500000 | tf_op jit(solution)/shard_map/carry_maps/pallas_call | solution.py:433
  18.5 0.0 collective-permute-done.4.refs_1_
  18.6 1.1 %collective-permute-done.5.refs_2_ = f32[2,24,256]{2,1,0:T(8,128)S(1)} collective-permute-done((f32[2,24,256]{2,1,0:T(8,128)S(1)}, f32[2,24,256]{2,1,0:T(8,128)S(1)}, u32[]{:S(2)}, u32[]{:S(2)}) %collective-permute-start.5) | collective-permute-done | bytes 49184 | tf_op jit(solution)/shard_map/ppermute | solution.py:415
  19.7 0.0 collective-permute-done.6.refs_3_
  (4 shorter events, 0.0 us)
Async XLA Ops:
  0.0 2.0 %copy-start.1 = (bf16[2,2,64,128]{3,2,1,0:T(8,128)(2,1)S(1)}, bf16[2,2,64,128]{3,2,1,0:T(8,128)(2,1)}, u32[]{:S(2)}) copy-start(bf16[2,2,64,128]{3,2,1,0:T(8,128)(2,1)} %u_ref.1) | copy-start | bytes 196612
  0.0 2.0 %copy-start.2 = (bf16[2,2,64,128]{3,2,1,0:T(8,128)(2,1)S(1)}, bf16[2,2,64,128]{3,2,1,0:T(8,128)(2,1)}, u32[]{:S(2)}) copy-start(bf16[2,2,64,128]{3,2,1,0:T(8,128)(2,1)} %rhs_ref.1) | copy-start | bytes 196612
  0.0 2.0 %collective-permute-start = (bf16[2,2,64,128]{3,2,1,0:T(8,128)(2,1)}, bf16[2,2,64,128]{3,2,1,0:T(8,128)(2,1)S(1)}, u32[]{:S(2)}, u32[]{:S(2)}) collective-permute-start(bf16[2,2,64,128]{3,2,1,0:T(8,128)(2,1)} %u_ref.1), channel_id=1, source_target_pairs={{0,1},{1,0},{2,3},{3,2},{4,5},{5,4},{6,7},{7,6},{8,9},{9,8},{10,11... | collective-permute-start | bytes 196616 | tf_op jit(solution)/shard_map/ppermute | solution.py:415
  2.0 5.0 %copy-start = (f32[8,64,64]{2,1,0:T(8,128)S(1)}, f32[8,64,64]{2,1,0:T(8,128)}, u32[]{:S(2)}) copy-start(f32[8,64,64]{2,1,0:T(8,128)} %inv_ref.1) | copy-start | bytes 393220
  2.1 5.0 %copy-start.3 = (f32[2,16,128]{2,1,0:T(8,128)S(1)}, f32[2,16,128]{2,1,0:T(8,128)}, u32[]{:S(2)}) copy-start(f32[2,16,128]{2,1,0:T(8,128)} %inflow_ref.1) | copy-start | bytes 49156
  2.9 5.9 %collective-permute-start.1 = (f32[2,24,256]{2,1,0:T(8,128)S(1)}, f32[2,24,256]{2,1,0:T(8,128)S(1)}, u32[]{:S(2)}, u32[]{:S(2)}) collective-permute-start(f32[2,24,256]{2,1,0:T(8,128)S(1)} %get-tuple-element.23.refs_0_), channel_id=1, source_target_pairs={{0,6},{1,7},{2,4},{3,5},{4,2},{5,3},{6,0},{7,1},{8,14},{9,15},{10,... | collective-permute-start | bytes 147464 | tf_op jit(solution)/shard_map/ppermute | solution.py:415
  6.4 4.1 %collective-permute-start.2 = (f32[2,24,256]{2,1,0:T(8,128)S(1)}, f32[2,24,256]{2,1,0:T(8,128)S(1)}, u32[]{:S(2)}, u32[]{:S(2)}) collective-permute-start(f32[2,24,256]{2,1,0:T(8,128)S(1)} %get-tuple-element.23.refs_0_), channel_id=1, source_target_pairs={{0,4},{1,5},{2,6},{3,7},{4,0},{5,1},{6,2},{7,3},{8,12},{9,13},{10,... | collective-permute-start | bytes 147464 | tf_op jit(solution)/shard_map/ppermute | solution.py:415
  6.9 4.1 %collective-permute-start.3 = (f32[2,24,256]{2,1,0:T(8,128)S(1)}, f32[2,24,256]{2,1,0:T(8,128)S(1)}, u32[]{:S(2)}, u32[]{:S(2)}) collective-permute-start(f32[2,24,256]{2,1,0:T(8,128)S(1)} %get-tuple-element.23.refs_0_), channel_id=1, source_target_pairs={{0,2},{1,3},{2,0},{3,1},{4,6},{5,7},{6,4},{7,5},{8,10},{9,11},{10,... | collective-permute-start | bytes 147464 | tf_op jit(solution)/shard_map/ppermute | solution.py:415
  11.5 7.0 %collective-permute-start.4 = (f32[2,24,256]{2,1,0:T(8,128)S(1)}, f32[2,24,256]{2,1,0:T(8,128)S(1)}, u32[]{:S(2)}, u32[]{:S(2)}) collective-permute-start(f32[2,24,256]{2,1,0:T(8,128)S(1)} %group_maps.1.refs_0_), channel_id=1, source_target_pairs={{0,24},{1,25},{2,26},{3,27},{4,28},{5,29},{6,30},{7,31},{8,16},{9,... | collective-permute-start | bytes 147464 | tf_op jit(solution)/shard_map/ppermute | solution.py:415
  14.6 5.1 %collective-permute-start.5 = (f32[2,24,256]{2,1,0:T(8,128)S(1)}, f32[2,24,256]{2,1,0:T(8,128)S(1)}, u32[]{:S(2)}, u32[]{:S(2)}) collective-permute-start(f32[2,24,256]{2,1,0:T(8,128)S(1)} %group_maps.1.refs_0_), channel_id=1, source_target_pairs={{0,16},{1,17},{2,18},{3,19},{4,20},{5,21},{6,22},{7,23},{8,24},{9,... | collective-permute-start | bytes 147464 | tf_op jit(solution)/shard_map/ppermute | solution.py:415
  14.6 5.1 %collective-permute-start.6 = (f32[2,24,256]{2,1,0:T(8,128)S(1)}, f32[2,24,256]{2,1,0:T(8,128)S(1)}, u32[]{:S(2)}, u32[]{:S(2)}) collective-permute-start(f32[2,24,256]{2,1,0:T(8,128)S(1)} %group_maps.1.refs_0_), channel_id=1, source_target_pairs={{0,8},{1,9},{2,10},{3,11},{4,12},{5,13},{6,14},{7,15},{8,0},{9,1},... | collective-permute-start | bytes 147464 | tf_op jit(solution)/shard_map/ppermute | solution.py:415

commit v5 on v4

--- a/solution.py
+++ b/solution.py
@@ -62,14 +62,10 @@
 
 
 def encode(value):
-    high, low = split(value)
-    both = jnp.concatenate([high, low], axis=1)
-    tile = (iota((256, FACE), 0) % FACE == iota((256, FACE), 1)).astype(BF16)
-    spread = dot(tile, both)
-    keep = iota((256, 256), 0) // FACE == iota((256, 256), 1) % FACE
-    spread = jnp.where(keep, spread, 0.0).astype(BF16)
+    keep = (iota((256, 128), 0) // FACE == iota((256, 128), 1) % FACE).astype(BF16)
+    spread = [jnp.concatenate([part] * 16, axis=0) * keep for part in split(value)]
     gather = (iota((8, 256), 1) % 128 // FACE == iota((8, 256), 0)).astype(BF16)
-    return dot_rows(gather, spread)
+    return dot_rows(gather, jnp.concatenate(spread, axis=1))
 
 
 def face_columns(inv_rows, nodes):
@@ -104,11 +100,12 @@
 
 def params_kernel(cls_hbm, flag_hbm, x_hbm, lat_hbm, inv_hbm, weight_ref, out_ref, step_ref, label_ref,
                   cls_ref, flag_ref, x_ref, lat_ref, inv_ref, sems):
-    pairs = ((cls_hbm, cls_ref), (flag_hbm, flag_ref), (x_hbm, x_ref), (lat_hbm, lat_ref), (inv_hbm, inv_ref))
+    pairs = ((cls_hbm, cls_ref), (flag_hbm, flag_ref), (x_hbm, x_ref), (lat_hbm, lat_ref))
+    pairs += ((inv_hbm.at[:, inv_hbm.shape[1] - FACE:, :], inv_ref),)
     copies = [pltpu.make_async_copy(a, b, sems.at[i]) for i, (a, b) in enumerate(pairs)]
     for copy in copies:
         copy.start()
-    count, nodes, _ = inv_ref.shape
+    count, nodes, _ = inv_hbm.shape
     planes = cls_ref.shape[0]
     item, lane = iota((FACE, 128), 0), iota((FACE, 128), 1)
     places = [(lane == 64 + FACE * f + item).astype(BF16) for f in range(4)]
@@ -126,7 +123,7 @@
     for f in range(5):
         rows = (lat_ref[f] if f < 4 else x_ref[...]).reshape(count * FACE, FACE)
         placed.append(dot(jnp.concatenate(split(rows), axis=0), places[f]).astype(BF16))
-    inv_rows = [inv_ref[k, nodes - FACE:, :] for k in range(count)]
+    inv_rows = [inv_ref[k] for k in range(count)]
     gathered = face_columns(jnp.concatenate(inv_rows, axis=0), nodes)
     outs, steps = [], []
     for k in range(count):
@@ -212,21 +209,21 @@
     data = jnp.concatenate(data, axis=1)
     every = dot(out_ref[...], jnp.concatenate([data, data], axis=0))
     keep = (iota((256, 256), 0) // FACE == iota((256, 256), 1) // FACE).astype(BF16)
-    wholes = []
-    for at in range(planes * rows_y):
-        here = linear[:, at * 256:at * 256 + 256]
-        lin_ref[at // rows_y, at % rows_y] = here[:FACE] + here[FACE:]
-        both = here.astype(BF16)
-        if at < rows_y:
-            wholes.append((here[:FACE] + here[FACE:], both))
+    wholes, pairs = None, None
+    for x in range(planes):
+        here = [linear[:, at * 256:at * 256 + 256] for at in range(x * rows_y, (x + 1) * rows_y)]
+        both = [(part[:FACE].astype(BF16), part[FACE:].astype(BF16)) for part in here]
+        for y in range(rows_y):
+            lin_ref[x, y] = here[y][:FACE] + here[y][FACE:]
+        if wholes is None:
+            wholes, pairs = [part[:FACE] + part[FACE:] for part in here], both
         else:
-            pair = wholes[at % rows_y][1]
-            first, second = [jnp.concatenate([part] * 16, axis=0) * keep for part in (both[:FACE], both[FACE:])]
-            parts = dot(pair, first)
-            whole = parts[:FACE] + parts[FACE:] + dot(pair[:FACE], second)
-            if at < (planes - 1) * rows_y:
-                both = jnp.concatenate(split(whole), axis=0)
-            wholes[at % rows_y] = (whole, both)
+            blocks = [[jnp.concatenate([part] * 16, axis=0) * keep for part in parts] for parts in both]
+            stacks = [jnp.concatenate(pair, axis=0) for pair in pairs]
+            firsts = [dot(stack, block[0]) for stack, block in zip(stacks, blocks)]
+            seconds = [dot(pair[0], block[1]) for pair, block in zip(pairs, blocks)]
+            wholes = [first[:FACE] + first[FACE:] + second for first, second in zip(firsts, seconds)]
+            pairs = [split(whole) for whole in wholes]
     total = None
     for x in range(planes):
         begin = x * rows_y * columns
@@ -237,7 +234,7 @@
             flow = flow + class_sum(dot(step_ref[...], stacked(total)), label, FACE)
         total = flow
     for y in range(rows_y):
-        map_ref[y, 0:FACE] = wholes[y][0]
+        map_ref[y, 0:FACE] = wholes[y]
         map_ref[y, FACE:] = encode(total[:, y * columns:(y + 1) * columns])
 
 
@@ -246,17 +243,33 @@
     return [jnp.concatenate([part] * 16, axis=0) * keep for part in split(linear)]
 
 
+def half_weights(high, low, begin):
+    keep = (iota((128, 128), 0) // FACE == iota((128, 128), 1) // FACE).astype(BF16)
+    parts = [jnp.concatenate([part[:, begin:begin + 128]] * 8, axis=0) * keep for part in (high, low)]
+    return jnp.concatenate(parts, axis=0)
+
+
+def half_rows(high, low, begin):
+    high, low = high[:, begin:begin + 128], low[:, begin:begin + 128]
+    upper = jnp.concatenate([high, high], axis=1)
+    return jnp.concatenate([upper, jnp.concatenate([low, jnp.zeros_like(low)], axis=1)], axis=0)
+
+
+def joined_rows(pairs):
+    ready = [
+        (half_rows(*rows, begin), half_weights(*linear, begin)) for rows, linear in pairs for begin in (0, 128)
+    ]
+    sums = [dot(rows, weights) for rows, weights in ready]
+    sums = [both[:both.shape[0] // 2] + both[both.shape[0] // 2:] for both in sums]
+    return [jnp.concatenate(sums[i:i + 2], axis=1) for i in range(0, len(sums), 2)]
+
+
 def join_many(pairs):
-    ready = []
-    for earlier, later in pairs:
-        halves = split(jnp.concatenate([earlier, jnp.zeros((8, 256), F32)], axis=0))
-        ready.append((halves[0], jnp.concatenate(halves, axis=0), block_diagonal(later[:FACE])))
-    firsts = [dot(both, blocks[0]) for _, both, blocks in ready]
-    seconds = [dot(high, blocks[1]) for high, _, blocks in ready]
+    rest = jnp.zeros((8, 256), F32)
+    split_pairs = [(split(jnp.concatenate([first, rest], axis=0)), split(second[:FACE])) for first, second in pairs]
     joined = []
-    for parts, more, (_, later) in zip(firsts, seconds, pairs):
-        total = (parts[:32] + parts[32:] + more)[:24]
-        joined.append(jnp.concatenate([total[:FACE], total[FACE:] + later[FACE:]], axis=0))
+    for total, (_, later) in zip(joined_rows(split_pairs), pairs):
+        joined.append(jnp.concatenate([total[:FACE], total[FACE:24] + later[FACE:]], axis=0))
     return joined
 
 
@@ -291,15 +304,13 @@
 
 
 def carried(parts, traces, count):
-    first, second = split(jnp.concatenate(traces, axis=1))
-    row, lane = iota((256, 2 * FACE), 0), iota((256, 2 * FACE), 1)
-    spread = (lane == row % 128 // FACE + FACE * (row >= 128)).astype(BF16)
-    rest = jnp.zeros((8, first.shape[1]), BF16)
-    rows = dot(spread, jnp.concatenate([first, rest, second, rest], axis=0))
-    keep = iota((256, 256), 0) % FACE == iota((256, 256), 1) // FACE
-    here = [jnp.where(keep, rows[:, y * 256:y * 256 + 256], 0.0).astype(BF16) for y in range(len(parts))]
-    by_first = [dot_rows(part, data[:128]) for part, data in zip(parts, here)]
-    by_second = [dot_rows(part[:count], data[128:]) for part, data in zip(parts, here)]
+    keep = (iota((128, 256), 0) % FACE == iota((128, 256), 1) // FACE).astype(BF16)
+    here = []
+    for trace in traces:
+        rows = jnp.concatenate([jnp.broadcast_to(trace[t:t + 1], (FACE, 256)) for t in range(8)], axis=0)
+        here.append([part * keep for part in split(rows)])
+    by_first = [dot_rows(part, data[0]) for part, data in zip(parts, here)]
+    by_second = [dot_rows(part[:count], data[1]) for part, data in zip(parts, here)]
     return [first[:count] + first[count:] + second for first, second in zip(by_first, by_second)]
 
 
@@ -474,7 +485,7 @@
             pltpu.VMEM(flags.shape, jnp.int32),
             pltpu.VMEM(x_face.shape, F32),
             pltpu.VMEM(lateral_faces.shape, F32),
-            pltpu.VMEM(inverse.shape, F32),
+            pltpu.VMEM((count, FACE, nodes), F32),
             pltpu.SemaphoreType.DMA((5,)),
         ],
         space=pltpu.HBM,

time: 19.9 us -> 19.6 us (0.985)
  Pallas kernels: 7.34 us -> 5.98 us
  waiting for transfers between devices: 3.31 us -> 4.42 us
    pallas_call x6, Pallas kernels: 7.34 us -> 5.98 us  [call(): pl.pallas_call(kernel, out_shape=outs, in_specs=in_specs, out_specs=out_s...]
    ppermute x7, waiting for transfers between devices: 3.31 us -> 4.42 us  [moved(): return lax.ppermute(value, ('gx', 'gy'), pairs)]
  transfers between devices with their start and end apart: 7 -> 7, of which waited for: 3 -> 4; matrix products, arithmetic and copies ran while one was open for 0% -> 0% of each run, Pallas kernels for 30% -> 24%
where the time goes in v5:
time: 19.6 us; the launch traced here: 19.5 us
  starting transfers between devices  8.99 us (46%)
  Pallas kernels  5.98 us (31%)
  waiting for transfers between devices  4.42 us (23%)
    ppermute x7, starting transfers between devices, moved(): return lax.ppermute(value, ('gx', 'gy'), pairs)  8.99 us
    pallas_call x6, Pallas kernels, call(): pl.pallas_call(kernel, out_shape=outs, in_specs=in_specs, out_specs=out_s...  5.98 us
    ppermute x7, waiting for transfers between devices, moved(): return lax.ppermute(value, ('gx', 'gy'), pairs)  4.42 us
  transfers between devices with their start and end apart: 7, of which 4 were waited for; matrix products, arithmetic and copies ran while one was open for 0% of the time, Pallas kernels for 24%

profile of v5, /device:TPU:0, one launch (start us, length us, event | category | flops | bytes accessed | tf_op | source)
XLA Modules:
  0.0 19.5 jit_solution(14945609370078457482)
XLA Ops:
  0.0 0.5 %collective-permute-start = (bf16[2,2,64,128]{3,2,1,0:T(8,128)(2,1)}, bf16[2,2,64,128]{3,2,1,0:T(8,128)(2,1)S(1)}, u32[]{:S(2)}, u32[]{:S(2)}) collective-permute-start(bf16[2,2,64,128]{3,2,1,0:T(8,128)(2,1)} %u_ref.1), channel_id=1, source_target_pairs={{0,1},{1,0},{2,3},{3,2},{4,5},{5,4},{6,7},{7,6},{8,9},{9,8},{10,11... | collective-permute-start | bytes 196616 | tf_op jit(solution)/shard_map/ppermute | solution.py:426
  0.5 1.5 %class_matrices.1 = (bf16[80,2048]{1,0:T(8,128)(2,1)S(1)}, bf16[128,256]{1,0:T(8,128)(2,1)S(1)}, bf16[128,128]{1,0:T(8,128)(2,1)S(1)}, f32[12,128]{1,0:T(8,128)S(1)}) custom-call(s32[2,2,16]{2,1,0:T(2,128)} %cls_hbm.1, s32[2,2,2,16]{3,2,1,0:T(2,128)} %flag_hbm.1, f32[8,16,16]{2,1,0:T(8,128)} %x_hbm.1, f32[4,8,16,16]{3,2,1,0:T(8,128)} %lat_hbm.1, ...), custom_call_target="tpu_custom_call" | custom-call | flops 1000000 | bytes 500000 | tf_op jit(solution)/shard_map/class_matrices/pallas_call | solution.py:444
  1.9 0.0 copy-start
  1.9 0.0 collective-permute-done.below_ref.above_ref
  2.0 0.0 copy-done.1
  2.0 0.0 copy-done.2
  2.0 0.0 copy-start.3
  2.0 0.8 %sources.1 = (bf16[2,2,128,128]{3,2,1,0:T(8,128)(2,1)S(1)}, f32[2,16,256]{2,1,0:T(8,128)S(1)}, f32[2,2,16,256]{3,2,1,0:T(8,128)S(1)}, f32[2,24,256]{2,1,0:T(8,128)S(1)}) custom-call(bf16[2,2,64,128]{3,2,1,0:T(8,128)(2,1)S(1)} %copy-done.1, bf16[2,2,64,128]{3,2,1,0:T(8,128)(2,1)S(1)} %copy-done.2, ...), custom_call_target="tpu_custom_call" | custom-call | flops 1000000 | bytes 500000 | tf_op jit(solution)/shard_map/sources/pallas_call | solution.py:444
  2.8 3.5 %collective-permute-start.1 = (f32[2,24,256]{2,1,0:T(8,128)S(1)}, f32[2,24,256]{2,1,0:T(8,128)S(1)}, u32[]{:S(2)}, u32[]{:S(2)}) collective-permute-start(f32[2,24,256]{2,1,0:T(8,128)S(1)} %get-tuple-element.23.refs_0_), channel_id=1, source_target_pairs={{0,6},{1,7},{2,4},{3,5},{4,2},{5,3},{6,0},{7,1},{8,14},{9,15},{10,... | collective-permute-start | bytes 147464 | tf_op jit(solution)/shard_map/ppermute | solution.py:426
  6.3 0.5 %collective-permute-start.2 = (f32[2,24,256]{2,1,0:T(8,128)S(1)}, f32[2,24,256]{2,1,0:T(8,128)S(1)}, u32[]{:S(2)}, u32[]{:S(2)}) collective-permute-start(f32[2,24,256]{2,1,0:T(8,128)S(1)} %get-tuple-element.23.refs_0_), channel_id=1, source_target_pairs={{0,4},{1,5},{2,6},{3,7},{4,0},{5,1},{6,2},{7,3},{8,12},{9,13},{10,... | collective-permute-start | bytes 147464 | tf_op jit(solution)/shard_map/ppermute | solution.py:426
  6.8 0.1 collective-permute-start.3
  6.9 0.0 copy-done.3
  6.9 1.3 %local_solve.1 = (f32[2,2,64,128]{3,2,1,0:T(8,128)S(1)}, f32[2,8,256]{2,1,0:T(8,128)S(1)}, bf16[2,2,128,256]{3,2,1,0:T(8,128)(2,1)S(1)}, f32[1,2,8,256]{3,2,1,0:T(8,128)S(1)}) custom-call(bf16[2,2,128,128]{3,2,1,0:T(8,128)(2,1)S(1)} %get-tuple-element.24.data_ref, f32[12,128]{1,0:T(8,128)S(1)} %get-tuple-element.20.label_ref, ...), custom_call_target="tpu_custom_call" | custom-call | flops 1000000 | bytes 500000 | tf_op jit(solution)/shard_map/local_solve/pallas_call | solution.py:444
  8.1 0.5 %collective-permute-done.1.refs_1_ = f32[2,24,256]{2,1,0:T(8,128)S(1)} collective-permute-done((f32[2,24,256]{2,1,0:T(8,128)S(1)}, f32[2,24,256]{2,1,0:T(8,128)S(1)}, u32[]{:S(2)}, u32[]{:S(2)}) %collective-permute-start.1) | collective-permute-done | bytes 49184 | tf_op jit(solution)/shard_map/ppermute | solution.py:426
  8.6 1.7 %collective-permute-done.2.refs_2_ = f32[2,24,256]{2,1,0:T(8,128)S(1)} collective-permute-done((f32[2,24,256]{2,1,0:T(8,128)S(1)}, f32[2,24,256]{2,1,0:T(8,128)S(1)}, u32[]{:S(2)}, u32[]{:S(2)}) %collective-permute-start.2) | collective-permute-done | bytes 49184 | tf_op jit(solution)/shard_map/ppermute | solution.py:426
  10.4 0.5 %collective-permute-done.3.refs_3_ = f32[2,24,256]{2,1,0:T(8,128)S(1)} collective-permute-done((f32[2,24,256]{2,1,0:T(8,128)S(1)}, f32[2,24,256]{2,1,0:T(8,128)S(1)}, u32[]{:S(2)}, u32[]{:S(2)}) %collective-permute-start.3) | collective-permute-done | bytes 49184 | tf_op jit(solution)/shard_map/ppermute | solution.py:426
  10.9 0.4 %group_maps.1.refs_0_ = f32[2,24,256]{2,1,0:T(8,128)S(1)} custom-call(f32[2,24,256]{2,1,0:T(8,128)S(1)} %get-tuple-element.23.refs_0_, f32[2,24,256]{2,1,0:T(8,128)S(1)} %collective-permute-done.1.refs_1_, f32[2,24,256]{2,1,0:T(8,128)S(1)} %collective-permute-done.2.refs_2_, f32[2,24,256]{2,1,0:T(8,128)S(1)} %collective-permute-done.3.refs_3_, ...), custom_call_target="tpu_custom_call" | custom-call | flops 1000000 | bytes 500000 | tf_op jit(solution)/shard_map/group_maps/pallas_call | solution.py:444
  11.3 3.2 %collective-permute-start.4 = (f32[2,24,256]{2,1,0:T(8,128)S(1)}, f32[2,24,256]{2,1,0:T(8,128)S(1)}, u32[]{:S(2)}, u32[]{:S(2)}) collective-permute-start(f32[2,24,256]{2,1,0:T(8,128)S(1)} %group_maps.1.refs_0_), channel_id=1, source_target_pairs={{0,24},{1,25},{2,26},{3,27},{4,28},{5,29},{6,30},{7,31},{8,16},{9,... | collective-permute-start | bytes 147464 | tf_op jit(solution)/shard_map/ppermute | solution.py:426
  14.5 0.0 collective-permute-start.5
  14.5 1.2 %collective-permute-start.6 = (f32[2,24,256]{2,1,0:T(8,128)S(1)}, f32[2,24,256]{2,1,0:T(8,128)S(1)}, u32[]{:S(2)}, u32[]{:S(2)}) collective-permute-start(f32[2,24,256]{2,1,0:T(8,128)S(1)} %group_maps.1.refs_0_), channel_id=1, source_target_pairs={{0,8},{1,9},{2,10},{3,11},{4,12},{5,13},{6,14},{7,15},{8,0},{9,1},... | collective-permute-start | bytes 147464 | tf_op jit(solution)/shard_map/ppermute | solution.py:426
  15.7 2.0 %carry_maps.1 = (f32[2,2,64,128]{3,2,1,0:T(8,128)S(1)}, bf16[2,256,256]{2,1,0:T(8,128)(2,1)S(1)}, f32[2,2,64,128]{3,2,1,0:T(8,128)}) custom-call(f32[2,24,256]{2,1,0:T(8,128)S(1)} %get-tuple-element.23.refs_0_, f32[2,24,256]{2,1,0:T(8,128)S(1)} %collective-permute-done.1.refs_1_, f32[2,24,256]{2,1,0:T(8,128)S(1)} %collective-permute-done.2.refs_2_, ...), custom_call_target="tpu_custom_call" | custom-call | flops 1000000 | bytes 500000 | tf_op jit(solution)/shard_map/carry_maps/pallas_call | solution.py:444
  17.8 0.0 collective-permute-done.4.refs_1_
  17.8 1.7 %collective-permute-done.5.refs_2_ = f32[2,24,256]{2,1,0:T(8,128)S(1)} collective-permute-done((f32[2,24,256]{2,1,0:T(8,128)S(1)}, f32[2,24,256]{2,1,0:T(8,128)S(1)}, u32[]{:S(2)}, u32[]{:S(2)}) %collective-permute-start.5) | collective-permute-done | bytes 49184 | tf_op jit(solution)/shard_map/ppermute | solution.py:426
  19.5 0.0 collective-permute-done.6.refs_3_
  (4 shorter events, 0.0 us)
Async XLA Ops:
  0.0 2.0 %copy-start.1 = (bf16[2,2,64,128]{3,2,1,0:T(8,128)(2,1)S(1)}, bf16[2,2,64,128]{3,2,1,0:T(8,128)(2,1)}, u32[]{:S(2)}) copy-start(bf16[2,2,64,128]{3,2,1,0:T(8,128)(2,1)} %u_ref.1) | copy-start | bytes 196612
  0.0 2.0 %copy-start.2 = (bf16[2,2,64,128]{3,2,1,0:T(8,128)(2,1)S(1)}, bf16[2,2,64,128]{3,2,1,0:T(8,128)(2,1)}, u32[]{:S(2)}) copy-start(bf16[2,2,64,128]{3,2,1,0:T(8,128)(2,1)} %rhs_ref.1) | copy-start | bytes 196612
  0.0 1.9 %collective-permute-start = (bf16[2,2,64,128]{3,2,1,0:T(8,128)(2,1)}, bf16[2,2,64,128]{3,2,1,0:T(8,128)(2,1)S(1)}, u32[]{:S(2)}, u32[]{:S(2)}) collective-permute-start(bf16[2,2,64,128]{3,2,1,0:T(8,128)(2,1)} %u_ref.1), channel_id=1, source_target_pairs={{0,1},{1,0},{2,3},{3,2},{4,5},{5,4},{6,7},{7,6},{8,9},{9,8},{10,11... | collective-permute-start | bytes 196616 | tf_op jit(solution)/shard_map/ppermute | solution.py:426
  1.9 4.9 %copy-start = (f32[8,64,64]{2,1,0:T(8,128)S(1)}, f32[8,64,64]{2,1,0:T(8,128)}, u32[]{:S(2)}) copy-start(f32[8,64,64]{2,1,0:T(8,128)} %inv_ref.1) | copy-start | bytes 393220
  2.0 4.9 %copy-start.3 = (f32[2,16,128]{2,1,0:T(8,128)S(1)}, f32[2,16,128]{2,1,0:T(8,128)}, u32[]{:S(2)}) copy-start(f32[2,16,128]{2,1,0:T(8,128)} %inflow_ref.1) | copy-start | bytes 49156
  2.8 5.9 %collective-permute-start.1 = (f32[2,24,256]{2,1,0:T(8,128)S(1)}, f32[2,24,256]{2,1,0:T(8,128)S(1)}, u32[]{:S(2)}, u32[]{:S(2)}) collective-permute-start(f32[2,24,256]{2,1,0:T(8,128)S(1)} %get-tuple-element.23.refs_0_), channel_id=1, source_target_pairs={{0,6},{1,7},{2,4},{3,5},{4,2},{5,3},{6,0},{7,1},{8,14},{9,15},{10,... | collective-permute-start | bytes 147464 | tf_op jit(solution)/shard_map/ppermute | solution.py:426
  6.3 4.1 %collective-permute-start.2 = (f32[2,24,256]{2,1,0:T(8,128)S(1)}, f32[2,24,256]{2,1,0:T(8,128)S(1)}, u32[]{:S(2)}, u32[]{:S(2)}) collective-permute-start(f32[2,24,256]{2,1,0:T(8,128)S(1)} %get-tuple-element.23.refs_0_), channel_id=1, source_target_pairs={{0,4},{1,5},{2,6},{3,7},{4,0},{5,1},{6,2},{7,3},{8,12},{9,13},{10,... | collective-permute-start | bytes 147464 | tf_op jit(solution)/shard_map/ppermute | solution.py:426
  6.8 4.1 %collective-permute-start.3 = (f32[2,24,256]{2,1,0:T(8,128)S(1)}, f32[2,24,256]{2,1,0:T(8,128)S(1)}, u32[]{:S(2)}, u32[]{:S(2)}) collective-permute-start(f32[2,24,256]{2,1,0:T(8,128)S(1)} %get-tuple-element.23.refs_0_), channel_id=1, source_target_pairs={{0,2},{1,3},{2,0},{3,1},{4,6},{5,7},{6,4},{7,5},{8,10},{9,11},{10,... | collective-permute-start | bytes 147464 | tf_op jit(solution)/shard_map/ppermute | solution.py:426
  11.3 6.5 %collective-permute-start.4 = (f32[2,24,256]{2,1,0:T(8,128)S(1)}, f32[2,24,256]{2,1,0:T(8,128)S(1)}, u32[]{:S(2)}, u32[]{:S(2)}) collective-permute-start(f32[2,24,256]{2,1,0:T(8,128)S(1)} %group_maps.1.refs_0_), channel_id=1, source_target_pairs={{0,24},{1,25},{2,26},{3,27},{4,28},{5,29},{6,30},{7,31},{8,16},{9,... | collective-permute-start | bytes 147464 | tf_op jit(solution)/shard_map/ppermute | solution.py:426
  14.5 5.0 %collective-permute-start.5 = (f32[2,24,256]{2,1,0:T(8,128)S(1)}, f32[2,24,256]{2,1,0:T(8,128)S(1)}, u32[]{:S(2)}, u32[]{:S(2)}) collective-permute-start(f32[2,24,256]{2,1,0:T(8,128)S(1)} %group_maps.1.refs_0_), channel_id=1, source_target_pairs={{0,16},{1,17},{2,18},{3,19},{4,20},{5,21},{6,22},{7,23},{8,24},{9,... | collective-permute-start | bytes 147464 | tf_op jit(solution)/shard_map/ppermute | solution.py:426
  14.5 5.0 %collective-permute-start.6 = (f32[2,24,256]{2,1,0:T(8,128)S(1)}, f32[2,24,256]{2,1,0:T(8,128)S(1)}, u32[]{:S(2)}, u32[]{:S(2)}) collective-permute-start(f32[2,24,256]{2,1,0:T(8,128)S(1)} %group_maps.1.refs_0_), channel_id=1, source_target_pairs={{0,8},{1,9},{2,10},{3,11},{4,12},{5,13},{6,14},{7,15},{8,0},{9,1},... | collective-permute-start | bytes 147464 | tf_op jit(solution)/shard_map/ppermute | solution.py:426

commit v6 on v5

--- a/solution.py
+++ b/solution.py
@@ -273,9 +273,13 @@
     return joined
 
 
-def block_slot(mine, other, size, power):
+def sent_steps(size, first):
+    return (2, 1) + tuple(range(3, size)) if first == 2 and size > 2 else tuple(range(1, size))
+
+
+def block_slot(mine, other, size, power, first):
     step = (mine ^ other) if power else (mine - other + size) % size
-    return (size - step) % size
+    return step + 1 * (step == 1) - 1 * (step == 2) if first == 2 and size > 2 else step
 
 
 def group_kernel(size, power, outer, *refs):
@@ -288,7 +292,7 @@
     def _():
         for s in range(size):
             held[s] = blocks[s][...]
-        slots = [block_slot(mine, j, size, power) for j in range(size)]
+        slots = [block_slot(mine, j, size, power, 1) for j in range(size)]
         maps = [[held[slot, y] for slot in slots] for y in range(rows_y)]
         while len(maps[0]) > 1:
             length = len(maps[0])
@@ -356,40 +360,78 @@
                 offset_ref[x, y] = encode(flow_ref[x, :, y * columns:(y + 1) * columns])
 
 
-def carry_kernel(size, power, *refs):
-    blocks = refs[:size]
-    local_ref, start_ref, chosen_ref, offset_ref, lin_ref = refs[size:size + 5]
-    base_ref, part_ref, out_ref, held, result_ref, sems = refs[size + 5:]
-    planes, rows_y, nodes, _ = base_ref.shape
+def ahead_kernel(size, power, *refs):
+    blocks, ahead_ref, held = refs[:size], refs[size + 1], refs[size + 2]
+    rows_y = ahead_ref.shape[0]
     for s in range(size):
         held[s] = blocks[s][...]
-    place = lax.axis_index("gx")
-    mine = place % size
+    mine = lax.axis_index("gx") % size
     same = (iota((24, 256), 1) % FACE == iota((24, 256), 0)).astype(F32)
     ahead = [same] * rows_y
     for j in range(size - 1):
-        slot = block_slot(mine, j, size, power)
+        slot = block_slot(mine, j, size, power, 1)
         block = [held[slot, y] for y in range(rows_y)]
         joined = block if j == 0 else join_many([(ahead[y], block[y]) for y in range(rows_y)])
         ahead = [jnp.where(mine > j, joined[y], ahead[y]) for y in range(rows_y)]
-    for x in range(planes):
-        chosen = [chosen_ref[x, y] for y in range(rows_y)]
-        sums = carried(chosen, [ahead[y][FACE:] for y in range(rows_y)], nodes)
-        pairs = [block_diagonal(ahead[y][:FACE]) for y in range(rows_y)]
-        firsts = [dot_rows(chosen[y], pairs[y][0]) for y in range(rows_y)]
-        seconds = [dot_rows(chosen[y][:nodes], pairs[y][1]) for y in range(rows_y)]
-        for y in range(rows_y):
-            base_ref[x, y] = local_ref[x, y] + sums[y]
-            high, low = split(firsts[y][:nodes] + firsts[y][nodes:] + seconds[y])
-            part_ref[y, pl.ds(x * nodes, nodes), :] = high
-            part_ref[y, pl.ds((planes + x) * nodes, nodes), :] = low
-        if x < planes - 1:
-            own = [jnp.concatenate([lin_ref[x, y], offset_ref[x, y]], axis=0) for y in range(rows_y)]
-            ahead = join_many([(ahead[y], own[y]) for y in range(rows_y)])
+    for y in range(rows_y):
+        ahead_ref[y] = ahead[y]
+
+
+def carry_kernel(size, swapped, ahead_ref, local_ref, start_ref, chosen_ref, offset_ref, lin_ref, base_ref, part_ref, out_ref, result_ref, sems):
+    planes, rows_y, nodes, _ = base_ref.shape
+    place = lax.axis_index("gx")
+    if swapped:
+        ahead_ref = ahead_ref.at[1 - lax.axis_index("gy") % 2]
+    row_range = range(rows_y)
+
+    def plane_map(x):
+        return [jnp.concatenate([lin_ref[x, y], offset_ref[x, y]], axis=0) for y in row_range]
 
     @pl.when(place < size)
     def _():
-        write_nodes(result_ref, out_ref, sems, base_ref, part_ref, [start_ref[y] for y in range(rows_y)])
+        traces = [advance(start_ref[y], ahead_ref[y]) for y in row_range]
+        copies = []
+        for x in range(planes):
+            sums = carried([chosen_ref[x, y] for y in row_range], traces, nodes)
+            for y in row_range:
+                result_ref[x, y] = local_ref[x, y] + sums[y]
+                copies.append(pltpu.make_async_copy(result_ref.at[x, y], out_ref.at[x, y], sems.at[x, y]))
+                copies[-1].start()
+            if x < planes - 1:
+                traces = [advance(trace, own) for trace, own in zip(traces, plane_map(x))]
+        for copy in copies:
+            copy.wait()
+
+    @pl.when(place >= size)
+    def _():
+        ahead = [ahead_ref[y] for y in row_range]
+        for x in range(planes):
+            chosen = [chosen_ref[x, y] for y in row_range]
+            sums = carried(chosen, [ahead[y][FACE:] for y in row_range], nodes)
+            pairs = [block_diagonal(ahead[y][:FACE]) for y in row_range]
+            firsts = [dot_rows(chosen[y], pairs[y][0]) for y in row_range]
+            seconds = [dot_rows(chosen[y][:nodes], pairs[y][1]) for y in row_range]
+            for y in row_range:
+                base_ref[x, y] = local_ref[x, y] + sums[y]
+                high, low = split(firsts[y][:nodes] + firsts[y][nodes:] + seconds[y])
+                part_ref[y, pl.ds(x * nodes, nodes), :] = high
+                part_ref[y, pl.ds((planes + x) * nodes, nodes), :] = low
+            if x < planes - 1:
+                ahead = join_many(list(zip(ahead, plane_map(x))))
+
+
+def finish_places(places, steps, inner, *refs):
+    blocks = refs[:len(steps)]
+    start_ref, base_ref, part_ref, _, out_ref, result_ref, sems = refs[len(steps):]
+    mine = lax.axis_index("gx") // inner
+    for place in places:
+        @pl.when(mine == place)
+        def _():
+            traces = [start_ref[y] for y in range(base_ref.shape[1])]
+            for j in range(place):
+                block = blocks[steps.index(place ^ j)]
+                traces = [advance(trace, block[y]) for y, trace in enumerate(traces)]
+            write_nodes(result_ref, out_ref, sems, base_ref, part_ref, traces)
 
 
 def finish_kernel(size, inner, power, *refs):
@@ -397,29 +439,20 @@
     start_ref, base_ref, part_ref, _, out_ref, result_ref, sems = refs[size:size + 7]
     rows_y = base_ref.shape[1]
     mine = lax.axis_index("gx") // inner
-    if power and size <= 4:
-        for place in range(1, size):
-            @pl.when(mine == place)
-            def _():
-                traces = [start_ref[y] for y in range(rows_y)]
-                for j in range(place):
-                    traces = [advance(traces[y], blocks[block_slot(place, j, size, power)][y]) for y in range(rows_y)]
-                write_nodes(result_ref, out_ref, sems, base_ref, part_ref, traces)
-    else:
-        held = refs[size + 7]
-        for s in range(size):
-            held[s] = blocks[s][...]
-
-        @pl.when(mine > 0)
-        def _():
-            traces = []
-            for y in range(rows_y):
-                trace = start_ref[y]
-                for j in range(size - 1):
-                    slot = block_slot(mine, j, size, power)
-                    trace = jnp.where(mine > j, advance(trace, held[slot, y]), trace)
-                traces.append(trace)
-            write_nodes(result_ref, out_ref, sems, base_ref, part_ref, traces)
+    held = refs[size + 7]
+    for s in range(size):
+        held[s] = blocks[s][...]
+
+    @pl.when(mine > 0)
+    def _():
+        traces = []
+        for y in range(rows_y):
+            trace = start_ref[y]
+            for j in range(size - 1):
+                slot = block_slot(mine, j, size, power, 2)
+                trace = jnp.where(mine > j, advance(trace, held[slot, y]), trace)
+            traces.append(trace)
+        write_nodes(result_ref, out_ref, sems, base_ref, part_ref, traces)
 
 
 def moved(value, pairs):
@@ -504,9 +537,14 @@
     inner = 4 if gx_size % 4 == 0 else 1
     outer = gx_size // inner
     power = outer & (outer - 1) == 0
-    near = [here]
-    for s in range(inner - 1, 0, -1):
-        near.append(moved(here, [(at(x, y), at(x ^ s, y)) for x, y in everyone]))
+    other = 1 if gy_size % 2 == 0 else 0
+
+    def exchanged(value, step):
+        if power or step < inner:
+            return moved(value, [(at(x, y), at(x ^ step, y ^ other)) for x, y in everyone])
+        return moved(value, [(at(x, y), at((x + step) % gx_size, y ^ other)) for x, y in everyone])
+
+    near = ((exchanged(here, 0) if other else here),) + tuple(exchanged(here, s) for s in sent_steps(inner, 1))
     nodes_shape = (planes, rows_y, nodes, columns)
     writing = [pltpu.VMEM(nodes_shape, F32), pltpu.SemaphoreType.DMA((planes, rows_y))]
     local, start, chosen, offsets = call(
@@ -525,39 +563,64 @@
         functools.partial(group_kernel, inner, True, outer),
         shape((rows_y, 24, 256)),
         "group_maps",
-        tuple(near) + (start,),
+        near + (start,),
         [pltpu.VMEM((inner, rows_y, 24, 256), F32)],
     )
-    blocks = [total]
-    for s in range(outer - 1, 0, -1):
-        if power:
-            pairs = [(at(x, y), at(x ^ (s * inner), y)) for x, y in everyone]
-        else:
-            pairs = [(at(x, y), at((x + s * inner) % gx_size, y)) for x, y in everyone]
-        blocks.append(moved(total, pairs))
+    blocks = [total] + [exchanged(total, s * inner) for s in sent_steps(outer, 2)]
+    ahead = call(
+        functools.partial(ahead_kernel, inner, True),
+        shape((rows_y, 24, 256)),
+        "maps_ahead",
+        near + (total,),
+        [pltpu.VMEM((inner, rows_y, 24, 256), F32)],
+    )
+    if other:
+        couples = [[y, y + 1] for y in range(0, gy_size, 2)]
+        ahead = lax.all_gather(ahead, "gy", axis_index_groups=couples)
     base, parts, out = call(
-        functools.partial(carry_kernel, inner, True),
+        functools.partial(carry_kernel, inner, other == 1),
         (
             shape(nodes_shape),
             shape((rows_y, 2 * planes * nodes, 256), BF16),
             pltpu.HBM(nodes_shape, F32),
         ),
         "carry_maps",
-        tuple(near) + (local, start, chosen, offsets, linear),
-        [pltpu.VMEM((inner, rows_y, 24, 256), F32)] + writing,
+        (ahead, local, start, chosen, offsets, linear),
+        writing,
         out_spaces=(pltpu.VMEM, pltpu.VMEM, pltpu.HBM),
     )
-    held = [] if power and outer <= 4 else [pltpu.VMEM((outer, rows_y, 24, 256), F32)]
-    args = tuple(blocks) + (start, base, parts, out)
-    return call(
+    def written(kernel, name, args, scratch):
+        return call(
+            kernel,
+            pltpu.HBM(nodes_shape, F32),
+            name,
+            args,
+            scratch,
+            space=(pltpu.VMEM,) * (len(args) - 1) + (pltpu.HBM,),
+            out_spaces=pltpu.HBM,
+            aliases={len(args) - 1: 0},
+        )
+
+    if power and outer == 4:
+        steps = sent_steps(outer, 2)
+        early = (3, 1)
+        out = written(
+            functools.partial(finish_places, (1,), early, inner),
+            "finish_second",
+            tuple(blocks[1 + steps.index(one)] for one in early) + (start, base, parts, out),
+            writing,
+        )
+        return written(
+            functools.partial(finish_places, (2, 3), steps, inner),
+            "finish_last",
+            tuple(blocks[1:]) + (start, base, parts, out),
+            writing,
+        )
+    return written(
         functools.partial(finish_kernel, outer, inner, power),
-        pltpu.HBM(nodes_shape, F32),
         "finish",
-        args,
-        writing + held,
-        space=(pltpu.VMEM,) * (len(args) - 1) + (pltpu.HBM,),
-        out_spaces=pltpu.HBM,
-        aliases={len(args) - 1: 0},
+        tuple(blocks) + (start, base, parts, out),
+        writing + [pltpu.VMEM((outer, rows_y, 24, 256), F32)],
     )
 
 

time: 19.6 us -> 18.7 us (0.954)
  waiting for transfers between devices: 4.42 us -> 2.07 us
  blocking collectives: 0 us -> 1.88 us
  Pallas kernels: 5.98 us -> 5.65 us
    ppermute x7 -> x8, waiting for transfers between devices: 4.42 us -> 2.07 us  [moved(): return lax.ppermute(value, ('gx', 'gy'), pairs)]
    all_gather x0 -> x1, blocking collectives: none -> 1.88 us  [on_device(): ahead = lax.all_gather(ahead, 'gy', axis_index_groups=couples)]
    pallas_call x6 -> x8, Pallas kernels: 5.98 us -> 5.65 us  [call(): pl.pallas_call(kernel, out_shape=outs, in_specs=in_specs, out_specs=out_s...]
    ppermute x7 -> x8, starting transfers between devices: 8.99 us -> 8.82 us  [moved(): return lax.ppermute(value, ('gx', 'gy'), pairs)]
  transfers between devices with their start and end apart: 7 -> 8, of which waited for: 4 -> 3; matrix products, arithmetic and copies ran while one was open for 0% -> 0% of each run, Pallas kernels for 24% -> 24%
where the time goes in v6:
time: 18.7 us; the launch traced here: 18.5 us
  starting transfers between devices  8.82 us (47%)
  Pallas kernels  5.65 us (30%)
  waiting for transfers between devices  2.07 us (11%)
  blocking collectives  1.88 us (10%)
    ppermute x8, starting transfers between devices, moved(): return lax.ppermute(value, ('gx', 'gy'), pairs)  8.82 us
    pallas_call x8, Pallas kernels, call(): pl.pallas_call(kernel, out_shape=outs, in_specs=in_specs, out_specs=out_s...  5.65 us
    ppermute x8, waiting for transfers between devices, moved(): return lax.ppermute(value, ('gx', 'gy'), pairs)  2.07 us
    all_gather x1, blocking collectives, on_device(): ahead = lax.all_gather(ahead, 'gy', axis_index_groups=couples)  1.88 us
  transfers between devices with their start and end apart: 8, of which 3 were waited for; matrix products, arithmetic and copies ran while one was open for 0% of the time, Pallas kernels for 24%

profile of v6, /device:TPU:0, one launch (start us, length us, event | category | flops | bytes accessed | tf_op | source)
XLA Modules:
  0.0 18.5 jit_solution(16160852786418495009)
XLA Ops:
  0.0 0.5 %collective-permute-start = (bf16[2,2,64,128]{3,2,1,0:T(8,128)(2,1)}, bf16[2,2,64,128]{3,2,1,0:T(8,128)(2,1)S(1)}, u32[]{:S(2)}, u32[]{:S(2)}) collective-permute-start(bf16[2,2,64,128]{3,2,1,0:T(8,128)(2,1)} %u_ref.1), channel_id=1, source_target_pairs={{0,1},{1,0},{2,3},{3,2},{4,5},{5,4},{6,7},{7,6},{8,9},{9,8},{10,11... | collective-permute-start | bytes 196616 | tf_op jit(solution)/shard_map/ppermute | solution.py:459
  0.5 1.5 %class_matrices.1 = (bf16[80,2048]{1,0:T(8,128)(2,1)S(1)}, bf16[128,256]{1,0:T(8,128)(2,1)S(1)}, bf16[128,128]{1,0:T(8,128)(2,1)S(1)}, f32[12,128]{1,0:T(8,128)S(1)}) custom-call(s32[2,2,16]{2,1,0:T(2,128)} %cls_hbm.1, s32[2,2,2,16]{3,2,1,0:T(2,128)} %flag_hbm.1, f32[8,16,16]{2,1,0:T(8,128)} %x_hbm.1, f32[4,8,16,16]{3,2,1,0:T(8,128)} %lat_hbm.1, ...), custom_call_target="tpu_custom_call" | custom-call | flops 1000000 | bytes 500000 | tf_op jit(solution)/shard_map/class_matrices/pallas_call | solution.py:477
  1.9 0.0 copy-start
  1.9 0.0 collective-permute-done.below_ref.above_ref
  2.0 0.0 copy-start.3
  2.0 0.8 %sources.1 = (bf16[2,2,128,128]{3,2,1,0:T(8,128)(2,1)S(1)}, f32[2,16,256]{2,1,0:T(8,128)S(1)}, f32[2,2,16,256]{3,2,1,0:T(8,128)S(1)}, f32[2,24,256]{2,1,0:T(8,128)S(1)}) custom-call(bf16[2,2,64,128]{3,2,1,0:T(8,128)(2,1)S(1)} %copy-done.1, bf16[2,2,64,128]{3,2,1,0:T(8,128)(2,1)S(1)} %copy-done.2, ...), custom_call_target="tpu_custom_call" | custom-call | flops 1000000 | bytes 500000 | tf_op jit(solution)/shard_map/sources/pallas_call | solution.py:477
  2.8 3.6 %collective-permute-start.4 = (f32[2,24,256]{2,1,0:T(8,128)S(1)}, f32[2,24,256]{2,1,0:T(8,128)S(1)}, u32[]{:S(2)}, u32[]{:S(2)}) collective-permute-start(f32[2,24,256]{2,1,0:T(8,128)S(1)} %get-tuple-element.23), channel_id=1, source_target_pairs={{0,7},{1,6},{2,5},{3,4},{4,3},{5,2},{6,1},{7,0},{8,15},{9,14},{10,... | collective-permute-start | bytes 147464 | tf_op jit(solution)/shard_map/ppermute | solution.py:459
  6.3 0.1 collective-permute-start.3
  6.5 0.1 collective-permute-start.2
  6.6 0.5 %collective-permute-start.1 = (f32[2,24,256]{2,1,0:T(8,128)S(1)}, f32[2,24,256]{2,1,0:T(8,128)S(1)}, u32[]{:S(2)}, u32[]{:S(2)}) collective-permute-start(f32[2,24,256]{2,1,0:T(8,128)S(1)} %get-tuple-element.23), channel_id=1, source_target_pairs={{0,1},{1,0},{2,3},{3,2},{4,5},{5,4},{6,7},{7,6},{8,9},{9,8},{10,11... | collective-permute-start | bytes 147464 | tf_op jit(solution)/shard_map/ppermute | solution.py:459
  7.1 1.3 %local_solve.1 = (f32[2,2,64,128]{3,2,1,0:T(8,128)S(1)}, f32[2,8,256]{2,1,0:T(8,128)S(1)}, bf16[2,2,128,256]{3,2,1,0:T(8,128)(2,1)S(1)}, f32[1,2,8,256]{3,2,1,0:T(8,128)S(1)}) custom-call(bf16[2,2,128,128]{3,2,1,0:T(8,128)(2,1)S(1)} %get-tuple-element.24.data_ref, f32[12,128]{1,0:T(8,128)S(1)} %get-tuple-element.20.label_ref, ...), custom_call_target="tpu_custom_call" | custom-call | flops 1000000 | bytes 500000 | tf_op jit(solution)/shard_map/local_solve/pallas_call | solution.py:477
  8.3 0.1 collective-permute-done.4.refs_3_
  8.5 1.7 %collective-permute-done.3.refs_2_ = f32[2,24,256]{2,1,0:T(8,128)S(1)} collective-permute-done((f32[2,24,256]{2,1,0:T(8,128)S(1)}, f32[2,24,256]{2,1,0:T(8,128)S(1)}, u32[]{:S(2)}, u32[]{:S(2)}) %collective-permute-start.3) | collective-permute-done | bytes 49184 | tf_op jit(solution)/shard_map/ppermute | solution.py:459
  10.2 0.0 collective-permute-done.2.refs_1_
  10.2 0.0 collective-permute-done.1.refs_0_
  10.2 0.4 %group_maps.1.refs_4_ = f32[2,24,256]{2,1,0:T(8,128)S(1)} custom-call(f32[2,24,256]{2,1,0:T(8,128)S(1)} %collective-permute-done.1.refs_0_, f32[2,24,256]{2,1,0:T(8,128)S(1)} %collective-permute-done.2.refs_1_, f32[2,24,256]{2,1,0:T(8,128)S(1)} %collective-permute-done.3.refs_2_, f32[2,24,256]{2,1,0:T(8,128)S(1)} %collective-permute-done.4.refs_3_, ...), custom_call_target="tpu_custom_call" | custom-call | flops 1000000 | bytes 500000 | tf_op jit(solution)/shard_map/group_maps/pallas_call | solution.py:477
  10.6 3.2 %collective-permute-start.7 = (f32[2,24,256]{2,1,0:T(8,128)S(1)}, f32[2,24,256]{2,1,0:T(8,128)S(1)}, u32[]{:S(2)}, u32[]{:S(2)}) collective-permute-start(f32[2,24,256]{2,1,0:T(8,128)S(1)} %group_maps.1.refs_4_), channel_id=1, source_target_pairs={{0,25},{1,24},{2,27},{3,26},{4,29},{5,28},{6,31},{7,30},{8,17},{9,... | collective-permute-start | bytes 147464 | tf_op jit(solution)/shard_map/ppermute | solution.py:459
  13.8 0.9 %collective-permute-start.5 = (f32[2,24,256]{2,1,0:T(8,128)S(1)}, f32[2,24,256]{2,1,0:T(8,128)S(1)}, u32[]{:S(2)}, u32[]{:S(2)}) collective-permute-start(f32[2,24,256]{2,1,0:T(8,128)S(1)} %group_maps.1.refs_4_), channel_id=1, source_target_pairs={{0,17},{1,16},{2,19},{3,18},{4,21},{5,20},{6,23},{7,22},{8,25},{9,... | collective-permute-start | bytes 147464 | tf_op jit(solution)/shard_map/ppermute | solution.py:459
  14.7 0.3 %maps_ahead.1 = f32[2,24,256]{2,1,0:T(8,128)S(1)} custom-call(f32[2,24,256]{2,1,0:T(8,128)S(1)} %collective-permute-done.1.refs_0_, f32[2,24,256]{2,1,0:T(8,128)S(1)} %collective-permute-done.2.refs_1_, f32[2,24,256]{2,1,0:T(8,128)S(1)} %collective-permute-done.3.refs_2_, f32[2,24,256]{2,1,0:T(8,128)S(1)} %collective-permute-done.4.refs_3_, ...), custom_call_target="tpu_custom_call" | custom-call | flops 1000000 | bytes 500000 | tf_op jit(solution)/shard_map/maps_ahead/pallas_call | solution.py:477
  15.0 1.9 %all-gather = f32[4,24,256]{2,1,0:T(8,128)S(1)} all-gather(f32[2,24,256]{2,1,0:T(8,128)S(1)} %maps_ahead.1), channel_id=2, replica_groups={{0,1},{2,3},{4,5},{6,7},{8,9},{10,11},{12,13},{14,15},{16,17},{18,19},{..., dimensions={0}, use_global_device_ids=true | all-gather | bytes 147456 | tf_op jit(solution)/shard_map/all_gather | solution.py:579
  16.9 1.3 %carry_maps.1 = (f32[2,2,64,128]{3,2,1,0:T(8,128)S(1)}, bf16[2,256,256]{2,1,0:T(8,128)(2,1)S(1)}, f32[2,2,64,128]{3,2,1,0:T(8,128)}) custom-call(f32[2,2,24,256]{3,2,1,0:T(8,128)S(1)} %bitcast.1, f32[2,2,64,128]{3,2,1,0:T(8,128)S(1)} %get-tuple-element.28.local_ref, f32[2,8,256]{2,1,0:T(8,128)S(1)} %get-tuple-element.27.refs_4_.start_ref.refs_2_.refs_3_, ...), custom_call_target="tpu_custom_call" | custom-call | flops 1000000 | bytes 500000 | tf_op jit(solution)/shard_map/carry_maps/pallas_call | solution.py:477
  18.2 0.0 collective-permute-done.6.refs_1_
  18.2 0.1 finish_second.1.refs_6_
  18.3 0.2 %collective-permute-done.5.refs_0_ = f32[2,24,256]{2,1,0:T(8,128)S(1)} collective-permute-done((f32[2,24,256]{2,1,0:T(8,128)S(1)}, f32[2,24,256]{2,1,0:T(8,128)S(1)}, u32[]{:S(2)}, u32[]{:S(2)}) %collective-permute-start.5) | collective-permute-done | bytes 49184 | tf_op jit(solution)/shard_map/ppermute | solution.py:459
  (9 shorter events, 0.1 us)
Async XLA Ops:
  0.0 2.0 %copy-start.1 = (bf16[2,2,64,128]{3,2,1,0:T(8,128)(2,1)S(1)}, bf16[2,2,64,128]{3,2,1,0:T(8,128)(2,1)}, u32[]{:S(2)}) copy-start(bf16[2,2,64,128]{3,2,1,0:T(8,128)(2,1)} %u_ref.1) | copy-start | bytes 196612
  0.0 2.0 %copy-start.2 = (bf16[2,2,64,128]{3,2,1,0:T(8,128)(2,1)S(1)}, bf16[2,2,64,128]{3,2,1,0:T(8,128)(2,1)}, u32[]{:S(2)}) copy-start(bf16[2,2,64,128]{3,2,1,0:T(8,128)(2,1)} %rhs_ref.1) | copy-start | bytes 196612
  0.0 1.9 %collective-permute-start = (bf16[2,2,64,128]{3,2,1,0:T(8,128)(2,1)}, bf16[2,2,64,128]{3,2,1,0:T(8,128)(2,1)S(1)}, u32[]{:S(2)}, u32[]{:S(2)}) collective-permute-start(bf16[2,2,64,128]{3,2,1,0:T(8,128)(2,1)} %u_ref.1), channel_id=1, source_target_pairs={{0,1},{1,0},{2,3},{3,2},{4,5},{5,4},{6,7},{7,6},{8,9},{9,8},{10,11... | collective-permute-start | bytes 196616 | tf_op jit(solution)/shard_map/ppermute | solution.py:459
  1.9 5.1 %copy-start = (f32[8,64,64]{2,1,0:T(8,128)S(1)}, f32[8,64,64]{2,1,0:T(8,128)}, u32[]{:S(2)}) copy-start(f32[8,64,64]{2,1,0:T(8,128)} %inv_ref.1) | copy-start | bytes 393220
  2.0 5.1 %copy-start.3 = (f32[2,16,128]{2,1,0:T(8,128)S(1)}, f32[2,16,128]{2,1,0:T(8,128)}, u32[]{:S(2)}) copy-start(f32[2,16,128]{2,1,0:T(8,128)} %inflow_ref.1) | copy-start | bytes 49156
  2.8 5.7 %collective-permute-start.4 = (f32[2,24,256]{2,1,0:T(8,128)S(1)}, f32[2,24,256]{2,1,0:T(8,128)S(1)}, u32[]{:S(2)}, u32[]{:S(2)}) collective-permute-start(f32[2,24,256]{2,1,0:T(8,128)S(1)} %get-tuple-element.23), channel_id=1, source_target_pairs={{0,7},{1,6},{2,5},{3,4},{4,3},{5,2},{6,1},{7,0},{8,15},{9,14},{10,... | collective-permute-start | bytes 147464 | tf_op jit(solution)/shard_map/ppermute | solution.py:459
  6.3 3.8 %collective-permute-start.3 = (f32[2,24,256]{2,1,0:T(8,128)S(1)}, f32[2,24,256]{2,1,0:T(8,128)S(1)}, u32[]{:S(2)}, u32[]{:S(2)}) collective-permute-start(f32[2,24,256]{2,1,0:T(8,128)S(1)} %get-tuple-element.23), channel_id=1, source_target_pairs={{0,5},{1,4},{2,7},{3,6},{4,1},{5,0},{6,3},{7,2},{8,13},{9,12},{10,... | collective-permute-start | bytes 147464 | tf_op jit(solution)/shard_map/ppermute | solution.py:459
  6.5 3.7 %collective-permute-start.2 = (f32[2,24,256]{2,1,0:T(8,128)S(1)}, f32[2,24,256]{2,1,0:T(8,128)S(1)}, u32[]{:S(2)}, u32[]{:S(2)}) collective-permute-start(f32[2,24,256]{2,1,0:T(8,128)S(1)} %get-tuple-element.23), channel_id=1, source_target_pairs={{0,3},{1,2},{2,1},{3,0},{4,7},{5,6},{6,5},{7,4},{8,11},{9,10},{10,... | collective-permute-start | bytes 147464 | tf_op jit(solution)/shard_map/ppermute | solution.py:459
  6.6 3.6 %collective-permute-start.1 = (f32[2,24,256]{2,1,0:T(8,128)S(1)}, f32[2,24,256]{2,1,0:T(8,128)S(1)}, u32[]{:S(2)}, u32[]{:S(2)}) collective-permute-start(f32[2,24,256]{2,1,0:T(8,128)S(1)} %get-tuple-element.23), channel_id=1, source_target_pairs={{0,1},{1,0},{2,3},{3,2},{4,5},{5,4},{6,7},{7,6},{8,9},{9,8},{10,11... | collective-permute-start | bytes 147464 | tf_op jit(solution)/shard_map/ppermute | solution.py:459
  10.6 7.6 %collective-permute-start.7 = (f32[2,24,256]{2,1,0:T(8,128)S(1)}, f32[2,24,256]{2,1,0:T(8,128)S(1)}, u32[]{:S(2)}, u32[]{:S(2)}) collective-permute-start(f32[2,24,256]{2,1,0:T(8,128)S(1)} %group_maps.1.refs_4_), channel_id=1, source_target_pairs={{0,25},{1,24},{2,27},{3,26},{4,29},{5,28},{6,31},{7,30},{8,17},{9,... | collective-permute-start | bytes 147464 | tf_op jit(solution)/shard_map/ppermute | solution.py:459
  13.8 4.5 %collective-permute-start.6 = (f32[2,24,256]{2,1,0:T(8,128)S(1)}, f32[2,24,256]{2,1,0:T(8,128)S(1)}, u32[]{:S(2)}, u32[]{:S(2)}) collective-permute-start(f32[2,24,256]{2,1,0:T(8,128)S(1)} %group_maps.1.refs_4_), channel_id=1, source_target_pairs={{0,9},{1,8},{2,11},{3,10},{4,13},{5,12},{6,15},{7,14},{8,1},{9,0},... | collective-permute-start | bytes 147464 | tf_op jit(solution)/shard_map/ppermute | solution.py:459
  13.8 4.7 %collective-permute-start.5 = (f32[2,24,256]{2,1,0:T(8,128)S(1)}, f32[2,24,256]{2,1,0:T(8,128)S(1)}, u32[]{:S(2)}, u32[]{:S(2)}) collective-permute-start(f32[2,24,256]{2,1,0:T(8,128)S(1)} %group_maps.1.refs_4_), channel_id=1, source_target_pairs={{0,17},{1,16},{2,19},{3,18},{4,21},{5,20},{6,23},{7,22},{8,25},{9,... | collective-permute-start | bytes 147464 | tf_op jit(solution)/shard_map/ppermute | solution.py:459

commit v7 on v6

--- a/solution.py
+++ b/solution.py
@@ -277,6 +277,12 @@
     return (2, 1) + tuple(range(3, size)) if first == 2 and size > 2 else tuple(range(1, size))
 
 
+def advance_many(traces, maps):
+    rest = jnp.zeros((8, 256), F32)
+    pairs = [(split(jnp.concatenate([trace, rest], axis=0)), split(one[:FACE])) for trace, one in zip(traces, maps)]
+    return [total[:8] + one[FACE:] for total, one in zip(joined_rows(pairs), maps)]
+
+
 def block_slot(mine, other, size, power, first):
     step = (mine ^ other) if power else (mine - other + size) % size
     return step + 1 * (step == 1) - 1 * (step == 2) if first == 2 and size > 2 else step
@@ -389,16 +395,18 @@
 
     @pl.when(place < size)
     def _():
-        traces = [advance(start_ref[y], ahead_ref[y]) for y in row_range]
+        traces = advance_many([start_ref[y] for y in row_range], [ahead_ref[y] for y in row_range])
+        entering = list(traces)
+        for x in range(planes - 1):
+            traces = advance_many(traces, plane_map(x))
+            entering += traces
+        sums = carried([chosen_ref[x, y] for x in range(planes) for y in row_range], entering, nodes)
         copies = []
         for x in range(planes):
-            sums = carried([chosen_ref[x, y] for y in row_range], traces, nodes)
             for y in row_range:
-                result_ref[x, y] = local_ref[x, y] + sums[y]
+                result_ref[x, y] = local_ref[x, y] + sums[x * rows_y + y]
                 copies.append(pltpu.make_async_copy(result_ref.at[x, y], out_ref.at[x, y], sems.at[x, y]))
                 copies[-1].start()
-            if x < planes - 1:
-                traces = [advance(trace, own) for trace, own in zip(traces, plane_map(x))]
         for copy in copies:
             copy.wait()
 
@@ -430,7 +438,7 @@
             traces = [start_ref[y] for y in range(base_ref.shape[1])]
             for j in range(place):
                 block = blocks[steps.index(place ^ j)]
-                traces = [advance(trace, block[y]) for y, trace in enumerate(traces)]
+                traces = advance_many(traces, [block[y] for y in range(len(traces))])
             write_nodes(result_ref, out_ref, sems, base_ref, part_ref, traces)
 
 

time: 18.7 us -> 18.7 us (level)
  transfers between devices with their start and end apart: 8 -> 8, of which waited for: 3 -> 3; matrix products, arithmetic and copies ran while one was open for 0% -> 0% of each run, Pallas kernels for 24% -> 23%
where the time goes in v7:
time: 18.7 us; the launch traced here: 18.5 us
  starting transfers between devices  8.82 us (47%)
  Pallas kernels  5.55 us (30%)
  waiting for transfers between devices  2.17 us (12%)
  blocking collectives  1.88 us (10%)
    ppermute x8, starting transfers between devices, moved(): return lax.ppermute(value, ('gx', 'gy'), pairs)  8.82 us
    pallas_call x8, Pallas kernels, call(): pl.pallas_call(kernel, out_shape=outs, in_specs=in_specs, out_specs=out_s...  5.55 us
    ppermute x8, waiting for transfers between devices, moved(): return lax.ppermute(value, ('gx', 'gy'), pairs)  2.17 us
    all_gather x1, blocking collectives, on_device(): ahead = lax.all_gather(ahead, 'gy', axis_index_groups=couples)  1.88 us
  transfers between devices with their start and end apart: 8, of which 3 were waited for; matrix products, arithmetic and copies ran while one was open for 0% of the time, Pallas kernels for 23%

profile of v7, /device:TPU:0, one launch (start us, length us, event | category | flops | bytes accessed | tf_op | source)
XLA Modules:
  0.0 18.5 jit_solution(11968006461970496830)
XLA Ops:
  0.0 0.5 %collective-permute-start = (bf16[2,2,64,128]{3,2,1,0:T(8,128)(2,1)}, bf16[2,2,64,128]{3,2,1,0:T(8,128)(2,1)S(1)}, u32[]{:S(2)}, u32[]{:S(2)}) collective-permute-start(bf16[2,2,64,128]{3,2,1,0:T(8,128)(2,1)} %u_ref.1), channel_id=1, source_target_pairs={{0,1},{1,0},{2,3},{3,2},{4,5},{5,4},{6,7},{7,6},{8,9},{9,8},{10,11... | collective-permute-start | bytes 196616 | tf_op jit(solution)/shard_map/ppermute | solution.py:467
  0.5 1.5 %class_matrices.1 = (bf16[80,2048]{1,0:T(8,128)(2,1)S(1)}, bf16[128,256]{1,0:T(8,128)(2,1)S(1)}, bf16[128,128]{1,0:T(8,128)(2,1)S(1)}, f32[12,128]{1,0:T(8,128)S(1)}) custom-call(s32[2,2,16]{2,1,0:T(2,128)} %cls_hbm.1, s32[2,2,2,16]{3,2,1,0:T(2,128)} %flag_hbm.1, f32[8,16,16]{2,1,0:T(8,128)} %x_hbm.1, f32[4,8,16,16]{3,2,1,0:T(8,128)} %lat_hbm.1, ...), custom_call_target="tpu_custom_call" | custom-call | flops 1000000 | bytes 500000 | tf_op jit(solution)/shard_map/class_matrices/pallas_call | solution.py:485
  1.9 0.0 copy-start
  1.9 0.0 collective-permute-done.below_ref.above_ref
  2.0 0.0 copy-start.3
  2.0 0.8 %sources.1 = (bf16[2,2,128,128]{3,2,1,0:T(8,128)(2,1)S(1)}, f32[2,16,256]{2,1,0:T(8,128)S(1)}, f32[2,2,16,256]{3,2,1,0:T(8,128)S(1)}, f32[2,24,256]{2,1,0:T(8,128)S(1)}) custom-call(bf16[2,2,64,128]{3,2,1,0:T(8,128)(2,1)S(1)} %copy-done.1, bf16[2,2,64,128]{3,2,1,0:T(8,128)(2,1)S(1)} %copy-done.2, ...), custom_call_target="tpu_custom_call" | custom-call | flops 1000000 | bytes 500000 | tf_op jit(solution)/shard_map/sources/pallas_call | solution.py:485
  2.8 3.6 %collective-permute-start.4 = (f32[2,24,256]{2,1,0:T(8,128)S(1)}, f32[2,24,256]{2,1,0:T(8,128)S(1)}, u32[]{:S(2)}, u32[]{:S(2)}) collective-permute-start(f32[2,24,256]{2,1,0:T(8,128)S(1)} %get-tuple-element.23), channel_id=1, source_target_pairs={{0,7},{1,6},{2,5},{3,4},{4,3},{5,2},{6,1},{7,0},{8,15},{9,14},{10,... | collective-permute-start | bytes 147464 | tf_op jit(solution)/shard_map/ppermute | solution.py:467
  6.3 0.1 collective-permute-start.3
  6.5 0.1 collective-permute-start.2
  6.6 0.5 %collective-permute-start.1 = (f32[2,24,256]{2,1,0:T(8,128)S(1)}, f32[2,24,256]{2,1,0:T(8,128)S(1)}, u32[]{:S(2)}, u32[]{:S(2)}) collective-permute-start(f32[2,24,256]{2,1,0:T(8,128)S(1)} %get-tuple-element.23), channel_id=1, source_target_pairs={{0,1},{1,0},{2,3},{3,2},{4,5},{5,4},{6,7},{7,6},{8,9},{9,8},{10,11... | collective-permute-start | bytes 147464 | tf_op jit(solution)/shard_map/ppermute | solution.py:467
  7.1 1.3 %local_solve.1 = (f32[2,2,64,128]{3,2,1,0:T(8,128)S(1)}, f32[2,8,256]{2,1,0:T(8,128)S(1)}, bf16[2,2,128,256]{3,2,1,0:T(8,128)(2,1)S(1)}, f32[1,2,8,256]{3,2,1,0:T(8,128)S(1)}) custom-call(bf16[2,2,128,128]{3,2,1,0:T(8,128)(2,1)S(1)} %get-tuple-element.24.data_ref, f32[12,128]{1,0:T(8,128)S(1)} %get-tuple-element.20.label_ref, ...), custom_call_target="tpu_custom_call" | custom-call | flops 1000000 | bytes 500000 | tf_op jit(solution)/shard_map/local_solve/pallas_call | solution.py:485
  8.3 0.1 collective-permute-done.4.refs_3_
  8.5 1.7 %collective-permute-done.3.refs_2_ = f32[2,24,256]{2,1,0:T(8,128)S(1)} collective-permute-done((f32[2,24,256]{2,1,0:T(8,128)S(1)}, f32[2,24,256]{2,1,0:T(8,128)S(1)}, u32[]{:S(2)}, u32[]{:S(2)}) %collective-permute-start.3) | collective-permute-done | bytes 49184 | tf_op jit(solution)/shard_map/ppermute | solution.py:467
  10.2 0.0 collective-permute-done.2.refs_1_
  10.2 0.0 collective-permute-done.1.refs_0_
  10.2 0.4 %group_maps.1.refs_4_ = f32[2,24,256]{2,1,0:T(8,128)S(1)} custom-call(f32[2,24,256]{2,1,0:T(8,128)S(1)} %collective-permute-done.1.refs_0_, f32[2,24,256]{2,1,0:T(8,128)S(1)} %collective-permute-done.2.refs_1_, f32[2,24,256]{2,1,0:T(8,128)S(1)} %collective-permute-done.3.refs_2_, f32[2,24,256]{2,1,0:T(8,128)S(1)} %collective-permute-done.4.refs_3_, ...), custom_call_target="tpu_custom_call" | custom-call | flops 1000000 | bytes 500000 | tf_op jit(solution)/shard_map/group_maps/pallas_call | solution.py:485
  10.6 3.2 %collective-permute-start.7 = (f32[2,24,256]{2,1,0:T(8,128)S(1)}, f32[2,24,256]{2,1,0:T(8,128)S(1)}, u32[]{:S(2)}, u32[]{:S(2)}) collective-permute-start(f32[2,24,256]{2,1,0:T(8,128)S(1)} %group_maps.1.refs_4_), channel_id=1, source_target_pairs={{0,25},{1,24},{2,27},{3,26},{4,29},{5,28},{6,31},{7,30},{8,17},{9,... | collective-permute-start | bytes 147464 | tf_op jit(solution)/shard_map/ppermute | solution.py:467
  13.8 0.0 collective-permute-start.6
  13.8 0.9 %collective-permute-start.5 = (f32[2,24,256]{2,1,0:T(8,128)S(1)}, f32[2,24,256]{2,1,0:T(8,128)S(1)}, u32[]{:S(2)}, u32[]{:S(2)}) collective-permute-start(f32[2,24,256]{2,1,0:T(8,128)S(1)} %group_maps.1.refs_4_), channel_id=1, source_target_pairs={{0,17},{1,16},{2,19},{3,18},{4,21},{5,20},{6,23},{7,22},{8,25},{9,... | collective-permute-start | bytes 147464 | tf_op jit(solution)/shard_map/ppermute | solution.py:467
  14.7 0.3 %maps_ahead.1 = f32[2,24,256]{2,1,0:T(8,128)S(1)} custom-call(f32[2,24,256]{2,1,0:T(8,128)S(1)} %collective-permute-done.1.refs_0_, f32[2,24,256]{2,1,0:T(8,128)S(1)} %collective-permute-done.2.refs_1_, f32[2,24,256]{2,1,0:T(8,128)S(1)} %collective-permute-done.3.refs_2_, f32[2,24,256]{2,1,0:T(8,128)S(1)} %collective-permute-done.4.refs_3_, ...), custom_call_target="tpu_custom_call" | custom-call | flops 1000000 | bytes 500000 | tf_op jit(solution)/shard_map/maps_ahead/pallas_call | solution.py:485
  15.0 1.9 %all-gather = f32[4,24,256]{2,1,0:T(8,128)S(1)} all-gather(f32[2,24,256]{2,1,0:T(8,128)S(1)} %maps_ahead.1), channel_id=2, replica_groups={{0,1},{2,3},{4,5},{6,7},{8,9},{10,11},{12,13},{14,15},{16,17},{18,19},{..., dimensions={0}, use_global_device_ids=true | all-gather | bytes 147456 | tf_op jit(solution)/shard_map/all_gather | solution.py:587
  16.9 1.2 %carry_maps.1 = (f32[2,2,64,128]{3,2,1,0:T(8,128)S(1)}, bf16[2,256,256]{2,1,0:T(8,128)(2,1)S(1)}, f32[2,2,64,128]{3,2,1,0:T(8,128)}) custom-call(f32[2,2,24,256]{3,2,1,0:T(8,128)S(1)} %bitcast.1, f32[2,2,64,128]{3,2,1,0:T(8,128)S(1)} %get-tuple-element.28.local_ref, f32[2,8,256]{2,1,0:T(8,128)S(1)} %get-tuple-element.27.refs_4_.start_ref.refs_2_.refs_3_, ...), custom_call_target="tpu_custom_call" | custom-call | flops 1000000 | bytes 500000 | tf_op jit(solution)/shard_map/carry_maps/pallas_call | solution.py:485
  18.1 0.1 finish_second.1.refs_6_
  18.2 0.3 %collective-permute-done.5.refs_0_ = f32[2,24,256]{2,1,0:T(8,128)S(1)} collective-permute-done((f32[2,24,256]{2,1,0:T(8,128)S(1)}, f32[2,24,256]{2,1,0:T(8,128)S(1)}, u32[]{:S(2)}, u32[]{:S(2)}) %collective-permute-start.5) | collective-permute-done | bytes 49184 | tf_op jit(solution)/shard_map/ppermute | solution.py:467
  (9 shorter events, 0.1 us)
Async XLA Ops:
  0.0 2.0 %copy-start.1 = (bf16[2,2,64,128]{3,2,1,0:T(8,128)(2,1)S(1)}, bf16[2,2,64,128]{3,2,1,0:T(8,128)(2,1)}, u32[]{:S(2)}) copy-start(bf16[2,2,64,128]{3,2,1,0:T(8,128)(2,1)} %u_ref.1) | copy-start | bytes 196612
  0.0 2.0 %copy-start.2 = (bf16[2,2,64,128]{3,2,1,0:T(8,128)(2,1)S(1)}, bf16[2,2,64,128]{3,2,1,0:T(8,128)(2,1)}, u32[]{:S(2)}) copy-start(bf16[2,2,64,128]{3,2,1,0:T(8,128)(2,1)} %rhs_ref.1) | copy-start | bytes 196612
  0.0 1.9 %collective-permute-start = (bf16[2,2,64,128]{3,2,1,0:T(8,128)(2,1)}, bf16[2,2,64,128]{3,2,1,0:T(8,128)(2,1)S(1)}, u32[]{:S(2)}, u32[]{:S(2)}) collective-permute-start(bf16[2,2,64,128]{3,2,1,0:T(8,128)(2,1)} %u_ref.1), channel_id=1, source_target_pairs={{0,1},{1,0},{2,3},{3,2},{4,5},{5,4},{6,7},{7,6},{8,9},{9,8},{10,11... | collective-permute-start | bytes 196616 | tf_op jit(solution)/shard_map/ppermute | solution.py:467
  1.9 5.1 %copy-start = (f32[8,64,64]{2,1,0:T(8,128)S(1)}, f32[8,64,64]{2,1,0:T(8,128)}, u32[]{:S(2)}) copy-start(f32[8,64,64]{2,1,0:T(8,128)} %inv_ref.1) | copy-start | bytes 393220
  2.0 5.1 %copy-start.3 = (f32[2,16,128]{2,1,0:T(8,128)S(1)}, f32[2,16,128]{2,1,0:T(8,128)}, u32[]{:S(2)}) copy-start(f32[2,16,128]{2,1,0:T(8,128)} %inflow_ref.1) | copy-start | bytes 49156
  2.8 5.7 %collective-permute-start.4 = (f32[2,24,256]{2,1,0:T(8,128)S(1)}, f32[2,24,256]{2,1,0:T(8,128)S(1)}, u32[]{:S(2)}, u32[]{:S(2)}) collective-permute-start(f32[2,24,256]{2,1,0:T(8,128)S(1)} %get-tuple-element.23), channel_id=1, source_target_pairs={{0,7},{1,6},{2,5},{3,4},{4,3},{5,2},{6,1},{7,0},{8,15},{9,14},{10,... | collective-permute-start | bytes 147464 | tf_op jit(solution)/shard_map/ppermute | solution.py:467
  6.3 3.8 %collective-permute-start.3 = (f32[2,24,256]{2,1,0:T(8,128)S(1)}, f32[2,24,256]{2,1,0:T(8,128)S(1)}, u32[]{:S(2)}, u32[]{:S(2)}) collective-permute-start(f32[2,24,256]{2,1,0:T(8,128)S(1)} %get-tuple-element.23), channel_id=1, source_target_pairs={{0,5},{1,4},{2,7},{3,6},{4,1},{5,0},{6,3},{7,2},{8,13},{9,12},{10,... | collective-permute-start | bytes 147464 | tf_op jit(solution)/shard_map/ppermute | solution.py:467
  6.5 3.7 %collective-permute-start.2 = (f32[2,24,256]{2,1,0:T(8,128)S(1)}, f32[2,24,256]{2,1,0:T(8,128)S(1)}, u32[]{:S(2)}, u32[]{:S(2)}) collective-permute-start(f32[2,24,256]{2,1,0:T(8,128)S(1)} %get-tuple-element.23), channel_id=1, source_target_pairs={{0,3},{1,2},{2,1},{3,0},{4,7},{5,6},{6,5},{7,4},{8,11},{9,10},{10,... | collective-permute-start | bytes 147464 | tf_op jit(solution)/shard_map/ppermute | solution.py:467
  6.6 3.6 %collective-permute-start.1 = (f32[2,24,256]{2,1,0:T(8,128)S(1)}, f32[2,24,256]{2,1,0:T(8,128)S(1)}, u32[]{:S(2)}, u32[]{:S(2)}) collective-permute-start(f32[2,24,256]{2,1,0:T(8,128)S(1)} %get-tuple-element.23), channel_id=1, source_target_pairs={{0,1},{1,0},{2,3},{3,2},{4,5},{5,4},{6,7},{7,6},{8,9},{9,8},{10,11... | collective-permute-start | bytes 147464 | tf_op jit(solution)/shard_map/ppermute | solution.py:467
  10.6 7.5 %collective-permute-start.7 = (f32[2,24,256]{2,1,0:T(8,128)S(1)}, f32[2,24,256]{2,1,0:T(8,128)S(1)}, u32[]{:S(2)}, u32[]{:S(2)}) collective-permute-start(f32[2,24,256]{2,1,0:T(8,128)S(1)} %group_maps.1.refs_4_), channel_id=1, source_target_pairs={{0,25},{1,24},{2,27},{3,26},{4,29},{5,28},{6,31},{7,30},{8,17},{9,... | collective-permute-start | bytes 147464 | tf_op jit(solution)/shard_map/ppermute | solution.py:467
  13.8 4.4 %collective-permute-start.6 = (f32[2,24,256]{2,1,0:T(8,128)S(1)}, f32[2,24,256]{2,1,0:T(8,128)S(1)}, u32[]{:S(2)}, u32[]{:S(2)}) collective-permute-start(f32[2,24,256]{2,1,0:T(8,128)S(1)} %group_maps.1.refs_4_), channel_id=1, source_target_pairs={{0,9},{1,8},{2,11},{3,10},{4,13},{5,12},{6,15},{7,14},{8,1},{9,0},... | collective-permute-start | bytes 147464 | tf_op jit(solution)/shard_map/ppermute | solution.py:467
  13.8 4.7 %collective-permute-start.5 = (f32[2,24,256]{2,1,0:T(8,128)S(1)}, f32[2,24,256]{2,1,0:T(8,128)S(1)}, u32[]{:S(2)}, u32[]{:S(2)}) collective-permute-start(f32[2,24,256]{2,1,0:T(8,128)S(1)} %group_maps.1.refs_4_), channel_id=1, source_target_pairs={{0,17},{1,16},{2,19},{3,18},{4,21},{5,20},{6,23},{7,22},{8,25},{9,... | collective-permute-start | bytes 147464 | tf_op jit(solution)/shard_map/ppermute | solution.py:467

commit v8 on v7

--- a/solution.py
+++ b/solution.py
@@ -103,7 +103,7 @@
     pairs = ((cls_hbm, cls_ref), (flag_hbm, flag_ref), (x_hbm, x_ref), (lat_hbm, lat_ref))
     pairs += ((inv_hbm.at[:, inv_hbm.shape[1] - FACE:, :], inv_ref),)
     copies = [pltpu.make_async_copy(a, b, sems.at[i]) for i, (a, b) in enumerate(pairs)]
-    for copy in copies:
+    for copy in copies[::-1]:
         copy.start()
     count, nodes, _ = inv_hbm.shape
     planes = cls_ref.shape[0]
@@ -162,7 +162,19 @@
     return jnp.concatenate([first, second, first, rest], axis=0)
 
 
-def sources_kernel(gy_size, u_ref, rhs_ref, below_ref, above_ref, label_ref, out_ref, step_ref, x_ref, flow_ref, lin_ref, map_ref):
+def sources_kernel(gx_size, gy_size, *refs):
+    place = lax.axis_index("gx")
+
+    @pl.when(place < gx_size - 1)
+    def _():
+        gather_sources(gy_size, True, *refs)
+
+    @pl.when(place == gx_size - 1)
+    def _():
+        gather_sources(gy_size, False, *refs)
+
+
+def gather_sources(gy_size, mapped, u_ref, rhs_ref, below_ref, above_ref, label_ref, out_ref, step_ref, x_ref, flow_ref, lin_ref, map_ref):
     planes, rows_y, nodes, columns = u_ref.shape
     place = lax.axis_index("gy")
     node, item = iota((nodes, nodes), 1), iota((nodes, nodes), 0)
@@ -217,7 +229,7 @@
             lin_ref[x, y] = here[y][:FACE] + here[y][FACE:]
         if wholes is None:
             wholes, pairs = [part[:FACE] + part[FACE:] for part in here], both
-        else:
+        elif mapped:
             blocks = [[jnp.concatenate([part] * 16, axis=0) * keep for part in parts] for parts in both]
             stacks = [jnp.concatenate(pair, axis=0) for pair in pairs]
             firsts = [dot(stack, block[0]) for stack, block in zip(stacks, blocks)]
@@ -230,9 +242,12 @@
         label = jnp.concatenate([label_ref[pl.ds(x * rows_y + y, 1), :] for y in range(rows_y)], axis=1)
         flow = class_sum(every[:, begin:begin + rows_y * columns], label, FACE)
         flow_ref[x] = flow
-        if total is not None:
+        if total is not None and (mapped or x < planes - 1):
             flow = flow + class_sum(dot(step_ref[...], stacked(total)), label, FACE)
         total = flow
+    if not mapped:
+        map_ref[...] = jnp.zeros(map_ref.shape, F32)
+        return
     for y in range(rows_y):
         map_ref[y, 0:FACE] = wholes[y]
         map_ref[y, FACE:] = encode(total[:, y * columns:(y + 1) * columns])
@@ -274,7 +289,9 @@
 
 
 def sent_steps(size, first):
-    return (2, 1) + tuple(range(3, size)) if first == 2 and size > 2 else tuple(range(1, size))
+    if first == 2:
+        return (2, 1) + tuple(range(3, size)) if size > 2 else tuple(range(1, size))
+    return (1, 3, 2) + tuple(range(4, size)) if size > 3 else tuple(range(1, size))
 
 
 def advance_many(traces, maps):
@@ -285,7 +302,9 @@
 
 def block_slot(mine, other, size, power, first):
     step = (mine ^ other) if power else (mine - other + size) % size
-    return step + 1 * (step == 1) - 1 * (step == 2) if first == 2 and size > 2 else step
+    if first == 2:
+        return step + 1 * (step == 1) - 1 * (step == 2) if size > 2 else step
+    return step + 1 * (step == 2) - 1 * (step == 3) if size > 3 else step
 
 
 def group_kernel(size, power, outer, *refs):
@@ -532,7 +551,7 @@
         space=pltpu.HBM,
     )
     data, flow, linear, here = call(
-        functools.partial(sources_kernel, gy_size),
+        functools.partial(sources_kernel, gx_size, gy_size),
         (
             shape((planes, rows_y, 128, columns), BF16),
             shape((planes, FACE, rows_y * columns)),

time: 18.7 us -> 18.7 us (level)
  transfers between devices with their start and end apart: 8 -> 8, of which waited for: 3 -> 2; matrix products, arithmetic and copies ran while one was open for 0% -> 0% of each run, Pallas kernels for 23% -> 23%
where the time goes in v8:
time: 18.7 us; the launch traced here: 18.6 us
  starting transfers between devices  8.84 us (47%)
  Pallas kernels  5.54 us (30%)
  waiting for transfers between devices  2.18 us (12%)
  blocking collectives  1.88 us (10%)
    ppermute x8, starting transfers between devices, moved(): return lax.ppermute(value, ('gx', 'gy'), pairs)  8.84 us
    pallas_call x8, Pallas kernels, call(): pl.pallas_call(kernel, out_shape=outs, in_specs=in_specs, out_specs=out_s...  5.54 us
    ppermute x8, waiting for transfers between devices, moved(): return lax.ppermute(value, ('gx', 'gy'), pairs)  2.18 us
    all_gather x1, blocking collectives, on_device(): ahead = lax.all_gather(ahead, 'gy', axis_index_groups=couples)  1.88 us
  transfers between devices with their start and end apart: 8, of which 2 were waited for; matrix products, arithmetic and copies ran while one was open for 0% of the time, Pallas kernels for 23%

profile of v8, /device:TPU:0, one launch (start us, length us, event | category | flops | bytes accessed | tf_op | source)
XLA Modules:
  0.0 18.6 jit_solution(15723639213558875819)
XLA Ops:
  0.0 0.5 %collective-permute-start = (bf16[2,2,64,128]{3,2,1,0:T(8,128)(2,1)}, bf16[2,2,64,128]{3,2,1,0:T(8,128)(2,1)S(1)}, u32[]{:S(2)}, u32[]{:S(2)}) collective-permute-start(bf16[2,2,64,128]{3,2,1,0:T(8,128)(2,1)} %refs_0_.1), channel_id=1, source_target_pairs={{0,1},{1,0},{2,3},{3,2},{4,5},{5,4},{6,7},{7,6},{8,9},{9,8},{10,11... | collective-permute-start | bytes 196616 | tf_op jit(solution)/shard_map/ppermute | solution.py:486
  0.5 1.4 %class_matrices.1 = (bf16[80,2048]{1,0:T(8,128)(2,1)S(1)}, bf16[128,256]{1,0:T(8,128)(2,1)S(1)}, bf16[128,128]{1,0:T(8,128)(2,1)S(1)}, f32[12,128]{1,0:T(8,128)S(1)}) custom-call(s32[2,2,16]{2,1,0:T(2,128)} %cls_hbm.1, s32[2,2,2,16]{3,2,1,0:T(2,128)} %flag_hbm.1, f32[8,16,16]{2,1,0:T(8,128)} %x_hbm.1, f32[4,8,16,16]{3,2,1,0:T(8,128)} %lat_hbm.1, ...), custom_call_target="tpu_custom_call" | custom-call | flops 1000000 | bytes 500000 | tf_op jit(solution)/shard_map/class_matrices/pallas_call | solution.py:504
  1.9 0.0 copy-start
  1.9 0.0 collective-permute-done.refs_2_.refs_3_
  1.9 0.0 copy-start.3
  2.0 0.8 %sources.1 = (bf16[2,2,128,128]{3,2,1,0:T(8,128)(2,1)S(1)}, f32[2,16,256]{2,1,0:T(8,128)S(1)}, f32[2,2,16,256]{3,2,1,0:T(8,128)S(1)}, f32[2,24,256]{2,1,0:T(8,128)S(1)}) custom-call(bf16[2,2,64,128]{3,2,1,0:T(8,128)(2,1)S(1)} %copy-done.1, bf16[2,2,64,128]{3,2,1,0:T(8,128)(2,1)S(1)} %copy-done.2, ...), custom_call_target="tpu_custom_call" | custom-call | flops 1000000 | bytes 500000 | tf_op jit(solution)/shard_map/sources/pallas_call | solution.py:504
  2.7 2.6 %collective-permute-start.4 = (f32[2,24,256]{2,1,0:T(8,128)S(1)}, f32[2,24,256]{2,1,0:T(8,128)S(1)}, u32[]{:S(2)}, u32[]{:S(2)}) collective-permute-start(f32[2,24,256]{2,1,0:T(8,128)S(1)} %get-tuple-element.23), channel_id=1, source_target_pairs={{0,5},{1,4},{2,7},{3,6},{4,1},{5,0},{6,3},{7,2},{8,13},{9,12},{10,... | collective-permute-start | bytes 147464 | tf_op jit(solution)/shard_map/ppermute | solution.py:486
  5.4 1.1 %collective-permute-start.3 = (f32[2,24,256]{2,1,0:T(8,128)S(1)}, f32[2,24,256]{2,1,0:T(8,128)S(1)}, u32[]{:S(2)}, u32[]{:S(2)}) collective-permute-start(f32[2,24,256]{2,1,0:T(8,128)S(1)} %get-tuple-element.23), channel_id=1, source_target_pairs={{0,7},{1,6},{2,5},{3,4},{4,3},{5,2},{6,1},{7,0},{8,15},{9,14},{10,... | collective-permute-start | bytes 147464 | tf_op jit(solution)/shard_map/ppermute | solution.py:486
  6.5 0.1 collective-permute-start.2
  6.5 0.5 %collective-permute-start.1 = (f32[2,24,256]{2,1,0:T(8,128)S(1)}, f32[2,24,256]{2,1,0:T(8,128)S(1)}, u32[]{:S(2)}, u32[]{:S(2)}) collective-permute-start(f32[2,24,256]{2,1,0:T(8,128)S(1)} %get-tuple-element.23), channel_id=1, source_target_pairs={{0,1},{1,0},{2,3},{3,2},{4,5},{5,4},{6,7},{7,6},{8,9},{9,8},{10,11... | collective-permute-start | bytes 147464 | tf_op jit(solution)/shard_map/ppermute | solution.py:486
  7.0 1.3 %local_solve.1 = (f32[2,2,64,128]{3,2,1,0:T(8,128)S(1)}, f32[2,8,256]{2,1,0:T(8,128)S(1)}, bf16[2,2,128,256]{3,2,1,0:T(8,128)(2,1)S(1)}, f32[1,2,8,256]{3,2,1,0:T(8,128)S(1)}) custom-call(bf16[2,2,128,128]{3,2,1,0:T(8,128)(2,1)S(1)} %get-tuple-element.24.data_ref, f32[12,128]{1,0:T(8,128)S(1)} %get-tuple-element.20.refs_4_.label_ref, ...), custom_call_target="tpu_custom_call" | custom-call | flops 1000000 | bytes 500000 | tf_op jit(solution)/shard_map/local_solve/pallas_call | solution.py:504
  8.3 0.0 collective-permute-done.4.refs_3_
  8.3 1.8 %collective-permute-done.3.refs_2_ = f32[2,24,256]{2,1,0:T(8,128)S(1)} collective-permute-done((f32[2,24,256]{2,1,0:T(8,128)S(1)}, f32[2,24,256]{2,1,0:T(8,128)S(1)}, u32[]{:S(2)}, u32[]{:S(2)}) %collective-permute-start.3) | collective-permute-done | bytes 49184 | tf_op jit(solution)/shard_map/ppermute | solution.py:486
  10.1 0.0 collective-permute-done.2.refs_1_
  10.1 0.4 %group_maps.1.refs_4_ = f32[2,24,256]{2,1,0:T(8,128)S(1)} custom-call(f32[2,24,256]{2,1,0:T(8,128)S(1)} %collective-permute-done.1.refs_0_, f32[2,24,256]{2,1,0:T(8,128)S(1)} %collective-permute-done.2.refs_1_, f32[2,24,256]{2,1,0:T(8,128)S(1)} %collective-permute-done.3.refs_2_, f32[2,24,256]{2,1,0:T(8,128)S(1)} %collective-permute-done.4.refs_3_, ...), custom_call_target="tpu_custom_call" | custom-call | flops 1000000 | bytes 500000 | tf_op jit(solution)/shard_map/group_maps/pallas_call | solution.py:504
  10.5 3.2 %collective-permute-start.7 = (f32[2,24,256]{2,1,0:T(8,128)S(1)}, f32[2,24,256]{2,1,0:T(8,128)S(1)}, u32[]{:S(2)}, u32[]{:S(2)}) collective-permute-start(f32[2,24,256]{2,1,0:T(8,128)S(1)} %group_maps.1.refs_4_), channel_id=1, source_target_pairs={{0,25},{1,24},{2,27},{3,26},{4,29},{5,28},{6,31},{7,30},{8,17},{9,... | collective-permute-start | bytes 147464 | tf_op jit(solution)/shard_map/ppermute | solution.py:486
  13.7 0.0 collective-permute-start.6
  13.7 0.9 %collective-permute-start.5 = (f32[2,24,256]{2,1,0:T(8,128)S(1)}, f32[2,24,256]{2,1,0:T(8,128)S(1)}, u32[]{:S(2)}, u32[]{:S(2)}) collective-permute-start(f32[2,24,256]{2,1,0:T(8,128)S(1)} %group_maps.1.refs_4_), channel_id=1, source_target_pairs={{0,17},{1,16},{2,19},{3,18},{4,21},{5,20},{6,23},{7,22},{8,25},{9,... | collective-permute-start | bytes 147464 | tf_op jit(solution)/shard_map/ppermute | solution.py:486
  14.6 0.3 %maps_ahead.1 = f32[2,24,256]{2,1,0:T(8,128)S(1)} custom-call(f32[2,24,256]{2,1,0:T(8,128)S(1)} %collective-permute-done.1.refs_0_, f32[2,24,256]{2,1,0:T(8,128)S(1)} %collective-permute-done.2.refs_1_, f32[2,24,256]{2,1,0:T(8,128)S(1)} %collective-permute-done.3.refs_2_, f32[2,24,256]{2,1,0:T(8,128)S(1)} %collective-permute-done.4.refs_3_, ...), custom_call_target="tpu_custom_call" | custom-call | flops 1000000 | bytes 500000 | tf_op jit(solution)/shard_map/maps_ahead/pallas_call | solution.py:504
  15.0 1.9 %all-gather = f32[4,24,256]{2,1,0:T(8,128)S(1)} all-gather(f32[2,24,256]{2,1,0:T(8,128)S(1)} %maps_ahead.1), channel_id=2, replica_groups={{0,1},{2,3},{4,5},{6,7},{8,9},{10,11},{12,13},{14,15},{16,17},{18,19},{..., dimensions={0}, use_global_device_ids=true | all-gather | bytes 147456 | tf_op jit(solution)/shard_map/all_gather | solution.py:606
  16.9 1.2 %carry_maps.1 = (f32[2,2,64,128]{3,2,1,0:T(8,128)S(1)}, bf16[2,256,256]{2,1,0:T(8,128)(2,1)S(1)}, f32[2,2,64,128]{3,2,1,0:T(8,128)}) custom-call(f32[2,2,24,256]{3,2,1,0:T(8,128)S(1)} %bitcast.1, f32[2,2,64,128]{3,2,1,0:T(8,128)S(1)} %get-tuple-element.28.local_ref, f32[2,8,256]{2,1,0:T(8,128)S(1)} %get-tuple-element.27.refs_4_.start_ref.refs_2_.refs_3_, ...), custom_call_target="tpu_custom_call" | custom-call | flops 1000000 | bytes 500000 | tf_op jit(solution)/shard_map/carry_maps/pallas_call | solution.py:504
  18.1 0.0 collective-permute-done.7.refs_0_.refs_2_
  18.1 0.1 finish_second.1.refs_6_
  18.2 0.3 %collective-permute-done.5.refs_0_ = f32[2,24,256]{2,1,0:T(8,128)S(1)} collective-permute-done((f32[2,24,256]{2,1,0:T(8,128)S(1)}, f32[2,24,256]{2,1,0:T(8,128)S(1)}, u32[]{:S(2)}, u32[]{:S(2)}) %collective-permute-start.5) | collective-permute-done | bytes 49184 | tf_op jit(solution)/shard_map/ppermute | solution.py:486
  (9 shorter events, 0.1 us)
Async XLA Ops:
  0.0 1.9 %copy-start.1 = (bf16[2,2,64,128]{3,2,1,0:T(8,128)(2,1)S(1)}, bf16[2,2,64,128]{3,2,1,0:T(8,128)(2,1)}, u32[]{:S(2)}) copy-start(bf16[2,2,64,128]{3,2,1,0:T(8,128)(2,1)} %refs_0_.1) | copy-start | bytes 196612
  0.0 1.9 %copy-start.2 = (bf16[2,2,64,128]{3,2,1,0:T(8,128)(2,1)S(1)}, bf16[2,2,64,128]{3,2,1,0:T(8,128)(2,1)}, u32[]{:S(2)}) copy-start(bf16[2,2,64,128]{3,2,1,0:T(8,128)(2,1)} %refs_1_.1) | copy-start | bytes 196612
  0.0 1.9 %collective-permute-start = (bf16[2,2,64,128]{3,2,1,0:T(8,128)(2,1)}, bf16[2,2,64,128]{3,2,1,0:T(8,128)(2,1)S(1)}, u32[]{:S(2)}, u32[]{:S(2)}) collective-permute-start(bf16[2,2,64,128]{3,2,1,0:T(8,128)(2,1)} %refs_0_.1), channel_id=1, source_target_pairs={{0,1},{1,0},{2,3},{3,2},{4,5},{5,4},{6,7},{7,6},{8,9},{9,8},{10,11... | collective-permute-start | bytes 196616 | tf_op jit(solution)/shard_map/ppermute | solution.py:486
  1.9 5.1 %copy-start = (f32[8,64,64]{2,1,0:T(8,128)S(1)}, f32[8,64,64]{2,1,0:T(8,128)}, u32[]{:S(2)}) copy-start(f32[8,64,64]{2,1,0:T(8,128)} %inv_ref.1) | copy-start | bytes 393220
  1.9 5.1 %copy-start.3 = (f32[2,16,128]{2,1,0:T(8,128)S(1)}, f32[2,16,128]{2,1,0:T(8,128)}, u32[]{:S(2)}) copy-start(f32[2,16,128]{2,1,0:T(8,128)} %inflow_ref.1) | copy-start | bytes 49156
  2.7 5.5 %collective-permute-start.4 = (f32[2,24,256]{2,1,0:T(8,128)S(1)}, f32[2,24,256]{2,1,0:T(8,128)S(1)}, u32[]{:S(2)}, u32[]{:S(2)}) collective-permute-start(f32[2,24,256]{2,1,0:T(8,128)S(1)} %get-tuple-element.23), channel_id=1, source_target_pairs={{0,5},{1,4},{2,7},{3,6},{4,1},{5,0},{6,3},{7,2},{8,13},{9,12},{10,... | collective-permute-start | bytes 147464 | tf_op jit(solution)/shard_map/ppermute | solution.py:486
  5.4 4.7 %collective-permute-start.3 = (f32[2,24,256]{2,1,0:T(8,128)S(1)}, f32[2,24,256]{2,1,0:T(8,128)S(1)}, u32[]{:S(2)}, u32[]{:S(2)}) collective-permute-start(f32[2,24,256]{2,1,0:T(8,128)S(1)} %get-tuple-element.23), channel_id=1, source_target_pairs={{0,7},{1,6},{2,5},{3,4},{4,3},{5,2},{6,1},{7,0},{8,15},{9,14},{10,... | collective-permute-start | bytes 147464 | tf_op jit(solution)/shard_map/ppermute | solution.py:486
  6.5 3.6 %collective-permute-start.2 = (f32[2,24,256]{2,1,0:T(8,128)S(1)}, f32[2,24,256]{2,1,0:T(8,128)S(1)}, u32[]{:S(2)}, u32[]{:S(2)}) collective-permute-start(f32[2,24,256]{2,1,0:T(8,128)S(1)} %get-tuple-element.23), channel_id=1, source_target_pairs={{0,3},{1,2},{2,1},{3,0},{4,7},{5,6},{6,5},{7,4},{8,11},{9,10},{10,... | collective-permute-start | bytes 147464 | tf_op jit(solution)/shard_map/ppermute | solution.py:486
  6.5 3.6 %collective-permute-start.1 = (f32[2,24,256]{2,1,0:T(8,128)S(1)}, f32[2,24,256]{2,1,0:T(8,128)S(1)}, u32[]{:S(2)}, u32[]{:S(2)}) collective-permute-start(f32[2,24,256]{2,1,0:T(8,128)S(1)} %get-tuple-element.23), channel_id=1, source_target_pairs={{0,1},{1,0},{2,3},{3,2},{4,5},{5,4},{6,7},{7,6},{8,9},{9,8},{10,11... | collective-permute-start | bytes 147464 | tf_op jit(solution)/shard_map/ppermute | solution.py:486
  10.5 7.6 %collective-permute-start.7 = (f32[2,24,256]{2,1,0:T(8,128)S(1)}, f32[2,24,256]{2,1,0:T(8,128)S(1)}, u32[]{:S(2)}, u32[]{:S(2)}) collective-permute-start(f32[2,24,256]{2,1,0:T(8,128)S(1)} %group_maps.1.refs_4_), channel_id=1, source_target_pairs={{0,25},{1,24},{2,27},{3,26},{4,29},{5,28},{6,31},{7,30},{8,17},{9,... | collective-permute-start | bytes 147464 | tf_op jit(solution)/shard_map/ppermute | solution.py:486
  13.7 4.4 %collective-permute-start.6 = (f32[2,24,256]{2,1,0:T(8,128)S(1)}, f32[2,24,256]{2,1,0:T(8,128)S(1)}, u32[]{:S(2)}, u32[]{:S(2)}) collective-permute-start(f32[2,24,256]{2,1,0:T(8,128)S(1)} %group_maps.1.refs_4_), channel_id=1, source_target_pairs={{0,9},{1,8},{2,11},{3,10},{4,13},{5,12},{6,15},{7,14},{8,1},{9,0},... | collective-permute-start | bytes 147464 | tf_op jit(solution)/shard_map/ppermute | solution.py:486
  13.7 4.8 %collective-permute-start.5 = (f32[2,24,256]{2,1,0:T(8,128)S(1)}, f32[2,24,256]{2,1,0:T(8,128)S(1)}, u32[]{:S(2)}, u32[]{:S(2)}) collective-permute-start(f32[2,24,256]{2,1,0:T(8,128)S(1)} %group_maps.1.refs_4_), channel_id=1, source_target_pairs={{0,17},{1,16},{2,19},{3,18},{4,21},{5,20},{6,23},{7,22},{8,25},{9,... | collective-permute-start | bytes 147464 | tf_op jit(solution)/shard_map/ppermute | solution.py:486

commit v9 on v7

--- a/solution.py
+++ b/solution.py
@@ -168,7 +168,12 @@
     node, item = iota((nodes, nodes), 1), iota((nodes, nodes), 0)
     chosen = (node == wanted_node(item // FACE, item % FACE)).astype(BF16)
     own = [u_ref[x, y] for x in range(planes) for y in range(rows_y)]
-    other = [below_ref[x, below_ref.shape[1] - 1] for x in range(planes)] + [above_ref[x, 0] for x in range(planes)]
+    pair = gy_size == 2
+    if pair:
+        row = jnp.where(place > 0, below_ref.shape[1] - 1, 0)
+        other = [below_ref[x, row] for x in range(planes)]
+    else:
+        other = [below_ref[x, below_ref.shape[1] - 1] for x in range(planes)] + [above_ref[x, 0] for x in range(planes)]
     step = step_ref[...]
     row, lane = iota((2 * FACE, 128), 0), iota((2 * FACE, 128), 1)
     flip = (lane == row + FACE * (row >= FACE)).astype(BF16)
@@ -185,7 +190,7 @@
     data = []
     for x in range(planes):
         under = faces[len(own) + x][16:32] * has_below
-        over = faces[len(own) + planes + x][0:16] * has_above
+        over = faces[len(own) + (0 if pair else planes) + x][0:16] * has_above
         for y in range(rows_y):
             at = x * rows_y + y
             y_flag = label_ref[pl.ds(planes * rows_y + at, 1), :]

time: 18.7 us -> 18.7 us (level)
  no operation moved by 1% of the time
where the time goes in v9:
time: 18.7 us; the launch traced here: 18.5 us
  starting transfers between devices  8.82 us (47%)
  Pallas kernels  5.53 us (30%)
  waiting for transfers between devices  2.17 us (12%)
  blocking collectives  1.88 us (10%)
    ppermute x8, starting transfers between devices, moved(): return lax.ppermute(value, ('gx', 'gy'), pairs)  8.82 us
    pallas_call x8, Pallas kernels, call(): pl.pallas_call(kernel, out_shape=outs, in_specs=in_specs, out_specs=out_s...  5.53 us
    ppermute x8, waiting for transfers between devices, moved(): return lax.ppermute(value, ('gx', 'gy'), pairs)  2.17 us
    all_gather x1, blocking collectives, on_device(): ahead = lax.all_gather(ahead, 'gy', axis_index_groups=couples)  1.88 us
  transfers between devices with their start and end apart: 8, of which 3 were waited for; matrix products, arithmetic and copies ran while one was open for 0% of the time, Pallas kernels for 23%

profile of v9, /device:TPU:0, one launch (start us, length us, event | category | flops | bytes accessed | tf_op | source)
XLA Modules:
  0.0 18.5 jit_solution(8791959160048160195)
XLA Ops:
  0.0 0.5 %collective-permute-start = (bf16[2,2,64,128]{3,2,1,0:T(8,128)(2,1)}, bf16[2,2,64,128]{3,2,1,0:T(8,128)(2,1)S(1)}, u32[]{:S(2)}, u32[]{:S(2)}) collective-permute-start(bf16[2,2,64,128]{3,2,1,0:T(8,128)(2,1)} %u_ref.1), channel_id=1, source_target_pairs={{0,1},{1,0},{2,3},{3,2},{4,5},{5,4},{6,7},{7,6},{8,9},{9,8},{10,11... | collective-permute-start | bytes 196616 | tf_op jit(solution)/shard_map/ppermute | solution.py:472
  0.5 1.5 %class_matrices.1 = (bf16[80,2048]{1,0:T(8,128)(2,1)S(1)}, bf16[128,256]{1,0:T(8,128)(2,1)S(1)}, bf16[128,128]{1,0:T(8,128)(2,1)S(1)}, f32[12,128]{1,0:T(8,128)S(1)}) custom-call(s32[2,2,16]{2,1,0:T(2,128)} %cls_hbm.1, s32[2,2,2,16]{3,2,1,0:T(2,128)} %flag_hbm.1, f32[8,16,16]{2,1,0:T(8,128)} %x_hbm.1, f32[4,8,16,16]{3,2,1,0:T(8,128)} %lat_hbm.1, ...), custom_call_target="tpu_custom_call" | custom-call | flops 1000000 | bytes 500000 | tf_op jit(solution)/shard_map/class_matrices/pallas_call | solution.py:490
  1.9 0.0 copy-start
  1.9 0.0 collective-permute-done.below_ref.above_ref
  2.0 0.0 copy-start.3
  2.0 0.7 %sources.1 = (bf16[2,2,128,128]{3,2,1,0:T(8,128)(2,1)S(1)}, f32[2,16,256]{2,1,0:T(8,128)S(1)}, f32[2,2,16,256]{3,2,1,0:T(8,128)S(1)}, f32[2,24,256]{2,1,0:T(8,128)S(1)}) custom-call(bf16[2,2,64,128]{3,2,1,0:T(8,128)(2,1)S(1)} %copy-done.1, bf16[2,2,64,128]{3,2,1,0:T(8,128)(2,1)S(1)} %copy-done.2, ...), custom_call_target="tpu_custom_call" | custom-call | flops 1000000 | bytes 500000 | tf_op jit(solution)/shard_map/sources/pallas_call | solution.py:490
  2.7 3.6 %collective-permute-start.4 = (f32[2,24,256]{2,1,0:T(8,128)S(1)}, f32[2,24,256]{2,1,0:T(8,128)S(1)}, u32[]{:S(2)}, u32[]{:S(2)}) collective-permute-start(f32[2,24,256]{2,1,0:T(8,128)S(1)} %get-tuple-element.23), channel_id=1, source_target_pairs={{0,7},{1,6},{2,5},{3,4},{4,3},{5,2},{6,1},{7,0},{8,15},{9,14},{10,... | collective-permute-start | bytes 147464 | tf_op jit(solution)/shard_map/ppermute | solution.py:472
  6.3 0.2 collective-permute-start.3
  6.5 0.1 collective-permute-start.2
  6.5 0.5 %collective-permute-start.1 = (f32[2,24,256]{2,1,0:T(8,128)S(1)}, f32[2,24,256]{2,1,0:T(8,128)S(1)}, u32[]{:S(2)}, u32[]{:S(2)}) collective-permute-start(f32[2,24,256]{2,1,0:T(8,128)S(1)} %get-tuple-element.23), channel_id=1, source_target_pairs={{0,1},{1,0},{2,3},{3,2},{4,5},{5,4},{6,7},{7,6},{8,9},{9,8},{10,11... | collective-permute-start | bytes 147464 | tf_op jit(solution)/shard_map/ppermute | solution.py:472
  7.0 1.3 %local_solve.1 = (f32[2,2,64,128]{3,2,1,0:T(8,128)S(1)}, f32[2,8,256]{2,1,0:T(8,128)S(1)}, bf16[2,2,128,256]{3,2,1,0:T(8,128)(2,1)S(1)}, f32[1,2,8,256]{3,2,1,0:T(8,128)S(1)}) custom-call(bf16[2,2,128,128]{3,2,1,0:T(8,128)(2,1)S(1)} %get-tuple-element.24.data_ref, f32[12,128]{1,0:T(8,128)S(1)} %get-tuple-element.20.label_ref, ...), custom_call_target="tpu_custom_call" | custom-call | flops 1000000 | bytes 500000 | tf_op jit(solution)/shard_map/local_solve/pallas_call | solution.py:490
  8.3 0.1 collective-permute-done.4.refs_3_
  8.4 1.7 %collective-permute-done.3.refs_2_ = f32[2,24,256]{2,1,0:T(8,128)S(1)} collective-permute-done((f32[2,24,256]{2,1,0:T(8,128)S(1)}, f32[2,24,256]{2,1,0:T(8,128)S(1)}, u32[]{:S(2)}, u32[]{:S(2)}) %collective-permute-start.3) | collective-permute-done | bytes 49184 | tf_op jit(solution)/shard_map/ppermute | solution.py:472
  10.1 0.0 collective-permute-done.2.refs_1_
  10.1 0.0 collective-permute-done.1.refs_0_
  10.1 0.4 %group_maps.1.refs_4_ = f32[2,24,256]{2,1,0:T(8,128)S(1)} custom-call(f32[2,24,256]{2,1,0:T(8,128)S(1)} %collective-permute-done.1.refs_0_, f32[2,24,256]{2,1,0:T(8,128)S(1)} %collective-permute-done.2.refs_1_, f32[2,24,256]{2,1,0:T(8,128)S(1)} %collective-permute-done.3.refs_2_, f32[2,24,256]{2,1,0:T(8,128)S(1)} %collective-permute-done.4.refs_3_, ...), custom_call_target="tpu_custom_call" | custom-call | flops 1000000 | bytes 500000 | tf_op jit(solution)/shard_map/group_maps/pallas_call | solution.py:490
  10.6 3.2 %collective-permute-start.7 = (f32[2,24,256]{2,1,0:T(8,128)S(1)}, f32[2,24,256]{2,1,0:T(8,128)S(1)}, u32[]{:S(2)}, u32[]{:S(2)}) collective-permute-start(f32[2,24,256]{2,1,0:T(8,128)S(1)} %group_maps.1.refs_4_), channel_id=1, source_target_pairs={{0,25},{1,24},{2,27},{3,26},{4,29},{5,28},{6,31},{7,30},{8,17},{9,... | collective-permute-start | bytes 147464 | tf_op jit(solution)/shard_map/ppermute | solution.py:472
  13.7 0.9 %collective-permute-start.5 = (f32[2,24,256]{2,1,0:T(8,128)S(1)}, f32[2,24,256]{2,1,0:T(8,128)S(1)}, u32[]{:S(2)}, u32[]{:S(2)}) collective-permute-start(f32[2,24,256]{2,1,0:T(8,128)S(1)} %group_maps.1.refs_4_), channel_id=1, source_target_pairs={{0,17},{1,16},{2,19},{3,18},{4,21},{5,20},{6,23},{7,22},{8,25},{9,... | collective-permute-start | bytes 147464 | tf_op jit(solution)/shard_map/ppermute | solution.py:472
  14.6 0.3 %maps_ahead.1 = f32[2,24,256]{2,1,0:T(8,128)S(1)} custom-call(f32[2,24,256]{2,1,0:T(8,128)S(1)} %collective-permute-done.1.refs_0_, f32[2,24,256]{2,1,0:T(8,128)S(1)} %collective-permute-done.2.refs_1_, f32[2,24,256]{2,1,0:T(8,128)S(1)} %collective-permute-done.3.refs_2_, f32[2,24,256]{2,1,0:T(8,128)S(1)} %collective-permute-done.4.refs_3_, ...), custom_call_target="tpu_custom_call" | custom-call | flops 1000000 | bytes 500000 | tf_op jit(solution)/shard_map/maps_ahead/pallas_call | solution.py:490
  15.0 1.9 %all-gather = f32[4,24,256]{2,1,0:T(8,128)S(1)} all-gather(f32[2,24,256]{2,1,0:T(8,128)S(1)} %maps_ahead.1), channel_id=2, replica_groups={{0,1},{2,3},{4,5},{6,7},{8,9},{10,11},{12,13},{14,15},{16,17},{18,19},{..., dimensions={0}, use_global_device_ids=true | all-gather | bytes 147456 | tf_op jit(solution)/shard_map/all_gather | solution.py:592
  16.9 1.2 %carry_maps.1 = (f32[2,2,64,128]{3,2,1,0:T(8,128)S(1)}, bf16[2,256,256]{2,1,0:T(8,128)(2,1)S(1)}, f32[2,2,64,128]{3,2,1,0:T(8,128)}) custom-call(f32[2,2,24,256]{3,2,1,0:T(8,128)S(1)} %bitcast.1, f32[2,2,64,128]{3,2,1,0:T(8,128)S(1)} %get-tuple-element.28.local_ref, f32[2,8,256]{2,1,0:T(8,128)S(1)} %get-tuple-element.27.refs_4_.start_ref.refs_2_.refs_3_, ...), custom_call_target="tpu_custom_call" | custom-call | flops 1000000 | bytes 500000 | tf_op jit(solution)/shard_map/carry_maps/pallas_call | solution.py:490
  18.1 0.0 collective-permute-done.6.refs_1_
  18.1 0.1 finish_second.1.refs_6_
  18.2 0.3 %collective-permute-done.5.refs_0_ = f32[2,24,256]{2,1,0:T(8,128)S(1)} collective-permute-done((f32[2,24,256]{2,1,0:T(8,128)S(1)}, f32[2,24,256]{2,1,0:T(8,128)S(1)}, u32[]{:S(2)}, u32[]{:S(2)}) %collective-permute-start.5) | collective-permute-done | bytes 49184 | tf_op jit(solution)/shard_map/ppermute | solution.py:472
  (9 shorter events, 0.1 us)
Async XLA Ops:
  0.0 2.0 %copy-start.1 = (bf16[2,2,64,128]{3,2,1,0:T(8,128)(2,1)S(1)}, bf16[2,2,64,128]{3,2,1,0:T(8,128)(2,1)}, u32[]{:S(2)}) copy-start(bf16[2,2,64,128]{3,2,1,0:T(8,128)(2,1)} %u_ref.1) | copy-start | bytes 196612
  0.0 2.0 %copy-start.2 = (bf16[2,2,64,128]{3,2,1,0:T(8,128)(2,1)S(1)}, bf16[2,2,64,128]{3,2,1,0:T(8,128)(2,1)}, u32[]{:S(2)}) copy-start(bf16[2,2,64,128]{3,2,1,0:T(8,128)(2,1)} %rhs_ref.1) | copy-start | bytes 196612
  0.0 1.9 %collective-permute-start = (bf16[2,2,64,128]{3,2,1,0:T(8,128)(2,1)}, bf16[2,2,64,128]{3,2,1,0:T(8,128)(2,1)S(1)}, u32[]{:S(2)}, u32[]{:S(2)}) collective-permute-start(bf16[2,2,64,128]{3,2,1,0:T(8,128)(2,1)} %u_ref.1), channel_id=1, source_target_pairs={{0,1},{1,0},{2,3},{3,2},{4,5},{5,4},{6,7},{7,6},{8,9},{9,8},{10,11... | collective-permute-start | bytes 196616 | tf_op jit(solution)/shard_map/ppermute | solution.py:472
  1.9 5.1 %copy-start = (f32[8,64,64]{2,1,0:T(8,128)S(1)}, f32[8,64,64]{2,1,0:T(8,128)}, u32[]{:S(2)}) copy-start(f32[8,64,64]{2,1,0:T(8,128)} %inv_ref.1) | copy-start | bytes 393220
  2.0 5.0 %copy-start.3 = (f32[2,16,128]{2,1,0:T(8,128)S(1)}, f32[2,16,128]{2,1,0:T(8,128)}, u32[]{:S(2)}) copy-start(f32[2,16,128]{2,1,0:T(8,128)} %inflow_ref.1) | copy-start | bytes 49156
  2.7 5.7 %collective-permute-start.4 = (f32[2,24,256]{2,1,0:T(8,128)S(1)}, f32[2,24,256]{2,1,0:T(8,128)S(1)}, u32[]{:S(2)}, u32[]{:S(2)}) collective-permute-start(f32[2,24,256]{2,1,0:T(8,128)S(1)} %get-tuple-element.23), channel_id=1, source_target_pairs={{0,7},{1,6},{2,5},{3,4},{4,3},{5,2},{6,1},{7,0},{8,15},{9,14},{10,... | collective-permute-start | bytes 147464 | tf_op jit(solution)/shard_map/ppermute | solution.py:472
  6.3 3.8 %collective-permute-start.3 = (f32[2,24,256]{2,1,0:T(8,128)S(1)}, f32[2,24,256]{2,1,0:T(8,128)S(1)}, u32[]{:S(2)}, u32[]{:S(2)}) collective-permute-start(f32[2,24,256]{2,1,0:T(8,128)S(1)} %get-tuple-element.23), channel_id=1, source_target_pairs={{0,5},{1,4},{2,7},{3,6},{4,1},{5,0},{6,3},{7,2},{8,13},{9,12},{10,... | collective-permute-start | bytes 147464 | tf_op jit(solution)/shard_map/ppermute | solution.py:472
  6.5 3.7 %collective-permute-start.2 = (f32[2,24,256]{2,1,0:T(8,128)S(1)}, f32[2,24,256]{2,1,0:T(8,128)S(1)}, u32[]{:S(2)}, u32[]{:S(2)}) collective-permute-start(f32[2,24,256]{2,1,0:T(8,128)S(1)} %get-tuple-element.23), channel_id=1, source_target_pairs={{0,3},{1,2},{2,1},{3,0},{4,7},{5,6},{6,5},{7,4},{8,11},{9,10},{10,... | collective-permute-start | bytes 147464 | tf_op jit(solution)/shard_map/ppermute | solution.py:472
  6.5 3.6 %collective-permute-start.1 = (f32[2,24,256]{2,1,0:T(8,128)S(1)}, f32[2,24,256]{2,1,0:T(8,128)S(1)}, u32[]{:S(2)}, u32[]{:S(2)}) collective-permute-start(f32[2,24,256]{2,1,0:T(8,128)S(1)} %get-tuple-element.23), channel_id=1, source_target_pairs={{0,1},{1,0},{2,3},{3,2},{4,5},{5,4},{6,7},{7,6},{8,9},{9,8},{10,11... | collective-permute-start | bytes 147464 | tf_op jit(solution)/shard_map/ppermute | solution.py:472
  10.6 7.5 %collective-permute-start.7 = (f32[2,24,256]{2,1,0:T(8,128)S(1)}, f32[2,24,256]{2,1,0:T(8,128)S(1)}, u32[]{:S(2)}, u32[]{:S(2)}) collective-permute-start(f32[2,24,256]{2,1,0:T(8,128)S(1)} %group_maps.1.refs_4_), channel_id=1, source_target_pairs={{0,25},{1,24},{2,27},{3,26},{4,29},{5,28},{6,31},{7,30},{8,17},{9,... | collective-permute-start | bytes 147464 | tf_op jit(solution)/shard_map/ppermute | solution.py:472
  13.7 4.4 %collective-permute-start.6 = (f32[2,24,256]{2,1,0:T(8,128)S(1)}, f32[2,24,256]{2,1,0:T(8,128)S(1)}, u32[]{:S(2)}, u32[]{:S(2)}) collective-permute-start(f32[2,24,256]{2,1,0:T(8,128)S(1)} %group_maps.1.refs_4_), channel_id=1, source_target_pairs={{0,9},{1,8},{2,11},{3,10},{4,13},{5,12},{6,15},{7,14},{8,1},{9,0},... | collective-permute-start | bytes 147464 | tf_op jit(solution)/shard_map/ppermute | solution.py:472
  13.7 4.7 %collective-permute-start.5 = (f32[2,24,256]{2,1,0:T(8,128)S(1)}, f32[2,24,256]{2,1,0:T(8,128)S(1)}, u32[]{:S(2)}, u32[]{:S(2)}) collective-permute-start(f32[2,24,256]{2,1,0:T(8,128)S(1)} %group_maps.1.refs_4_), channel_id=1, source_target_pairs={{0,17},{1,16},{2,19},{3,18},{4,21},{5,20},{6,23},{7,22},{8,25},{9,... | collective-permute-start | bytes 147464 | tf_op jit(solution)/shard_map/ppermute | solution.py:472

commit v10 on v9

--- a/solution.py
+++ b/solution.py
@@ -103,7 +103,7 @@
     pairs = ((cls_hbm, cls_ref), (flag_hbm, flag_ref), (x_hbm, x_ref), (lat_hbm, lat_ref))
     pairs += ((inv_hbm.at[:, inv_hbm.shape[1] - FACE:, :], inv_ref),)
     copies = [pltpu.make_async_copy(a, b, sems.at[i]) for i, (a, b) in enumerate(pairs)]
-    for copy in copies:
+    for copy in copies[::-1]:
         copy.start()
     count, nodes, _ = inv_hbm.shape
     planes = cls_ref.shape[0]
@@ -279,7 +279,9 @@
 
 
 def sent_steps(size, first):
-    return (2, 1) + tuple(range(3, size)) if first == 2 and size > 2 else tuple(range(1, size))
+    if first == 2:
+        return (2, 1) + tuple(range(3, size)) if size > 2 else tuple(range(1, size))
+    return (1, 3, 2) + tuple(range(4, size)) if size > 3 else tuple(range(1, size))
 
 
 def advance_many(traces, maps):
@@ -290,7 +292,9 @@
 
 def block_slot(mine, other, size, power, first):
     step = (mine ^ other) if power else (mine - other + size) % size
-    return step + 1 * (step == 1) - 1 * (step == 2) if first == 2 and size > 2 else step
+    if first == 2:
+        return step + 1 * (step == 1) - 1 * (step == 2) if size > 2 else step
+    return step + 1 * (step == 2) - 1 * (step == 3) if size > 3 else step
 
 
 def group_kernel(size, power, outer, *refs):

time: 18.7 us -> 18.6 us (level)
  transfers between devices with their start and end apart: 8 -> 8, of which waited for: 3 -> 2; matrix products, arithmetic and copies ran while one was open for 0% -> 0% of each run, Pallas kernels for 23% -> 23%
where the time goes in v10:
time: 18.6 us; the launch traced here: 18.4 us
  starting transfers between devices  8.84 us (48%)
  Pallas kernels  5.49 us (30%)
  waiting for transfers between devices  2.09 us (11%)
  blocking collectives  1.88 us (10%)
    ppermute x8, starting transfers between devices, moved(): return lax.ppermute(value, ('gx', 'gy'), pairs)  8.84 us
    pallas_call x8, Pallas kernels, call(): pl.pallas_call(kernel, out_shape=outs, in_specs=in_specs, out_specs=out_s...  5.49 us
    ppermute x8, waiting for transfers between devices, moved(): return lax.ppermute(value, ('gx', 'gy'), pairs)  2.09 us
    all_gather x1, blocking collectives, on_device(): ahead = lax.all_gather(ahead, 'gy', axis_index_groups=couples)  1.88 us
  transfers between devices with their start and end apart: 8, of which 2 were waited for; matrix products, arithmetic and copies ran while one was open for 0% of the time, Pallas kernels for 23%

profile of v10, /device:TPU:0, one launch (start us, length us, event | category | flops | bytes accessed | tf_op | source)
XLA Modules:
  0.0 18.4 jit_solution(8183904792135060369)
XLA Ops:
  0.0 0.5 %collective-permute-start = (bf16[2,2,64,128]{3,2,1,0:T(8,128)(2,1)}, bf16[2,2,64,128]{3,2,1,0:T(8,128)(2,1)S(1)}, u32[]{:S(2)}, u32[]{:S(2)}) collective-permute-start(bf16[2,2,64,128]{3,2,1,0:T(8,128)(2,1)} %u_ref.1), channel_id=1, source_target_pairs={{0,1},{1,0},{2,3},{3,2},{4,5},{5,4},{6,7},{7,6},{8,9},{9,8},{10,11... | collective-permute-start | bytes 196616 | tf_op jit(solution)/shard_map/ppermute | solution.py:476
  0.5 1.4 %class_matrices.1 = (bf16[80,2048]{1,0:T(8,128)(2,1)S(1)}, bf16[128,256]{1,0:T(8,128)(2,1)S(1)}, bf16[128,128]{1,0:T(8,128)(2,1)S(1)}, f32[12,128]{1,0:T(8,128)S(1)}) custom-call(s32[2,2,16]{2,1,0:T(2,128)} %cls_hbm.1, s32[2,2,2,16]{3,2,1,0:T(2,128)} %flag_hbm.1, f32[8,16,16]{2,1,0:T(8,128)} %x_hbm.1, f32[4,8,16,16]{3,2,1,0:T(8,128)} %lat_hbm.1, ...), custom_call_target="tpu_custom_call" | custom-call | flops 1000000 | bytes 500000 | tf_op jit(solution)/shard_map/class_matrices/pallas_call | solution.py:494
  1.9 0.0 copy-start
  1.9 0.0 collective-permute-done.below_ref.above_ref
  1.9 0.0 copy-start.3
  2.0 0.7 %sources.1 = (bf16[2,2,128,128]{3,2,1,0:T(8,128)(2,1)S(1)}, f32[2,16,256]{2,1,0:T(8,128)S(1)}, f32[2,2,16,256]{3,2,1,0:T(8,128)S(1)}, f32[2,24,256]{2,1,0:T(8,128)S(1)}) custom-call(bf16[2,2,64,128]{3,2,1,0:T(8,128)(2,1)S(1)} %copy-done.1, bf16[2,2,64,128]{3,2,1,0:T(8,128)(2,1)S(1)} %copy-done.2, ...), custom_call_target="tpu_custom_call" | custom-call | flops 1000000 | bytes 500000 | tf_op jit(solution)/shard_map/sources/pallas_call | solution.py:494
  2.7 2.6 %collective-permute-start.4 = (f32[2,24,256]{2,1,0:T(8,128)S(1)}, f32[2,24,256]{2,1,0:T(8,128)S(1)}, u32[]{:S(2)}, u32[]{:S(2)}) collective-permute-start(f32[2,24,256]{2,1,0:T(8,128)S(1)} %get-tuple-element.23), channel_id=1, source_target_pairs={{0,5},{1,4},{2,7},{3,6},{4,1},{5,0},{6,3},{7,2},{8,13},{9,12},{10,... | collective-permute-start | bytes 147464 | tf_op jit(solution)/shard_map/ppermute | solution.py:476
  5.4 1.1 %collective-permute-start.3 = (f32[2,24,256]{2,1,0:T(8,128)S(1)}, f32[2,24,256]{2,1,0:T(8,128)S(1)}, u32[]{:S(2)}, u32[]{:S(2)}) collective-permute-start(f32[2,24,256]{2,1,0:T(8,128)S(1)} %get-tuple-element.23), channel_id=1, source_target_pairs={{0,7},{1,6},{2,5},{3,4},{4,3},{5,2},{6,1},{7,0},{8,15},{9,14},{10,... | collective-permute-start | bytes 147464 | tf_op jit(solution)/shard_map/ppermute | solution.py:476
  6.4 0.1 collective-permute-start.2
  6.5 0.5 %collective-permute-start.1 = (f32[2,24,256]{2,1,0:T(8,128)S(1)}, f32[2,24,256]{2,1,0:T(8,128)S(1)}, u32[]{:S(2)}, u32[]{:S(2)}) collective-permute-start(f32[2,24,256]{2,1,0:T(8,128)S(1)} %get-tuple-element.23), channel_id=1, source_target_pairs={{0,1},{1,0},{2,3},{3,2},{4,5},{5,4},{6,7},{7,6},{8,9},{9,8},{10,11... | collective-permute-start | bytes 147464 | tf_op jit(solution)/shard_map/ppermute | solution.py:476
  7.0 1.3 %local_solve.1 = (f32[2,2,64,128]{3,2,1,0:T(8,128)S(1)}, f32[2,8,256]{2,1,0:T(8,128)S(1)}, bf16[2,2,128,256]{3,2,1,0:T(8,128)(2,1)S(1)}, f32[1,2,8,256]{3,2,1,0:T(8,128)S(1)}) custom-call(bf16[2,2,128,128]{3,2,1,0:T(8,128)(2,1)S(1)} %get-tuple-element.24.data_ref, f32[12,128]{1,0:T(8,128)S(1)} %get-tuple-element.20.label_ref, ...), custom_call_target="tpu_custom_call" | custom-call | flops 1000000 | bytes 500000 | tf_op jit(solution)/shard_map/local_solve/pallas_call | solution.py:494
  8.2 0.0 collective-permute-done.4.refs_3_
  8.2 1.8 %collective-permute-done.3.refs_2_ = f32[2,24,256]{2,1,0:T(8,128)S(1)} collective-permute-done((f32[2,24,256]{2,1,0:T(8,128)S(1)}, f32[2,24,256]{2,1,0:T(8,128)S(1)}, u32[]{:S(2)}, u32[]{:S(2)}) %collective-permute-start.3) | collective-permute-done | bytes 49184 | tf_op jit(solution)/shard_map/ppermute | solution.py:476
  10.1 0.0 collective-permute-done.2.refs_1_
  10.1 0.0 collective-permute-done.1.refs_0_
  10.1 0.4 %group_maps.1.refs_4_ = f32[2,24,256]{2,1,0:T(8,128)S(1)} custom-call(f32[2,24,256]{2,1,0:T(8,128)S(1)} %collective-permute-done.1.refs_0_, f32[2,24,256]{2,1,0:T(8,128)S(1)} %collective-permute-done.2.refs_1_, f32[2,24,256]{2,1,0:T(8,128)S(1)} %collective-permute-done.3.refs_2_, f32[2,24,256]{2,1,0:T(8,128)S(1)} %collective-permute-done.4.refs_3_, ...), custom_call_target="tpu_custom_call" | custom-call | flops 1000000 | bytes 500000 | tf_op jit(solution)/shard_map/group_maps/pallas_call | solution.py:494
  10.5 3.2 %collective-permute-start.7 = (f32[2,24,256]{2,1,0:T(8,128)S(1)}, f32[2,24,256]{2,1,0:T(8,128)S(1)}, u32[]{:S(2)}, u32[]{:S(2)}) collective-permute-start(f32[2,24,256]{2,1,0:T(8,128)S(1)} %group_maps.1.refs_4_), channel_id=1, source_target_pairs={{0,25},{1,24},{2,27},{3,26},{4,29},{5,28},{6,31},{7,30},{8,17},{9,... | collective-permute-start | bytes 147464 | tf_op jit(solution)/shard_map/ppermute | solution.py:476
  13.7 0.0 collective-permute-start.6
  13.7 0.9 %collective-permute-start.5 = (f32[2,24,256]{2,1,0:T(8,128)S(1)}, f32[2,24,256]{2,1,0:T(8,128)S(1)}, u32[]{:S(2)}, u32[]{:S(2)}) collective-permute-start(f32[2,24,256]{2,1,0:T(8,128)S(1)} %group_maps.1.refs_4_), channel_id=1, source_target_pairs={{0,17},{1,16},{2,19},{3,18},{4,21},{5,20},{6,23},{7,22},{8,25},{9,... | collective-permute-start | bytes 147464 | tf_op jit(solution)/shard_map/ppermute | solution.py:476
  14.6 0.3 %maps_ahead.1 = f32[2,24,256]{2,1,0:T(8,128)S(1)} custom-call(f32[2,24,256]{2,1,0:T(8,128)S(1)} %collective-permute-done.1.refs_0_, f32[2,24,256]{2,1,0:T(8,128)S(1)} %collective-permute-done.2.refs_1_, f32[2,24,256]{2,1,0:T(8,128)S(1)} %collective-permute-done.3.refs_2_, f32[2,24,256]{2,1,0:T(8,128)S(1)} %collective-permute-done.4.refs_3_, ...), custom_call_target="tpu_custom_call" | custom-call | flops 1000000 | bytes 500000 | tf_op jit(solution)/shard_map/maps_ahead/pallas_call | solution.py:494
  15.0 1.9 %all-gather = f32[4,24,256]{2,1,0:T(8,128)S(1)} all-gather(f32[2,24,256]{2,1,0:T(8,128)S(1)} %maps_ahead.1), channel_id=2, replica_groups={{0,1},{2,3},{4,5},{6,7},{8,9},{10,11},{12,13},{14,15},{16,17},{18,19},{..., dimensions={0}, use_global_device_ids=true | all-gather | bytes 147456 | tf_op jit(solution)/shard_map/all_gather | solution.py:596
  16.8 1.2 %carry_maps.1 = (f32[2,2,64,128]{3,2,1,0:T(8,128)S(1)}, bf16[2,256,256]{2,1,0:T(8,128)(2,1)S(1)}, f32[2,2,64,128]{3,2,1,0:T(8,128)}) custom-call(f32[2,2,24,256]{3,2,1,0:T(8,128)S(1)} %bitcast.1, f32[2,2,64,128]{3,2,1,0:T(8,128)S(1)} %get-tuple-element.28.local_ref, f32[2,8,256]{2,1,0:T(8,128)S(1)} %get-tuple-element.27.refs_4_.start_ref.refs_2_.refs_3_, ...), custom_call_target="tpu_custom_call" | custom-call | flops 1000000 | bytes 500000 | tf_op jit(solution)/shard_map/carry_maps/pallas_call | solution.py:494
  18.1 0.1 finish_second.1.refs_6_
  18.2 0.3 %collective-permute-done.5.refs_0_ = f32[2,24,256]{2,1,0:T(8,128)S(1)} collective-permute-done((f32[2,24,256]{2,1,0:T(8,128)S(1)}, f32[2,24,256]{2,1,0:T(8,128)S(1)}, u32[]{:S(2)}, u32[]{:S(2)}) %collective-permute-start.5) | collective-permute-done | bytes 49184 | tf_op jit(solution)/shard_map/ppermute | solution.py:476
  (9 shorter events, 0.1 us)
Async XLA Ops:
  0.0 1.9 %copy-start.1 = (bf16[2,2,64,128]{3,2,1,0:T(8,128)(2,1)S(1)}, bf16[2,2,64,128]{3,2,1,0:T(8,128)(2,1)}, u32[]{:S(2)}) copy-start(bf16[2,2,64,128]{3,2,1,0:T(8,128)(2,1)} %u_ref.1) | copy-start | bytes 196612
  0.0 1.9 %copy-start.2 = (bf16[2,2,64,128]{3,2,1,0:T(8,128)(2,1)S(1)}, bf16[2,2,64,128]{3,2,1,0:T(8,128)(2,1)}, u32[]{:S(2)}) copy-start(bf16[2,2,64,128]{3,2,1,0:T(8,128)(2,1)} %rhs_ref.1) | copy-start | bytes 196612
  0.0 1.9 %collective-permute-start = (bf16[2,2,64,128]{3,2,1,0:T(8,128)(2,1)}, bf16[2,2,64,128]{3,2,1,0:T(8,128)(2,1)S(1)}, u32[]{:S(2)}, u32[]{:S(2)}) collective-permute-start(bf16[2,2,64,128]{3,2,1,0:T(8,128)(2,1)} %u_ref.1), channel_id=1, source_target_pairs={{0,1},{1,0},{2,3},{3,2},{4,5},{5,4},{6,7},{7,6},{8,9},{9,8},{10,11... | collective-permute-start | bytes 196616 | tf_op jit(solution)/shard_map/ppermute | solution.py:476
  1.9 5.1 %copy-start = (f32[8,64,64]{2,1,0:T(8,128)S(1)}, f32[8,64,64]{2,1,0:T(8,128)}, u32[]{:S(2)}) copy-start(f32[8,64,64]{2,1,0:T(8,128)} %inv_ref.1) | copy-start | bytes 393220
  1.9 5.0 %copy-start.3 = (f32[2,16,128]{2,1,0:T(8,128)S(1)}, f32[2,16,128]{2,1,0:T(8,128)}, u32[]{:S(2)}) copy-start(f32[2,16,128]{2,1,0:T(8,128)} %inflow_ref.1) | copy-start | bytes 49156
  2.7 5.5 %collective-permute-start.4 = (f32[2,24,256]{2,1,0:T(8,128)S(1)}, f32[2,24,256]{2,1,0:T(8,128)S(1)}, u32[]{:S(2)}, u32[]{:S(2)}) collective-permute-start(f32[2,24,256]{2,1,0:T(8,128)S(1)} %get-tuple-element.23), channel_id=1, source_target_pairs={{0,5},{1,4},{2,7},{3,6},{4,1},{5,0},{6,3},{7,2},{8,13},{9,12},{10,... | collective-permute-start | bytes 147464 | tf_op jit(solution)/shard_map/ppermute | solution.py:476
  5.4 4.7 %collective-permute-start.3 = (f32[2,24,256]{2,1,0:T(8,128)S(1)}, f32[2,24,256]{2,1,0:T(8,128)S(1)}, u32[]{:S(2)}, u32[]{:S(2)}) collective-permute-start(f32[2,24,256]{2,1,0:T(8,128)S(1)} %get-tuple-element.23), channel_id=1, source_target_pairs={{0,7},{1,6},{2,5},{3,4},{4,3},{5,2},{6,1},{7,0},{8,15},{9,14},{10,... | collective-permute-start | bytes 147464 | tf_op jit(solution)/shard_map/ppermute | solution.py:476
  6.4 3.6 %collective-permute-start.2 = (f32[2,24,256]{2,1,0:T(8,128)S(1)}, f32[2,24,256]{2,1,0:T(8,128)S(1)}, u32[]{:S(2)}, u32[]{:S(2)}) collective-permute-start(f32[2,24,256]{2,1,0:T(8,128)S(1)} %get-tuple-element.23), channel_id=1, source_target_pairs={{0,3},{1,2},{2,1},{3,0},{4,7},{5,6},{6,5},{7,4},{8,11},{9,10},{10,... | collective-permute-start | bytes 147464 | tf_op jit(solution)/shard_map/ppermute | solution.py:476
  6.5 3.6 %collective-permute-start.1 = (f32[2,24,256]{2,1,0:T(8,128)S(1)}, f32[2,24,256]{2,1,0:T(8,128)S(1)}, u32[]{:S(2)}, u32[]{:S(2)}) collective-permute-start(f32[2,24,256]{2,1,0:T(8,128)S(1)} %get-tuple-element.23), channel_id=1, source_target_pairs={{0,1},{1,0},{2,3},{3,2},{4,5},{5,4},{6,7},{7,6},{8,9},{9,8},{10,11... | collective-permute-start | bytes 147464 | tf_op jit(solution)/shard_map/ppermute | solution.py:476
  10.5 7.6 %collective-permute-start.7 = (f32[2,24,256]{2,1,0:T(8,128)S(1)}, f32[2,24,256]{2,1,0:T(8,128)S(1)}, u32[]{:S(2)}, u32[]{:S(2)}) collective-permute-start(f32[2,24,256]{2,1,0:T(8,128)S(1)} %group_maps.1.refs_4_), channel_id=1, source_target_pairs={{0,25},{1,24},{2,27},{3,26},{4,29},{5,28},{6,31},{7,30},{8,17},{9,... | collective-permute-start | bytes 147464 | tf_op jit(solution)/shard_map/ppermute | solution.py:476
  13.7 4.4 %collective-permute-start.6 = (f32[2,24,256]{2,1,0:T(8,128)S(1)}, f32[2,24,256]{2,1,0:T(8,128)S(1)}, u32[]{:S(2)}, u32[]{:S(2)}) collective-permute-start(f32[2,24,256]{2,1,0:T(8,128)S(1)} %group_maps.1.refs_4_), channel_id=1, source_target_pairs={{0,9},{1,8},{2,11},{3,10},{4,13},{5,12},{6,15},{7,14},{8,1},{9,0},... | collective-permute-start | bytes 147464 | tf_op jit(solution)/shard_map/ppermute | solution.py:476
  13.7 4.7 %collective-permute-start.5 = (f32[2,24,256]{2,1,0:T(8,128)S(1)}, f32[2,24,256]{2,1,0:T(8,128)S(1)}, u32[]{:S(2)}, u32[]{:S(2)}) collective-permute-start(f32[2,24,256]{2,1,0:T(8,128)S(1)} %group_maps.1.refs_4_), channel_id=1, source_target_pairs={{0,17},{1,16},{2,19},{3,18},{4,21},{5,20},{6,23},{7,22},{8,25},{9,... | collective-permute-start | bytes 147464 | tf_op jit(solution)/shard_map/ppermute | solution.py:476

commit v11 on v8

--- a/solution.py
+++ b/solution.py
@@ -180,7 +180,12 @@
     node, item = iota((nodes, nodes), 1), iota((nodes, nodes), 0)
     chosen = (node == wanted_node(item // FACE, item % FACE)).astype(BF16)
     own = [u_ref[x, y] for x in range(planes) for y in range(rows_y)]
-    other = [below_ref[x, below_ref.shape[1] - 1] for x in range(planes)] + [above_ref[x, 0] for x in range(planes)]
+    pair = gy_size == 2
+    if pair:
+        row = jnp.where(place > 0, below_ref.shape[1] - 1, 0)
+        other = [below_ref[x, row] for x in range(planes)]
+    else:
+        other = [below_ref[x, below_ref.shape[1] - 1] for x in range(planes)] + [above_ref[x, 0] for x in range(planes)]
     step = step_ref[...]
     row, lane = iota((2 * FACE, 128), 0), iota((2 * FACE, 128), 1)
     flip = (lane == row + FACE * (row >= FACE)).astype(BF16)
@@ -197,7 +202,7 @@
     data = []
     for x in range(planes):
         under = faces[len(own) + x][16:32] * has_below
-        over = faces[len(own) + planes + x][0:16] * has_above
+        over = faces[len(own) + (0 if pair else planes) + x][0:16] * has_above
         for y in range(rows_y):
             at = x * rows_y + y
             y_flag = label_ref[pl.ds(planes * rows_y + at, 1), :]

time: 18.7 us -> 18.7 us (level)
  no operation moved by 1% of the time
where the time goes in v11:
time: 18.7 us; the launch traced here: 18.5 us
  starting transfers between devices  8.84 us (47%)
  Pallas kernels  5.51 us (29%)
  waiting for transfers between devices  2.18 us (12%)
  blocking collectives  1.88 us (10%)
    ppermute x8, starting transfers between devices, moved(): return lax.ppermute(value, ('gx', 'gy'), pairs)  8.84 us
    pallas_call x8, Pallas kernels, call(): pl.pallas_call(kernel, out_shape=outs, in_specs=in_specs, out_specs=out_s...  5.51 us
    ppermute x8, waiting for transfers between devices, moved(): return lax.ppermute(value, ('gx', 'gy'), pairs)  2.18 us
    all_gather x1, blocking collectives, on_device(): ahead = lax.all_gather(ahead, 'gy', axis_index_groups=couples)  1.88 us
  transfers between devices with their start and end apart: 8, of which 2 were waited for; matrix products, arithmetic and copies ran while one was open for 0% of the time, Pallas kernels for 23%

profile of v11, /device:TPU:0, one launch (start us, length us, event | category | flops | bytes accessed | tf_op | source)
XLA Modules:
  0.0 18.5 jit_solution(6447664778641148851)
XLA Ops:
  0.0 0.5 %collective-permute-start = (bf16[2,2,64,128]{3,2,1,0:T(8,128)(2,1)}, bf16[2,2,64,128]{3,2,1,0:T(8,128)(2,1)S(1)}, u32[]{:S(2)}, u32[]{:S(2)}) collective-permute-start(bf16[2,2,64,128]{3,2,1,0:T(8,128)(2,1)} %refs_0_.1), channel_id=1, source_target_pairs={{0,1},{1,0},{2,3},{3,2},{4,5},{5,4},{6,7},{7,6},{8,9},{9,8},{10,11... | collective-permute-start | bytes 196616 | tf_op jit(solution)/shard_map/ppermute | solution.py:491
  0.5 1.4 %class_matrices.1 = (bf16[80,2048]{1,0:T(8,128)(2,1)S(1)}, bf16[128,256]{1,0:T(8,128)(2,1)S(1)}, bf16[128,128]{1,0:T(8,128)(2,1)S(1)}, f32[12,128]{1,0:T(8,128)S(1)}) custom-call(s32[2,2,16]{2,1,0:T(2,128)} %cls_hbm.1, s32[2,2,2,16]{3,2,1,0:T(2,128)} %flag_hbm.1, f32[8,16,16]{2,1,0:T(8,128)} %x_hbm.1, f32[4,8,16,16]{3,2,1,0:T(8,128)} %lat_hbm.1, ...), custom_call_target="tpu_custom_call" | custom-call | flops 1000000 | bytes 500000 | tf_op jit(solution)/shard_map/class_matrices/pallas_call | solution.py:509
  1.9 0.0 copy-start
  1.9 0.0 collective-permute-done.refs_2_.refs_3_
  1.9 0.0 copy-start.3
  2.0 0.8 %sources.1 = (bf16[2,2,128,128]{3,2,1,0:T(8,128)(2,1)S(1)}, f32[2,16,256]{2,1,0:T(8,128)S(1)}, f32[2,2,16,256]{3,2,1,0:T(8,128)S(1)}, f32[2,24,256]{2,1,0:T(8,128)S(1)}) custom-call(bf16[2,2,64,128]{3,2,1,0:T(8,128)(2,1)S(1)} %copy-done.1, bf16[2,2,64,128]{3,2,1,0:T(8,128)(2,1)S(1)} %copy-done.2, ...), custom_call_target="tpu_custom_call" | custom-call | flops 1000000 | bytes 500000 | tf_op jit(solution)/shard_map/sources/pallas_call | solution.py:509
  2.7 2.6 %collective-permute-start.4 = (f32[2,24,256]{2,1,0:T(8,128)S(1)}, f32[2,24,256]{2,1,0:T(8,128)S(1)}, u32[]{:S(2)}, u32[]{:S(2)}) collective-permute-start(f32[2,24,256]{2,1,0:T(8,128)S(1)} %get-tuple-element.23), channel_id=1, source_target_pairs={{0,5},{1,4},{2,7},{3,6},{4,1},{5,0},{6,3},{7,2},{8,13},{9,12},{10,... | collective-permute-start | bytes 147464 | tf_op jit(solution)/shard_map/ppermute | solution.py:491
  5.4 1.1 %collective-permute-start.3 = (f32[2,24,256]{2,1,0:T(8,128)S(1)}, f32[2,24,256]{2,1,0:T(8,128)S(1)}, u32[]{:S(2)}, u32[]{:S(2)}) collective-permute-start(f32[2,24,256]{2,1,0:T(8,128)S(1)} %get-tuple-element.23), channel_id=1, source_target_pairs={{0,7},{1,6},{2,5},{3,4},{4,3},{5,2},{6,1},{7,0},{8,15},{9,14},{10,... | collective-permute-start | bytes 147464 | tf_op jit(solution)/shard_map/ppermute | solution.py:491
  6.5 0.1 collective-permute-start.2
  6.5 0.5 %collective-permute-start.1 = (f32[2,24,256]{2,1,0:T(8,128)S(1)}, f32[2,24,256]{2,1,0:T(8,128)S(1)}, u32[]{:S(2)}, u32[]{:S(2)}) collective-permute-start(f32[2,24,256]{2,1,0:T(8,128)S(1)} %get-tuple-element.23), channel_id=1, source_target_pairs={{0,1},{1,0},{2,3},{3,2},{4,5},{5,4},{6,7},{7,6},{8,9},{9,8},{10,11... | collective-permute-start | bytes 147464 | tf_op jit(solution)/shard_map/ppermute | solution.py:491
  7.0 1.3 %local_solve.1 = (f32[2,2,64,128]{3,2,1,0:T(8,128)S(1)}, f32[2,8,256]{2,1,0:T(8,128)S(1)}, bf16[2,2,128,256]{3,2,1,0:T(8,128)(2,1)S(1)}, f32[1,2,8,256]{3,2,1,0:T(8,128)S(1)}) custom-call(bf16[2,2,128,128]{3,2,1,0:T(8,128)(2,1)S(1)} %get-tuple-element.24.data_ref, f32[12,128]{1,0:T(8,128)S(1)} %get-tuple-element.20.refs_4_.label_ref, ...), custom_call_target="tpu_custom_call" | custom-call | flops 1000000 | bytes 500000 | tf_op jit(solution)/shard_map/local_solve/pallas_call | solution.py:509
  8.2 0.0 collective-permute-done.4.refs_3_
  8.3 1.8 %collective-permute-done.3.refs_2_ = f32[2,24,256]{2,1,0:T(8,128)S(1)} collective-permute-done((f32[2,24,256]{2,1,0:T(8,128)S(1)}, f32[2,24,256]{2,1,0:T(8,128)S(1)}, u32[]{:S(2)}, u32[]{:S(2)}) %collective-permute-start.3) | collective-permute-done | bytes 49184 | tf_op jit(solution)/shard_map/ppermute | solution.py:491
  10.1 0.0 collective-permute-done.2.refs_1_
  10.1 0.0 collective-permute-done.1.refs_0_
  10.1 0.4 %group_maps.1.refs_4_ = f32[2,24,256]{2,1,0:T(8,128)S(1)} custom-call(f32[2,24,256]{2,1,0:T(8,128)S(1)} %collective-permute-done.1.refs_0_, f32[2,24,256]{2,1,0:T(8,128)S(1)} %collective-permute-done.2.refs_1_, f32[2,24,256]{2,1,0:T(8,128)S(1)} %collective-permute-done.3.refs_2_, f32[2,24,256]{2,1,0:T(8,128)S(1)} %collective-permute-done.4.refs_3_, ...), custom_call_target="tpu_custom_call" | custom-call | flops 1000000 | bytes 500000 | tf_op jit(solution)/shard_map/group_maps/pallas_call | solution.py:509
  10.5 3.2 %collective-permute-start.7 = (f32[2,24,256]{2,1,0:T(8,128)S(1)}, f32[2,24,256]{2,1,0:T(8,128)S(1)}, u32[]{:S(2)}, u32[]{:S(2)}) collective-permute-start(f32[2,24,256]{2,1,0:T(8,128)S(1)} %group_maps.1.refs_4_), channel_id=1, source_target_pairs={{0,25},{1,24},{2,27},{3,26},{4,29},{5,28},{6,31},{7,30},{8,17},{9,... | collective-permute-start | bytes 147464 | tf_op jit(solution)/shard_map/ppermute | solution.py:491
  13.7 0.9 %collective-permute-start.5 = (f32[2,24,256]{2,1,0:T(8,128)S(1)}, f32[2,24,256]{2,1,0:T(8,128)S(1)}, u32[]{:S(2)}, u32[]{:S(2)}) collective-permute-start(f32[2,24,256]{2,1,0:T(8,128)S(1)} %group_maps.1.refs_4_), channel_id=1, source_target_pairs={{0,17},{1,16},{2,19},{3,18},{4,21},{5,20},{6,23},{7,22},{8,25},{9,... | collective-permute-start | bytes 147464 | tf_op jit(solution)/shard_map/ppermute | solution.py:491
  14.6 0.3 %maps_ahead.1 = f32[2,24,256]{2,1,0:T(8,128)S(1)} custom-call(f32[2,24,256]{2,1,0:T(8,128)S(1)} %collective-permute-done.1.refs_0_, f32[2,24,256]{2,1,0:T(8,128)S(1)} %collective-permute-done.2.refs_1_, f32[2,24,256]{2,1,0:T(8,128)S(1)} %collective-permute-done.3.refs_2_, f32[2,24,256]{2,1,0:T(8,128)S(1)} %collective-permute-done.4.refs_3_, ...), custom_call_target="tpu_custom_call" | custom-call | flops 1000000 | bytes 500000 | tf_op jit(solution)/shard_map/maps_ahead/pallas_call | solution.py:509
  15.0 1.9 %all-gather = f32[4,24,256]{2,1,0:T(8,128)S(1)} all-gather(f32[2,24,256]{2,1,0:T(8,128)S(1)} %maps_ahead.1), channel_id=2, replica_groups={{0,1},{2,3},{4,5},{6,7},{8,9},{10,11},{12,13},{14,15},{16,17},{18,19},{..., dimensions={0}, use_global_device_ids=true | all-gather | bytes 147456 | tf_op jit(solution)/shard_map/all_gather | solution.py:611
  16.8 1.2 %carry_maps.1 = (f32[2,2,64,128]{3,2,1,0:T(8,128)S(1)}, bf16[2,256,256]{2,1,0:T(8,128)(2,1)S(1)}, f32[2,2,64,128]{3,2,1,0:T(8,128)}) custom-call(f32[2,2,24,256]{3,2,1,0:T(8,128)S(1)} %bitcast.1, f32[2,2,64,128]{3,2,1,0:T(8,128)S(1)} %get-tuple-element.28.local_ref, f32[2,8,256]{2,1,0:T(8,128)S(1)} %get-tuple-element.27.refs_4_.start_ref.refs_2_.refs_3_, ...), custom_call_target="tpu_custom_call" | custom-call | flops 1000000 | bytes 500000 | tf_op jit(solution)/shard_map/carry_maps/pallas_call | solution.py:509
  18.1 0.0 collective-permute-done.7.refs_0_.refs_2_
  18.1 0.1 finish_second.1.refs_6_
  18.2 0.3 %collective-permute-done.5.refs_0_ = f32[2,24,256]{2,1,0:T(8,128)S(1)} collective-permute-done((f32[2,24,256]{2,1,0:T(8,128)S(1)}, f32[2,24,256]{2,1,0:T(8,128)S(1)}, u32[]{:S(2)}, u32[]{:S(2)}) %collective-permute-start.5) | collective-permute-done | bytes 49184 | tf_op jit(solution)/shard_map/ppermute | solution.py:491
  (9 shorter events, 0.1 us)
Async XLA Ops:
  0.0 1.9 %copy-start.1 = (bf16[2,2,64,128]{3,2,1,0:T(8,128)(2,1)S(1)}, bf16[2,2,64,128]{3,2,1,0:T(8,128)(2,1)}, u32[]{:S(2)}) copy-start(bf16[2,2,64,128]{3,2,1,0:T(8,128)(2,1)} %refs_0_.1) | copy-start | bytes 196612
  0.0 1.9 %copy-start.2 = (bf16[2,2,64,128]{3,2,1,0:T(8,128)(2,1)S(1)}, bf16[2,2,64,128]{3,2,1,0:T(8,128)(2,1)}, u32[]{:S(2)}) copy-start(bf16[2,2,64,128]{3,2,1,0:T(8,128)(2,1)} %refs_1_.1) | copy-start | bytes 196612
  0.0 1.9 %collective-permute-start = (bf16[2,2,64,128]{3,2,1,0:T(8,128)(2,1)}, bf16[2,2,64,128]{3,2,1,0:T(8,128)(2,1)S(1)}, u32[]{:S(2)}, u32[]{:S(2)}) collective-permute-start(bf16[2,2,64,128]{3,2,1,0:T(8,128)(2,1)} %refs_0_.1), channel_id=1, source_target_pairs={{0,1},{1,0},{2,3},{3,2},{4,5},{5,4},{6,7},{7,6},{8,9},{9,8},{10,11... | collective-permute-start | bytes 196616 | tf_op jit(solution)/shard_map/ppermute | solution.py:491
  1.9 5.1 %copy-start = (f32[8,64,64]{2,1,0:T(8,128)S(1)}, f32[8,64,64]{2,1,0:T(8,128)}, u32[]{:S(2)}) copy-start(f32[8,64,64]{2,1,0:T(8,128)} %inv_ref.1) | copy-start | bytes 393220
  1.9 5.0 %copy-start.3 = (f32[2,16,128]{2,1,0:T(8,128)S(1)}, f32[2,16,128]{2,1,0:T(8,128)}, u32[]{:S(2)}) copy-start(f32[2,16,128]{2,1,0:T(8,128)} %inflow_ref.1) | copy-start | bytes 49156
  2.7 5.5 %collective-permute-start.4 = (f32[2,24,256]{2,1,0:T(8,128)S(1)}, f32[2,24,256]{2,1,0:T(8,128)S(1)}, u32[]{:S(2)}, u32[]{:S(2)}) collective-permute-start(f32[2,24,256]{2,1,0:T(8,128)S(1)} %get-tuple-element.23), channel_id=1, source_target_pairs={{0,5},{1,4},{2,7},{3,6},{4,1},{5,0},{6,3},{7,2},{8,13},{9,12},{10,... | collective-permute-start | bytes 147464 | tf_op jit(solution)/shard_map/ppermute | solution.py:491
  5.4 4.7 %collective-permute-start.3 = (f32[2,24,256]{2,1,0:T(8,128)S(1)}, f32[2,24,256]{2,1,0:T(8,128)S(1)}, u32[]{:S(2)}, u32[]{:S(2)}) collective-permute-start(f32[2,24,256]{2,1,0:T(8,128)S(1)} %get-tuple-element.23), channel_id=1, source_target_pairs={{0,7},{1,6},{2,5},{3,4},{4,3},{5,2},{6,1},{7,0},{8,15},{9,14},{10,... | collective-permute-start | bytes 147464 | tf_op jit(solution)/shard_map/ppermute | solution.py:491
  6.5 3.6 %collective-permute-start.2 = (f32[2,24,256]{2,1,0:T(8,128)S(1)}, f32[2,24,256]{2,1,0:T(8,128)S(1)}, u32[]{:S(2)}, u32[]{:S(2)}) collective-permute-start(f32[2,24,256]{2,1,0:T(8,128)S(1)} %get-tuple-element.23), channel_id=1, source_target_pairs={{0,3},{1,2},{2,1},{3,0},{4,7},{5,6},{6,5},{7,4},{8,11},{9,10},{10,... | collective-permute-start | bytes 147464 | tf_op jit(solution)/shard_map/ppermute | solution.py:491
  6.5 3.6 %collective-permute-start.1 = (f32[2,24,256]{2,1,0:T(8,128)S(1)}, f32[2,24,256]{2,1,0:T(8,128)S(1)}, u32[]{:S(2)}, u32[]{:S(2)}) collective-permute-start(f32[2,24,256]{2,1,0:T(8,128)S(1)} %get-tuple-element.23), channel_id=1, source_target_pairs={{0,1},{1,0},{2,3},{3,2},{4,5},{5,4},{6,7},{7,6},{8,9},{9,8},{10,11... | collective-permute-start | bytes 147464 | tf_op jit(solution)/shard_map/ppermute | solution.py:491
  10.5 7.6 %collective-permute-start.7 = (f32[2,24,256]{2,1,0:T(8,128)S(1)}, f32[2,24,256]{2,1,0:T(8,128)S(1)}, u32[]{:S(2)}, u32[]{:S(2)}) collective-permute-start(f32[2,24,256]{2,1,0:T(8,128)S(1)} %group_maps.1.refs_4_), channel_id=1, source_target_pairs={{0,25},{1,24},{2,27},{3,26},{4,29},{5,28},{6,31},{7,30},{8,17},{9,... | collective-permute-start | bytes 147464 | tf_op jit(solution)/shard_map/ppermute | solution.py:491
  13.7 4.4 %collective-permute-start.6 = (f32[2,24,256]{2,1,0:T(8,128)S(1)}, f32[2,24,256]{2,1,0:T(8,128)S(1)}, u32[]{:S(2)}, u32[]{:S(2)}) collective-permute-start(f32[2,24,256]{2,1,0:T(8,128)S(1)} %group_maps.1.refs_4_), channel_id=1, source_target_pairs={{0,9},{1,8},{2,11},{3,10},{4,13},{5,12},{6,15},{7,14},{8,1},{9,0},... | collective-permute-start | bytes 147464 | tf_op jit(solution)/shard_map/ppermute | solution.py:491
  13.7 4.8 %collective-permute-start.5 = (f32[2,24,256]{2,1,0:T(8,128)S(1)}, f32[2,24,256]{2,1,0:T(8,128)S(1)}, u32[]{:S(2)}, u32[]{:S(2)}) collective-permute-start(f32[2,24,256]{2,1,0:T(8,128)S(1)} %group_maps.1.refs_4_), channel_id=1, source_target_pairs={{0,17},{1,16},{2,19},{3,18},{4,21},{5,20},{6,23},{7,22},{8,25},{9,... | collective-permute-start | bytes 147464 | tf_op jit(solution)/shard_map/ppermute | solution.py:491

commit v12 on v10

--- a/solution.py
+++ b/solution.py
@@ -279,8 +279,6 @@
 
 
 def sent_steps(size, first):
-    if first == 2:
-        return (2, 1) + tuple(range(3, size)) if size > 2 else tuple(range(1, size))
     return (1, 3, 2) + tuple(range(4, size)) if size > 3 else tuple(range(1, size))
 
 
@@ -292,8 +290,6 @@
 
 def block_slot(mine, other, size, power, first):
     step = (mine ^ other) if power else (mine - other + size) % size
-    if first == 2:
-        return step + 1 * (step == 1) - 1 * (step == 2) if size > 2 else step
     return step + 1 * (step == 2) - 1 * (step == 3) if size > 3 else step
 
 

time: 18.6 us -> 18.6 us (level)
  no operation moved by 1% of the time
where the time goes in v12:
time: 18.6 us; the launch traced here: 18.4 us
  starting transfers between devices  8.84 us (48%)
  Pallas kernels  5.49 us (30%)
  waiting for transfers between devices  2.09 us (11%)
  blocking collectives  1.88 us (10%)
    ppermute x8, starting transfers between devices, moved(): return lax.ppermute(value, ('gx', 'gy'), pairs)  8.84 us
    pallas_call x8, Pallas kernels, call(): pl.pallas_call(kernel, out_shape=outs, in_specs=in_specs, out_specs=out_s...  5.49 us
    ppermute x8, waiting for transfers between devices, moved(): return lax.ppermute(value, ('gx', 'gy'), pairs)  2.09 us
    all_gather x1, blocking collectives, on_device(): ahead = lax.all_gather(ahead, 'gy', axis_index_groups=couples)  1.88 us
  transfers between devices with their start and end apart: 8, of which 2 were waited for; matrix products, arithmetic and copies ran while one was open for 0% of the time, Pallas kernels for 23%

profile of v12, /device:TPU:0, one launch (start us, length us, event | category | flops | bytes accessed | tf_op | source)
XLA Modules:
  0.0 18.4 jit_solution(8499611496875833292)
XLA Ops:
  0.0 0.5 %collective-permute-start = (bf16[2,2,64,128]{3,2,1,0:T(8,128)(2,1)}, bf16[2,2,64,128]{3,2,1,0:T(8,128)(2,1)S(1)}, u32[]{:S(2)}, u32[]{:S(2)}) collective-permute-start(bf16[2,2,64,128]{3,2,1,0:T(8,128)(2,1)} %u_ref.1), channel_id=1, source_target_pairs={{0,1},{1,0},{2,3},{3,2},{4,5},{5,4},{6,7},{7,6},{8,9},{9,8},{10,11... | collective-permute-start | bytes 196616 | tf_op jit(solution)/shard_map/ppermute | solution.py:472
  0.5 1.4 %class_matrices.1 = (bf16[80,2048]{1,0:T(8,128)(2,1)S(1)}, bf16[128,256]{1,0:T(8,128)(2,1)S(1)}, bf16[128,128]{1,0:T(8,128)(2,1)S(1)}, f32[12,128]{1,0:T(8,128)S(1)}) custom-call(s32[2,2,16]{2,1,0:T(2,128)} %cls_hbm.1, s32[2,2,2,16]{3,2,1,0:T(2,128)} %flag_hbm.1, f32[8,16,16]{2,1,0:T(8,128)} %x_hbm.1, f32[4,8,16,16]{3,2,1,0:T(8,128)} %lat_hbm.1, ...), custom_call_target="tpu_custom_call" | custom-call | flops 1000000 | bytes 500000 | tf_op jit(solution)/shard_map/class_matrices/pallas_call | solution.py:490
  1.9 0.0 copy-start
  1.9 0.0 collective-permute-done.below_ref.above_ref
  1.9 0.0 copy-start.3
  2.0 0.7 %sources.1 = (bf16[2,2,128,128]{3,2,1,0:T(8,128)(2,1)S(1)}, f32[2,16,256]{2,1,0:T(8,128)S(1)}, f32[2,2,16,256]{3,2,1,0:T(8,128)S(1)}, f32[2,24,256]{2,1,0:T(8,128)S(1)}) custom-call(bf16[2,2,64,128]{3,2,1,0:T(8,128)(2,1)S(1)} %copy-done.1, bf16[2,2,64,128]{3,2,1,0:T(8,128)(2,1)S(1)} %copy-done.2, ...), custom_call_target="tpu_custom_call" | custom-call | flops 1000000 | bytes 500000 | tf_op jit(solution)/shard_map/sources/pallas_call | solution.py:490
  2.7 2.6 %collective-permute-start.4 = (f32[2,24,256]{2,1,0:T(8,128)S(1)}, f32[2,24,256]{2,1,0:T(8,128)S(1)}, u32[]{:S(2)}, u32[]{:S(2)}) collective-permute-start(f32[2,24,256]{2,1,0:T(8,128)S(1)} %get-tuple-element.23), channel_id=1, source_target_pairs={{0,5},{1,4},{2,7},{3,6},{4,1},{5,0},{6,3},{7,2},{8,13},{9,12},{10,... | collective-permute-start | bytes 147464 | tf_op jit(solution)/shard_map/ppermute | solution.py:472
  5.4 1.1 %collective-permute-start.3 = (f32[2,24,256]{2,1,0:T(8,128)S(1)}, f32[2,24,256]{2,1,0:T(8,128)S(1)}, u32[]{:S(2)}, u32[]{:S(2)}) collective-permute-start(f32[2,24,256]{2,1,0:T(8,128)S(1)} %get-tuple-element.23), channel_id=1, source_target_pairs={{0,7},{1,6},{2,5},{3,4},{4,3},{5,2},{6,1},{7,0},{8,15},{9,14},{10,... | collective-permute-start | bytes 147464 | tf_op jit(solution)/shard_map/ppermute | solution.py:472
  6.4 0.1 collective-permute-start.2
  6.5 0.5 %collective-permute-start.1 = (f32[2,24,256]{2,1,0:T(8,128)S(1)}, f32[2,24,256]{2,1,0:T(8,128)S(1)}, u32[]{:S(2)}, u32[]{:S(2)}) collective-permute-start(f32[2,24,256]{2,1,0:T(8,128)S(1)} %get-tuple-element.23), channel_id=1, source_target_pairs={{0,1},{1,0},{2,3},{3,2},{4,5},{5,4},{6,7},{7,6},{8,9},{9,8},{10,11... | collective-permute-start | bytes 147464 | tf_op jit(solution)/shard_map/ppermute | solution.py:472
  7.0 1.3 %local_solve.1 = (f32[2,2,64,128]{3,2,1,0:T(8,128)S(1)}, f32[2,8,256]{2,1,0:T(8,128)S(1)}, bf16[2,2,128,256]{3,2,1,0:T(8,128)(2,1)S(1)}, f32[1,2,8,256]{3,2,1,0:T(8,128)S(1)}) custom-call(bf16[2,2,128,128]{3,2,1,0:T(8,128)(2,1)S(1)} %get-tuple-element.24.data_ref, f32[12,128]{1,0:T(8,128)S(1)} %get-tuple-element.20.label_ref, ...), custom_call_target="tpu_custom_call" | custom-call | flops 1000000 | bytes 500000 | tf_op jit(solution)/shard_map/local_solve/pallas_call | solution.py:490
  8.2 0.0 collective-permute-done.4.refs_3_
  8.2 1.8 %collective-permute-done.3.refs_2_ = f32[2,24,256]{2,1,0:T(8,128)S(1)} collective-permute-done((f32[2,24,256]{2,1,0:T(8,128)S(1)}, f32[2,24,256]{2,1,0:T(8,128)S(1)}, u32[]{:S(2)}, u32[]{:S(2)}) %collective-permute-start.3) | collective-permute-done | bytes 49184 | tf_op jit(solution)/shard_map/ppermute | solution.py:472
  10.1 0.0 collective-permute-done.2.refs_1_
  10.1 0.0 collective-permute-done.1.refs_0_
  10.1 0.4 %group_maps.1.refs_4_ = f32[2,24,256]{2,1,0:T(8,128)S(1)} custom-call(f32[2,24,256]{2,1,0:T(8,128)S(1)} %collective-permute-done.1.refs_0_, f32[2,24,256]{2,1,0:T(8,128)S(1)} %collective-permute-done.2.refs_1_, f32[2,24,256]{2,1,0:T(8,128)S(1)} %collective-permute-done.3.refs_2_, f32[2,24,256]{2,1,0:T(8,128)S(1)} %collective-permute-done.4.refs_3_, ...), custom_call_target="tpu_custom_call" | custom-call | flops 1000000 | bytes 500000 | tf_op jit(solution)/shard_map/group_maps/pallas_call | solution.py:490
  10.5 3.2 %collective-permute-start.6 = (f32[2,24,256]{2,1,0:T(8,128)S(1)}, f32[2,24,256]{2,1,0:T(8,128)S(1)}, u32[]{:S(2)}, u32[]{:S(2)}) collective-permute-start(f32[2,24,256]{2,1,0:T(8,128)S(1)} %group_maps.1.refs_4_), channel_id=1, source_target_pairs={{0,25},{1,24},{2,27},{3,26},{4,29},{5,28},{6,31},{7,30},{8,17},{9,... | collective-permute-start | bytes 147464 | tf_op jit(solution)/shard_map/ppermute | solution.py:472
  13.7 0.0 collective-permute-start.5
  13.7 0.9 %collective-permute-start.7 = (f32[2,24,256]{2,1,0:T(8,128)S(1)}, f32[2,24,256]{2,1,0:T(8,128)S(1)}, u32[]{:S(2)}, u32[]{:S(2)}) collective-permute-start(f32[2,24,256]{2,1,0:T(8,128)S(1)} %group_maps.1.refs_4_), channel_id=1, source_target_pairs={{0,17},{1,16},{2,19},{3,18},{4,21},{5,20},{6,23},{7,22},{8,25},{9,... | collective-permute-start | bytes 147464 | tf_op jit(solution)/shard_map/ppermute | solution.py:472
  14.6 0.3 %maps_ahead.1 = f32[2,24,256]{2,1,0:T(8,128)S(1)} custom-call(f32[2,24,256]{2,1,0:T(8,128)S(1)} %collective-permute-done.1.refs_0_, f32[2,24,256]{2,1,0:T(8,128)S(1)} %collective-permute-done.2.refs_1_, f32[2,24,256]{2,1,0:T(8,128)S(1)} %collective-permute-done.3.refs_2_, f32[2,24,256]{2,1,0:T(8,128)S(1)} %collective-permute-done.4.refs_3_, ...), custom_call_target="tpu_custom_call" | custom-call | flops 1000000 | bytes 500000 | tf_op jit(solution)/shard_map/maps_ahead/pallas_call | solution.py:490
  15.0 1.9 %all-gather = f32[4,24,256]{2,1,0:T(8,128)S(1)} all-gather(f32[2,24,256]{2,1,0:T(8,128)S(1)} %maps_ahead.1), channel_id=2, replica_groups={{0,1},{2,3},{4,5},{6,7},{8,9},{10,11},{12,13},{14,15},{16,17},{18,19},{..., dimensions={0}, use_global_device_ids=true | all-gather | bytes 147456 | tf_op jit(solution)/shard_map/all_gather | solution.py:592
  16.8 1.2 %carry_maps.1 = (f32[2,2,64,128]{3,2,1,0:T(8,128)S(1)}, bf16[2,256,256]{2,1,0:T(8,128)(2,1)S(1)}, f32[2,2,64,128]{3,2,1,0:T(8,128)}) custom-call(f32[2,2,24,256]{3,2,1,0:T(8,128)S(1)} %bitcast.1, f32[2,2,64,128]{3,2,1,0:T(8,128)S(1)} %get-tuple-element.28.local_ref, f32[2,8,256]{2,1,0:T(8,128)S(1)} %get-tuple-element.27.refs_4_.start_ref.refs_2_.refs_3_, ...), custom_call_target="tpu_custom_call" | custom-call | flops 1000000 | bytes 500000 | tf_op jit(solution)/shard_map/carry_maps/pallas_call | solution.py:490
  18.1 0.1 finish_second.1.refs_6_
  18.2 0.3 %collective-permute-done.7.refs_2_ = f32[2,24,256]{2,1,0:T(8,128)S(1)} collective-permute-done((f32[2,24,256]{2,1,0:T(8,128)S(1)}, f32[2,24,256]{2,1,0:T(8,128)S(1)}, u32[]{:S(2)}, u32[]{:S(2)}) %collective-permute-start.7) | collective-permute-done | bytes 49184 | tf_op jit(solution)/shard_map/ppermute | solution.py:472
  (9 shorter events, 0.1 us)
Async XLA Ops:
  0.0 1.9 %copy-start.1 = (bf16[2,2,64,128]{3,2,1,0:T(8,128)(2,1)S(1)}, bf16[2,2,64,128]{3,2,1,0:T(8,128)(2,1)}, u32[]{:S(2)}) copy-start(bf16[2,2,64,128]{3,2,1,0:T(8,128)(2,1)} %u_ref.1) | copy-start | bytes 196612
  0.0 1.9 %copy-start.2 = (bf16[2,2,64,128]{3,2,1,0:T(8,128)(2,1)S(1)}, bf16[2,2,64,128]{3,2,1,0:T(8,128)(2,1)}, u32[]{:S(2)}) copy-start(bf16[2,2,64,128]{3,2,1,0:T(8,128)(2,1)} %rhs_ref.1) | copy-start | bytes 196612
  0.0 1.9 %collective-permute-start = (bf16[2,2,64,128]{3,2,1,0:T(8,128)(2,1)}, bf16[2,2,64,128]{3,2,1,0:T(8,128)(2,1)S(1)}, u32[]{:S(2)}, u32[]{:S(2)}) collective-permute-start(bf16[2,2,64,128]{3,2,1,0:T(8,128)(2,1)} %u_ref.1), channel_id=1, source_target_pairs={{0,1},{1,0},{2,3},{3,2},{4,5},{5,4},{6,7},{7,6},{8,9},{9,8},{10,11... | collective-permute-start | bytes 196616 | tf_op jit(solution)/shard_map/ppermute | solution.py:472
  1.9 5.1 %copy-start = (f32[8,64,64]{2,1,0:T(8,128)S(1)}, f32[8,64,64]{2,1,0:T(8,128)}, u32[]{:S(2)}) copy-start(f32[8,64,64]{2,1,0:T(8,128)} %inv_ref.1) | copy-start | bytes 393220
  1.9 5.0 %copy-start.3 = (f32[2,16,128]{2,1,0:T(8,128)S(1)}, f32[2,16,128]{2,1,0:T(8,128)}, u32[]{:S(2)}) copy-start(f32[2,16,128]{2,1,0:T(8,128)} %inflow_ref.1) | copy-start | bytes 49156
  2.7 5.5 %collective-permute-start.4 = (f32[2,24,256]{2,1,0:T(8,128)S(1)}, f32[2,24,256]{2,1,0:T(8,128)S(1)}, u32[]{:S(2)}, u32[]{:S(2)}) collective-permute-start(f32[2,24,256]{2,1,0:T(8,128)S(1)} %get-tuple-element.23), channel_id=1, source_target_pairs={{0,5},{1,4},{2,7},{3,6},{4,1},{5,0},{6,3},{7,2},{8,13},{9,12},{10,... | collective-permute-start | bytes 147464 | tf_op jit(solution)/shard_map/ppermute | solution.py:472
  5.4 4.7 %collective-permute-start.3 = (f32[2,24,256]{2,1,0:T(8,128)S(1)}, f32[2,24,256]{2,1,0:T(8,128)S(1)}, u32[]{:S(2)}, u32[]{:S(2)}) collective-permute-start(f32[2,24,256]{2,1,0:T(8,128)S(1)} %get-tuple-element.23), channel_id=1, source_target_pairs={{0,7},{1,6},{2,5},{3,4},{4,3},{5,2},{6,1},{7,0},{8,15},{9,14},{10,... | collective-permute-start | bytes 147464 | tf_op jit(solution)/shard_map/ppermute | solution.py:472
  6.4 3.6 %collective-permute-start.2 = (f32[2,24,256]{2,1,0:T(8,128)S(1)}, f32[2,24,256]{2,1,0:T(8,128)S(1)}, u32[]{:S(2)}, u32[]{:S(2)}) collective-permute-start(f32[2,24,256]{2,1,0:T(8,128)S(1)} %get-tuple-element.23), channel_id=1, source_target_pairs={{0,3},{1,2},{2,1},{3,0},{4,7},{5,6},{6,5},{7,4},{8,11},{9,10},{10,... | collective-permute-start | bytes 147464 | tf_op jit(solution)/shard_map/ppermute | solution.py:472
  6.5 3.6 %collective-permute-start.1 = (f32[2,24,256]{2,1,0:T(8,128)S(1)}, f32[2,24,256]{2,1,0:T(8,128)S(1)}, u32[]{:S(2)}, u32[]{:S(2)}) collective-permute-start(f32[2,24,256]{2,1,0:T(8,128)S(1)} %get-tuple-element.23), channel_id=1, source_target_pairs={{0,1},{1,0},{2,3},{3,2},{4,5},{5,4},{6,7},{7,6},{8,9},{9,8},{10,11... | collective-permute-start | bytes 147464 | tf_op jit(solution)/shard_map/ppermute | solution.py:472
  10.5 7.6 %collective-permute-start.6 = (f32[2,24,256]{2,1,0:T(8,128)S(1)}, f32[2,24,256]{2,1,0:T(8,128)S(1)}, u32[]{:S(2)}, u32[]{:S(2)}) collective-permute-start(f32[2,24,256]{2,1,0:T(8,128)S(1)} %group_maps.1.refs_4_), channel_id=1, source_target_pairs={{0,25},{1,24},{2,27},{3,26},{4,29},{5,28},{6,31},{7,30},{8,17},{9,... | collective-permute-start | bytes 147464 | tf_op jit(solution)/shard_map/ppermute | solution.py:472
  13.7 4.4 %collective-permute-start.5 = (f32[2,24,256]{2,1,0:T(8,128)S(1)}, f32[2,24,256]{2,1,0:T(8,128)S(1)}, u32[]{:S(2)}, u32[]{:S(2)}) collective-permute-start(f32[2,24,256]{2,1,0:T(8,128)S(1)} %group_maps.1.refs_4_), channel_id=1, source_target_pairs={{0,9},{1,8},{2,11},{3,10},{4,13},{5,12},{6,15},{7,14},{8,1},{9,0},... | collective-permute-start | bytes 147464 | tf_op jit(solution)/shard_map/ppermute | solution.py:472
  13.7 4.7 %collective-permute-start.7 = (f32[2,24,256]{2,1,0:T(8,128)S(1)}, f32[2,24,256]{2,1,0:T(8,128)S(1)}, u32[]{:S(2)}, u32[]{:S(2)}) collective-permute-start(f32[2,24,256]{2,1,0:T(8,128)S(1)} %group_maps.1.refs_4_), channel_id=1, source_target_pairs={{0,17},{1,16},{2,19},{3,18},{4,21},{5,20},{6,23},{7,22},{8,25},{9,... | collective-permute-start | bytes 147464 | tf_op jit(solution)/shard_map/ppermute | solution.py:472
